TPU v7x, 32 devices: a whole 2x2x4 slice. The times are simulated.
32 devices in a mesh: gx: 4 (over z), gy: 4 (over y, x), blk: 2 (over core).
Axes of the slice: x: 2, y: 2, z: 4, core: 2. Of those that a mesh axis runs over, the one named last changes fastest.
Arguments:
- pressure: float32 [64, 256, 256], P('gx', 'gy', 'blk'), may hold values from -6 to 6
- pressure_prev: float32 [64, 256, 256], P('gx', 'gy', 'blk'), may hold values from -6 to 6
- buoyancy: float32 [64, 256, 256], P('gx', 'gy', 'blk'), may hold values from 0.5 to 2
- kappa: float32 [64, 256, 256], P('gx', 'gy', 'blk'), may hold values from 0.5 to 2
- hull_accel: float32 [16384, 128], P(('gx', 'gy', 'blk')), may hold values from -6 to 6
- row_block: int32 [16384, 1], P(('gx', 'gy', 'blk')), may hold values from 0 to 15; in each aligned block of 512 rows (0 to 511, 512 to 1023, ...) at most 64 rows name the same one
- row_column: int32 [16384, 1], P(('gx', 'gy', 'blk')), may hold values from 0 to 1023
Outputs:
- pressure_next: float32 [64, 256, 256], P('gx', 'gy', 'blk')
- hull_pressure: float32 [16384, 128], P(('gx', 'gy', 'blk'))
Inputs may be any that keep to these rules, and one draw needn't show every extreme that they name: `row_block`: among the 512 rows of one device at most 64 name the same block, and exactly 64 do for some block.
All inputs are finite; a program needn't handle non-finite values.
Results may differ from a plain program's by a relative error of at most 0.00002.
Values sent between devices are 32-bit elements; how exact they have to be, the bound alone decides.
No kernel may reach another device: no remote copies, remote signals or barrier semaphores. Data moves between devices by JAX's collectives and lax.ppermute only.
A program may use at most 64 MiB of HBM per device.

v0:
```python
import jax
import jax.numpy as jnp
from jax import lax
from jax.sharding import PartitionSpec as P

courant_sq = 0.05
source_gain = 0.5


def extended(cells, sides, width):
    for axis, dim in sides:
        count = lax.axis_size(axis)
        ends = count - 1
        head = lax.slice_in_dim(cells, 0, width, axis=dim)
        tail = lax.slice_in_dim(cells, cells.shape[dim] - width, cells.shape[dim], axis=dim)
        cells = jnp.concatenate(
            [
                lax.ppermute(tail, axis, [(i, (i + 1) % count) for i in range(ends)]),
                cells,
                lax.ppermute(head, axis, [((i + 1) % count, i) for i in range(ends)]),
            ],
            axis=dim,
        )
    return cells


def trim_edge(field, width, skip_dim):
    for other_dim in range(3):
        if other_dim != skip_dim:
            field = lax.slice_in_dim(field, width, field.shape[other_dim] - width, axis=other_dim)
    return field


def fourth_diff(field, along_dim, length_out):

    def shifted(offset):
        return lax.slice_in_dim(field, offset, offset + length_out, axis=along_dim)

    return (27.0 * (shifted(2) - shifted(1)) - (shifted(3) - shifted(0))) / 24.0


def operator(padded, buoy_pad):
    summed = None
    for along_dim in range(3):
        press_line = trim_edge(padded, 3, along_dim)
        buoy_line = trim_edge(buoy_pad, 2, along_dim)
        length_out = padded.shape[along_dim] - 6
        gradient = fourth_diff(press_line, along_dim, length_out + 3)
        face_buoy = (
            lax.slice_in_dim(buoy_line, 0, length_out + 3, axis=along_dim)
            + lax.slice_in_dim(buoy_line, 1, length_out + 4, axis=along_dim)
        ) * 0.5
        axis_term = fourth_diff(gradient * face_buoy, along_dim, length_out)
        summed = axis_term if summed is None else summed + axis_term
    return summed


def route_out(outgoing, dest_cols):
    got_rows, got_cols = (
        lax.all_to_all(outgoing, ("gx", "gy"), split_axis=0, concat_axis=0, tiled=True),
        lax.all_to_all(dest_cols, ("gx", "gy"), split_axis=0, concat_axis=0, tiled=True),
    )
    return (got_rows.reshape(-1, outgoing.shape[-1]), got_cols.reshape(-1))


def route_back(sampled, num_gx, num_gy, capacity):
    depth_len = sampled.shape[-1]
    returned = lax.all_to_all(
        sampled.reshape(num_gx * num_gy, capacity, depth_len),
        ("gx", "gy"),
        split_axis=0,
        concat_axis=0,
        tiled=True,
    )
    return returned.reshape(-1, depth_len)


def local(pressure, pressure_prev, buoyancy, kappa, hull_accel, row_block, row_column):
    num_gx = lax.axis_size("gx")
    num_gy = lax.axis_size("gy")
    groups = num_gx * num_gy
    row_count = hull_accel.shape[0]
    depth_len = hull_accel.shape[1]
    capacity = 2 * row_count // groups
    columns_all = pressure.shape[0] * pressure.shape[1]
    block_ids = row_block[:, 0]
    column = row_column[:, 0]
    matches = (block_ids[:, None] == jnp.arange(groups, dtype=jnp.int32)[None, :]).astype(jnp.int32)
    earlier = jnp.cumsum(matches, axis=0) - matches
    slot_pos = jnp.sum(earlier * matches, axis=1)
    placing = block_ids * capacity + slot_pos
    outgoing = jnp.zeros((groups * capacity, depth_len), jnp.float32).at[placing].set(hull_accel)
    dest_cols = jnp.full((groups * capacity,), -1, jnp.int32).at[placing].set(column)
    outgoing = outgoing.reshape(groups, capacity, depth_len)
    dest_cols = dest_cols.reshape(groups, capacity)
    first_ext = extended(jnp.stack([pressure, buoyancy]), (("gx", 1), ("gy", 2), ("blk", 3)), 3)
    got_rows, got_cols = route_out(outgoing, dest_cols)
    target_idx = jnp.where(got_cols >= 0, got_cols, columns_all)
    source = (
        jnp.zeros((columns_all, depth_len), jnp.float32).at[target_idx].add(got_rows, mode="drop")
    )
    source = source.reshape(pressure.shape)
    buoy_pad = trim_edge(first_ext[1], 1, -1)
    lap_one = operator(first_ext[0], buoy_pad)
    pressure_mid = (
        2.0 * pressure - pressure_prev + kappa * (courant_sq * lap_one + source_gain * source)
    )
    padded_mid = extended(pressure_mid, (("gx", 0), ("gy", 1), ("blk", 2)), 3)
    lap_two = operator(padded_mid, buoy_pad)
    pressure_next = (
        2.0 * pressure_mid - pressure + kappa * (courant_sq * lap_two + source_gain * source)
    )
    flattened = pressure_next.reshape(columns_all, depth_len)
    picked = flattened[jnp.clip(got_cols, 0, columns_all - 1)]
    returned = route_back(picked, num_gx, num_gy, capacity)
    hull_pressure = returned[placing]
    return (pressure_next, hull_pressure)


def solution(mesh):
    return jax.shard_map(
        local,
        mesh=mesh,
        in_specs=(
            P("gx", "gy", "blk"),
            P("gx", "gy", "blk"),
            P("gx", "gy", "blk"),
            P("gx", "gy", "blk"),
            P(("gx", "gy", "blk"), None),
            P(("gx", "gy", "blk"), None),
            P(("gx", "gy", "blk"), None),
        ),
        out_specs=(P("gx", "gy", "blk"), P(("gx", "gy", "blk"), None)),
        check_vma=False,
    )
```

profile of v0, /device:TPU:0, one launch (start us, length us, event | category | flops | bytes accessed | tf_op | source)
XLA Modules:
  0.0 159.7 jit_solution(5721684938734681686)
XLA Ops:
  1.8 4.9 %collective-permute-start = (f32[2,3,64,128]{3,2,1,0:T(8,128)S(1)}, f32[2,3,64,128]{3,2,1,0:T(8,128)S(1)}, u32[]{:S(2)}, u32[]{:S(2)}) collective-permute-start(f32[2,3,64,128]{3,2,1,0:T(8,128)S(1)} %get-tuple-element.20), channel_id=1, source_target_pairs={{0,8},{8,16},{16,24},{1,9},{9,17},{17,25},{2,10},{10,18},{18,26},{... | collective-permute-start | bytes 589832 | tf_op jit(solution)/shard_map/ppermute | solution.py:18
  10.9 4.1 %collective-permute-done.1 = f32[2,3,64,128]{3,2,1,0:T(8,128)S(1)} collective-permute-done((f32[2,3,64,128]{3,2,1,0:T(8,128)S(1)}, f32[2,3,64,128]{3,2,1,0:T(8,128)S(1)}, u32[]{:S(2)}, u32[]{:S(2)}) %collective-permute-start.1) | collective-permute-done | bytes 196640 | tf_op jit(solution)/shard_map/ppermute | solution.py:20
  16.4 3.5 %collective-permute-start.2 = (f32[2,22,3,128]{3,0,2,1:T(2,128)S(1)}, f32[2,22,3,128]{3,0,2,1:T(2,128)S(1)}, u32[]{:S(2)}, u32[]{:S(2)}) collective-permute-start(f32[2,22,3,128]{3,0,2,1:T(2,128)S(1)} %copy.110), channel_id=1, source_target_pairs={{0,2},{2,4},{4,6},{1,3},{3,5},{5,7},{8,10},{10,12},{12,14},{9,11},... | collective-permute-start | bytes 202760 | tf_op jit(solution)/shard_map/ppermute | solution.py:18
  21.3 2.6 %scatter_custom_fusion = s32[1024]{0:T(1024)S(1)} fusion(s32[512]{0:T(512)S(1)} %bitcast.50, s32[512]{0:T(512)} %bitcast.55, s32[]{:T(128)} %constant.21.clone.1), kind=kCustom, calls=%fused_computation.134 | custom fusion | bytes 4608 | tf_op jit(solution)/shard_map/scatter | solution.py:93
  24.6 7.0 %all-to-all-start = ((s32[16,1,64]{2,1,0:T(1,128)}), s32[16,1,64]{2,1,0:T(1,128)S(1)}, u32[]{:S(2)}, u32[]{:S(2)}) async-start(s32[16,1,64]{2,1,0:T(1,128)} %all_to_all.12), calls=%async_computation | async-start | bytes 16384 | tf_op jit(solution)/shard_map/all_to_all | solution.py:61
  35.9 2.9 %scatter_custom_fusion.1 = f32[1024,128]{1,0:T(8,128)} fusion(s32[512]{0:T(512)S(1)} %bitcast.51, f32[512,128]{1,0:T(8,128)} %param.11, f32[]{:T(128)} %constant.20.clone.1), kind=kCustom, calls=%fused_computation.110 | custom fusion | bytes 524800 | tf_op jit(solution)/shard_map/scatter | solution.py:92
  38.8 6.9 %all-to-all-start.1 = ((f32[16,64,128]{2,1,0:T(8,128)}), f32[16,64,128]{2,1,0:T(8,128)}, u32[]{:S(2)}, u32[]{:S(2)}) async-start(f32[16,64,128]{2,1,0:T(8,128)} %bitcast.12), calls=%async_computation.1 | async-start | bytes 1048576 | tf_op jit(solution)/shard_map/all_to_all | solution.py:60
  47.0 2.2 %copy.90 = f32[2,22,64,128]{2,1,3,0:T(8,128)S(1)} copy(f32[2,22,64,128]{3,2,1,0:T(8,128)} %copy-done.10) | data formatting | bytes 2883584 | tf_op jit(solution)/shard_map/concatenate | solution.py:16
  49.2 2.8 %copy.89 = f32[2,22,3,128]{2,1,3,0:T(8,128)} copy(f32[2,22,3,128]{3,0,2,1:T(2,128)S(1)} %collective-permute-done.2) | data formatting | bytes 135168 | tf_op jit(solution)/shard_map/ppermute | solution.py:18
  52.1 2.8 %copy.91 = f32[2,22,3,128]{2,1,3,0:T(8,128)} copy(f32[2,22,3,128]{3,0,2,1:T(2,128)S(1)} %collective-permute-done.3) | data formatting | bytes 135168 | tf_op jit(solution)/shard_map/ppermute | solution.py:20
  60.8 1.7 %pad_maximum_fusion = f32[2,22,70,134]{2,1,3,0:T(8,128)S(1)} fusion(f32[2,22,70,3]{2,1,3,0:T(8,128)S(1)} %copy.95, f32[2,22,3,128]{2,1,3,0:T(8,128)S(1)} %copy-done.5, f32[2,22,64,128]{2,1,3,0:T(8,128)S(1)} %copy.90, f32[2,22,3,128]{2,1,3,0:T(8,128)S(1)} %copy-done.4, f32[2,22,70,3]{2,1,3,0:T(8,128)S(1)} %copy.94), kind=kLoop, calls=%fused_computation.5 | loop fusion | flops 1650880 | bytes 3301760 | tf_op jit(solution)/shard_map/concatenate | solution.py:16
  62.8 2.7 %fusion.17 = f32[16,64,131]{1,0,2:T(8,128)} fusion(f32[16,70,134]{1,0,2:T(8,128)S(1)} %slice_bitcast_fusion.2, f32[20,70,134]{1,0,2:T(8,128)S(1)} %slice_bitcast_fusion), kind=kLoop, calls=%fused_computation.48 | loop fusion | flops 1073152 | bytes 3756032 | tf_op jit(solution)/shard_map/mul | solution.py:53
  65.5 2.4 %fusion.49 = f32[16,67,128]{1,0,2:T(8,128)} fusion(f32[16,70,134]{1,0,2:T(8,128)S(1)} %slice_bitcast_fusion.2, f32[20,70,134]{1,0,2:T(8,128)S(1)} %slice_bitcast_fusion), kind=kLoop, calls=%fused_computation.100 | loop fusion | flops 1097728 | bytes 3842048 | tf_op jit(solution)/shard_map/mul | solution.py:53
  68.0 3.7 %fusion.7 = f32[19,64,128]{1,0,2:T(8,128)} fusion(f32[22,70,134]{1,0,2:T(8,128)S(1)} %slice_bitcast_fusion.1, f32[20,70,134]{1,0,2:T(8,128)S(1)} %slice_bitcast_fusion), kind=kLoop, calls=%fused_computation.19 | loop fusion | flops 1245184 | bytes 4358144 | tf_op jit(solution)/shard_map/mul | solution.py:53
  71.7 6.5 %scatter_custom_fusion.2 = f32[1024,128]{1,0:T(8,128)S(1)} fusion(s32[1024]{0:T(1024)S(1)} %bitcast.54, f32[1024,128]{1,0:T(8,128)} %bitcast.13, f32[]{:T(128)} %constant.20.clone.1), kind=kCustom, calls=%fused_computation.108 | custom fusion | flops 131072 | bytes 524800 | tf_op jit(solution)/shard_map/scatter-add | solution.py:100
  79.7 7.8 %fusion.41 = f32[16,64,128]{1,0,2:T(8,128)S(1)} fusion(f32[16,64,128]{1,0,2:T(8,128)} %copy.98, f32[16,64,128]{1,0,2:T(8,128)} %copy.97, f32[16,64,131]{1,0,2:T(8,128)} %fusion.17, f32[16,67,128]{1,0,2:T(8,128)} %fusion.49, f32[19,64,128]{1,0,2:T(8,128)} %fusion.7, f32[16,64,128]{1,0,2:T(8,128)} %copy.86, f32[16,64,128]{1,0,2:T(8,128)} %copy.85), kind=kLoop, calls=%fused_computation.87 | loop fusion | flops 2621440 | bytes 8912896 | tf_op jit(solution)/shard_map/add | solution.py:106
  87.7 3.8 %collective-permute-start.6 = (f32[3,64,128]{1,0,2:T(4,128)S(1)}, f32[3,64,128]{1,0,2:T(4,128)S(1)}, u32[]{:S(2)}, u32[]{:S(2)}) collective-permute-start(f32[3,64,128]{1,0,2:T(4,128)S(1)} %get-tuple-element.18), channel_id=1, source_target_pairs={{0,8},{8,16},{16,24},{1,9},{9,17},{17,25},{2,10},{10,18},{18,26},{... | collective-permute-start | bytes 294920 | tf_op jit(solution)/shard_map/ppermute | solution.py:18
  93.0 4.3 %collective-permute-done.6 = f32[3,64,128]{1,0,2:T(4,128)S(1)} collective-permute-done((f32[3,64,128]{1,0,2:T(4,128)S(1)}, f32[3,64,128]{1,0,2:T(4,128)S(1)}, u32[]{:S(2)}, u32[]{:S(2)}) %collective-permute-start.6) | collective-permute-done | bytes 98336 | tf_op jit(solution)/shard_map/ppermute | solution.py:18
  97.3 4.1 %collective-permute-done.7 = f32[3,64,128]{1,0,2:T(4,128)S(1)} collective-permute-done((f32[3,64,128]{1,0,2:T(4,128)S(1)}, f32[3,64,128]{1,0,2:T(4,128)S(1)}, u32[]{:S(2)}, u32[]{:S(2)}) %collective-permute-start.7) | collective-permute-done | bytes 98336 | tf_op jit(solution)/shard_map/ppermute | solution.py:20
  101.8 2.1 %fusion.63 = (f32[22,3,128]{1,0,2:T(8,128)}, f32[22,3,128]{1,0,2:T(8,128)}) fusion(f32[22,64,128]{1,0,2:T(8,128)S(1)} %pad_maximum_fusion.2), kind=kLoop, calls=%fused_computation.136 | loop fusion | bytes 135168 | tf_op jit(solution)/shard_map/slice | solution.py:15
  103.9 1.9 %copy.100 = f32[22,3,128]{2,0,1:T(8,128)S(1)} copy(f32[22,3,128]{1,0,2:T(8,128)} %get-tuple-element.14) | data formatting | bytes 67584 | tf_op jit(solution)/shard_map/slice | solution.py:15
  105.8 3.4 %collective-permute-start.8 = (f32[22,3,128]{2,0,1:T(8,128)S(1)}, f32[22,3,128]{2,0,1:T(8,128)S(1)}, u32[]{:S(2)}, u32[]{:S(2)}) collective-permute-start(f32[22,3,128]{2,0,1:T(8,128)S(1)} %copy.100), channel_id=1, source_target_pairs={{0,2},{2,4},{4,6},{1,3},{3,5},{5,7},{8,10},{10,12},{12,14},{9,11},... | collective-permute-start | bytes 101384 | tf_op jit(solution)/shard_map/ppermute | solution.py:18
  109.2 1.9 %copy.101 = f32[22,3,128]{2,0,1:T(8,128)S(1)} copy(f32[22,3,128]{1,0,2:T(8,128)} %get-tuple-element.15) | data formatting | bytes 67584 | tf_op jit(solution)/shard_map/slice | solution.py:14
  112.4 4.3 %fusion.3 = f32[19,64,128]{1,0,2:T(8,128)} fusion(f32[22,64,128]{1,0,2:T(8,128)} %copy-done.3, f32[3,64,128]{1,0,2:T(4,128)S(1)} %collective-permute-done.7, f32[16,64,128]{1,0,2:T(8,128)S(1)} %fusion.41, f32[3,64,128]{1,0,2:T(4,128)S(1)} %collective-permute-done.6, f32[20,70,134]{1,0,2:T(8,128)S(1)} %slice_bitcast_fusion), kind=kLoop, calls=%fused_computation.13 | loop fusion | flops 1556480 | bytes 3833856 | tf_op jit(solution)/shard_map/mul | solution.py:53
  116.6 1.7 %copy.102 = f32[22,3,128]{1,0,2:T(8,128)} copy(f32[22,3,128]{2,0,1:T(8,128)S(1)} %collective-permute-done.8) | data formatting | bytes 67584 | tf_op jit(solution)/shard_map/ppermute | solution.py:18
  118.3 1.7 %copy.103 = f32[22,3,128]{1,0,2:T(8,128)} copy(f32[22,3,128]{2,0,1:T(8,128)S(1)} %collective-permute-done.9) | data formatting | bytes 67584 | tf_op jit(solution)/shard_map/ppermute | solution.py:20
  124.9 1.9 %fusion.32 = f32[16,67,128]{1,0,2:T(8,128)S(1)} fusion(f32[22,3,128]{1,0,2:T(8,128)S(1)} %copy-done, f32[3,64,128]{1,0,2:T(4,128)S(1)} %collective-permute-done.7, f32[16,64,128]{1,0,2:T(8,128)S(1)} %fusion.41, f32[3,64,128]{1,0,2:T(4,128)S(1)} %collective-permute-done.6, f32[22,3,128]{1,0,2:T(8,128)S(1)} %copy-done.1, ...), kind=kLoop, calls=%fused_computation.69 | loop fusion | flops 1921024 | bytes 3532800 | tf_op jit(solution)/shard_map/mul | solution.py:53
  128.0 2.3 %fusion.12 = f32[16,64,131]{1,0,2:T(8,128)S(1)} fusion(f32[22,70,3]{1,0,2:T(8,128)S(1)} %collective-permute-done.10, f32[22,3,128]{1,0,2:T(8,128)S(1)} %copy-done.1, f32[22,3,128]{1,0,2:T(8,128)S(1)} %copy-done, f32[3,64,128]{1,0,2:T(4,128)S(1)} %collective-permute-done.7, f32[16,64,128]{1,0,2:T(8,128)S(1)} %fusion.41, ...), kind=kLoop, calls=%fused_computation.31 | loop fusion | flops 2414592 | bytes 3508320 | tf_op jit(solution)/shard_map/mul | solution.py:53
  132.0 4.0 %gather_fusion = f32[1024,128]{1,0:T(8,128)} fusion(f32[1024,128]{1,0:T(8,128)S(1)} %bitcast.40, s32[1024]{0:T(1024)S(1)} %broadcast_clamp_fusion), kind=kCustom, calls=%fused_computation | custom fusion | bytes 1052672 | tf_op jit(solution)/shard_map/gather | solution.py:114
  136.0 6.7 %all-to-all-start.2 = ((f32[16,64,128]{2,1,0:T(8,128)}), f32[16,64,128]{2,1,0:T(8,128)S(1)}, u32[]{:S(2)}, u32[]{:S(2)}) async-start(f32[16,64,128]{2,1,0:T(8,128)} %bitcast.17), calls=%async_computation.2 | async-start | bytes 1048576 | tf_op jit(solution)/shard_map/all_to_all | solution.py:68
  142.7 15.3 %all-to-all-done.2 = f32[16,64,128]{2,1,0:T(8,128)S(1)} async-done(((f32[16,64,128]{2,1,0:T(8,128)}), f32[16,64,128]{2,1,0:T(8,128)S(1)}, u32[]{:S(2)}, u32[]{:S(2)}) %all-to-all-start.2) | async-done | bytes 524320 | tf_op jit(solution)/shard_map/all_to_all | solution.py:68
  158.1 1.6 %gather_fusion.1 = f32[512,128]{1,0:T(8,128)} fusion(f32[1024,128]{1,0:T(8,128)S(1)} %bitcast.41, s32[1024]{0:T(1024)S(1)} %pad_clamp_fusion), kind=kCustom, calls=%fused_computation.1 | custom fusion | bytes 526336 | tf_op jit(solution)/shard_map/gather | solution.py:116
  (90 shorter events, 32.8 us)
Async XLA Ops:
  0.6 14.4 %copy-start.11 = (f32[16,64,128]{2,1,0:T(8,128)S(1)}, f32[16,64,128]{2,1,0:T(8,128)}, u32[]{:S(2)}) copy-start(f32[16,64,128]{2,1,0:T(8,128)} %param.7) | copy-start | bytes 1572868
  0.6 14.4 %copy-start.12 = (f32[16,64,128]{2,1,0:T(8,128)S(1)}, f32[16,64,128]{2,1,0:T(8,128)}, u32[]{:S(2)}) copy-start(f32[16,64,128]{2,1,0:T(8,128)} %param.9) | copy-start | bytes 1572868
  0.6 9.5 %copy-start.15 = (s32[512,1]{0,1:T(1,128)S(1)}, s32[512,1]{0,1:T(1,128)}, u32[]{:S(2)}) copy-start(s32[512,1]{0,1:T(1,128)} %param.12) | copy-start | bytes 6148
  1.8 9.1 %collective-permute-start = (f32[2,3,64,128]{3,2,1,0:T(8,128)S(1)}, f32[2,3,64,128]{3,2,1,0:T(8,128)S(1)}, u32[]{:S(2)}, u32[]{:S(2)}) collective-permute-start(f32[2,3,64,128]{3,2,1,0:T(8,128)S(1)} %get-tuple-element.20), channel_id=1, source_target_pairs={{0,8},{8,16},{16,24},{1,9},{9,17},{17,25},{2,10},{10,18},{18,26},{... | collective-permute-start | bytes 589832 | tf_op jit(solution)/shard_map/ppermute | solution.py:18
  6.8 8.3 %collective-permute-start.1 = (f32[2,3,64,128]{3,2,1,0:T(8,128)S(1)}, f32[2,3,64,128]{3,2,1,0:T(8,128)S(1)}, u32[]{:S(2)}, u32[]{:S(2)}) collective-permute-start(f32[2,3,64,128]{3,2,1,0:T(8,128)S(1)} %get-tuple-element.21), channel_id=1, source_target_pairs={{8,0},{16,8},{24,16},{9,1},{17,9},{25,17},{10,2},{18,10},{26,18},{... | collective-permute-start | bytes 589832 | tf_op jit(solution)/shard_map/ppermute | solution.py:20
  15.2 1.1 copy-start.10
  16.3 16.7 %copy-start.13 = (f32[16,64,128]{2,1,0:T(8,128)S(1)}, f32[16,64,128]{2,1,0:T(8,128)}, u32[]{:S(2)}) copy-start(f32[16,64,128]{2,1,0:T(8,128)} %param.10) | copy-start | bytes 1572868
  16.4 32.8 %collective-permute-start.2 = (f32[2,22,3,128]{3,0,2,1:T(2,128)S(1)}, f32[2,22,3,128]{3,0,2,1:T(2,128)S(1)}, u32[]{:S(2)}, u32[]{:S(2)}) collective-permute-start(f32[2,22,3,128]{3,0,2,1:T(2,128)S(1)} %copy.110), channel_id=1, source_target_pairs={{0,2},{2,4},{4,6},{1,3},{3,5},{5,7},{8,10},{10,12},{12,14},{9,11},... | collective-permute-start | bytes 202760 | tf_op jit(solution)/shard_map/ppermute | solution.py:18
  20.0 32.1 %collective-permute-start.3 = (f32[2,22,3,128]{3,0,2,1:T(2,128)S(1)}, f32[2,22,3,128]{3,0,2,1:T(2,128)S(1)}, u32[]{:S(2)}, u32[]{:S(2)}) collective-permute-start(f32[2,22,3,128]{3,0,2,1:T(2,128)S(1)} %copy.111), channel_id=1, source_target_pairs={{2,0},{4,2},{6,4},{3,1},{5,3},{7,5},{10,8},{12,10},{14,12},{11,9},... | collective-permute-start | bytes 202760 | tf_op jit(solution)/shard_map/ppermute | solution.py:20
  24.6 14.2 %all-to-all-start = ((s32[16,1,64]{2,1,0:T(1,128)}), s32[16,1,64]{2,1,0:T(1,128)S(1)}, u32[]{:S(2)}, u32[]{:S(2)}) async-start(s32[16,1,64]{2,1,0:T(1,128)} %all_to_all.12), calls=%async_computation | async-start | bytes 16384 | tf_op jit(solution)/shard_map/all_to_all | solution.py:61
  31.6 2.8 %copy-start.14 = (f32[16,64,128]{2,1,0:T(8,128)S(1)}, f32[16,64,128]{2,1,0:T(8,128)}, u32[]{:S(2)}) copy-start(f32[16,64,128]{2,1,0:T(8,128)} %param.8) | copy-start | bytes 1572868
  38.8 33.0 %all-to-all-start.1 = ((f32[16,64,128]{2,1,0:T(8,128)}), f32[16,64,128]{2,1,0:T(8,128)}, u32[]{:S(2)}, u32[]{:S(2)}) async-start(f32[16,64,128]{2,1,0:T(8,128)} %bitcast.12), calls=%async_computation.1 | async-start | bytes 1048576 | tf_op jit(solution)/shard_map/all_to_all | solution.py:60
  54.8 6.0 %copy-start.4 = (f32[2,22,3,128]{2,1,3,0:T(8,128)S(1)}, f32[2,22,3,128]{2,1,3,0:T(8,128)}, u32[]{:S(2)}) copy-start(f32[2,22,3,128]{2,1,3,0:T(8,128)} %copy.89) | copy-start | bytes 202756
  54.8 6.0 %copy-start.5 = (f32[2,22,3,128]{2,1,3,0:T(8,128)S(1)}, f32[2,22,3,128]{2,1,3,0:T(8,128)}, u32[]{:S(2)}) copy-start(f32[2,22,3,128]{2,1,3,0:T(8,128)} %copy.91) | copy-start | bytes 202756
  56.2 3.0 %collective-permute-start.4 = (f32[2,22,70,3]{2,0,3,1:T(2,128)S(1)}, f32[2,22,70,3]{2,0,3,1:T(2,128)S(1)}, u32[]{:S(2)}, u32[]{:S(2)}) collective-permute-start(f32[2,22,70,3]{2,0,3,1:T(2,128)S(1)} %copy.92), channel_id=1, source_target_pairs={{0,1},{2,3},{4,5},{6,7},{8,9},{10,11},{12,13},{14,15},{16,17},{18,... | collective-permute-start | bytes 110888 | tf_op jit(solution)/shard_map/ppermute | solution.py:18
  57.7 3.2 %collective-permute-start.5 = (f32[2,22,70,3]{2,0,3,1:T(2,128)S(1)}, f32[2,22,70,3]{2,0,3,1:T(2,128)S(1)}, u32[]{:S(2)}, u32[]{:S(2)}) collective-permute-start(f32[2,22,70,3]{2,0,3,1:T(2,128)S(1)} %copy.93), channel_id=1, source_target_pairs={{1,0},{3,2},{5,4},{7,6},{9,8},{11,10},{13,12},{15,14},{17,16},{19,... | collective-permute-start | bytes 110888 | tf_op jit(solution)/shard_map/ppermute | solution.py:20
  87.7 9.6 %collective-permute-start.6 = (f32[3,64,128]{1,0,2:T(4,128)S(1)}, f32[3,64,128]{1,0,2:T(4,128)S(1)}, u32[]{:S(2)}, u32[]{:S(2)}) collective-permute-start(f32[3,64,128]{1,0,2:T(4,128)S(1)} %get-tuple-element.18), channel_id=1, source_target_pairs={{0,8},{8,16},{16,24},{1,9},{9,17},{17,25},{2,10},{10,18},{18,26},{... | collective-permute-start | bytes 294920 | tf_op jit(solution)/shard_map/ppermute | solution.py:18
  91.5 10.0 %collective-permute-start.7 = (f32[3,64,128]{1,0,2:T(4,128)S(1)}, f32[3,64,128]{1,0,2:T(4,128)S(1)}, u32[]{:S(2)}, u32[]{:S(2)}) collective-permute-start(f32[3,64,128]{1,0,2:T(4,128)S(1)} %get-tuple-element.19), channel_id=1, source_target_pairs={{8,0},{16,8},{24,16},{9,1},{17,9},{25,17},{10,2},{18,10},{26,18},{... | collective-permute-start | bytes 294920 | tf_op jit(solution)/shard_map/ppermute | solution.py:20
  101.8 2.2 %copy-start.3 = (f32[22,64,128]{1,0,2:T(8,128)}, f32[22,64,128]{1,0,2:T(8,128)S(1)}, u32[]{:S(2)}) copy-start(f32[22,64,128]{1,0,2:T(8,128)S(1)} %pad_maximum_fusion.2) | copy-start | bytes 2162692
  105.8 10.8 %collective-permute-start.8 = (f32[22,3,128]{2,0,1:T(8,128)S(1)}, f32[22,3,128]{2,0,1:T(8,128)S(1)}, u32[]{:S(2)}, u32[]{:S(2)}) collective-permute-start(f32[22,3,128]{2,0,1:T(8,128)S(1)} %copy.100), channel_id=1, source_target_pairs={{0,2},{2,4},{4,6},{1,3},{3,5},{5,7},{8,10},{10,12},{12,14},{9,11},... | collective-permute-start | bytes 101384 | tf_op jit(solution)/shard_map/ppermute | solution.py:18
  111.1 7.2 %collective-permute-start.9 = (f32[22,3,128]{2,0,1:T(8,128)S(1)}, f32[22,3,128]{2,0,1:T(8,128)S(1)}, u32[]{:S(2)}, u32[]{:S(2)}) collective-permute-start(f32[22,3,128]{2,0,1:T(8,128)S(1)} %copy.101), channel_id=1, source_target_pairs={{2,0},{4,2},{6,4},{3,1},{5,3},{7,5},{10,8},{12,10},{14,12},{11,9},... | collective-permute-start | bytes 101384 | tf_op jit(solution)/shard_map/ppermute | solution.py:20
  120.0 3.7 %copy-start = (f32[22,3,128]{1,0,2:T(8,128)S(1)}, f32[22,3,128]{1,0,2:T(8,128)}, u32[]{:S(2)}) copy-start(f32[22,3,128]{1,0,2:T(8,128)} %copy.102) | copy-start | bytes 101380
  120.0 3.7 %copy-start.1 = (f32[22,3,128]{1,0,2:T(8,128)S(1)}, f32[22,3,128]{1,0,2:T(8,128)}, u32[]{:S(2)}) copy-start(f32[22,3,128]{1,0,2:T(8,128)} %copy.103) | copy-start | bytes 101380
  121.1 5.7 %collective-permute-start.10 = (f32[22,70,3]{1,0,2:T(8,128)S(1)}, f32[22,70,3]{1,0,2:T(8,128)S(1)}, u32[]{:S(2)}, u32[]{:S(2)}) collective-permute-start(f32[22,70,3]{1,0,2:T(8,128)S(1)} %get-tuple-element.13), channel_id=1, source_target_pairs={{0,1},{2,3},{4,5},{6,7},{8,9},{10,11},{12,13},{14,15},{16,17},{18,... | collective-permute-start | bytes 55448 | tf_op jit(solution)/shard_map/ppermute | solution.py:18
  122.4 4.4 %collective-permute-start.11 = (f32[22,70,3]{1,0,2:T(8,128)S(1)}, f32[22,70,3]{1,0,2:T(8,128)S(1)}, u32[]{:S(2)}, u32[]{:S(2)}) collective-permute-start(f32[22,70,3]{1,0,2:T(8,128)S(1)} %get-tuple-element.12), channel_id=1, source_target_pairs={{1,0},{3,2},{5,4},{7,6},{9,8},{11,10},{13,12},{15,14},{17,16},{19,... | collective-permute-start | bytes 55448 | tf_op jit(solution)/shard_map/ppermute | solution.py:20
  128.0 2.4 %copy-start.6 = (f32[19,64,128]{1,0,2:T(8,128)S(1)}, f32[19,64,128]{1,0,2:T(8,128)}, u32[]{:S(2)}) copy-start(f32[19,64,128]{1,0,2:T(8,128)} %fusion.3) | copy-start | bytes 1867780
  128.0 2.4 %copy-start.7 = (f32[16,64,128]{1,0,2:T(8,128)S(1)}, f32[16,64,128]{1,0,2:T(8,128)}, u32[]{:S(2)}) copy-start(f32[16,64,128]{1,0,2:T(8,128)} %copy.85) | copy-start | bytes 1572868
  128.0 2.4 %copy-start.8 = (f32[16,64,128]{1,0,2:T(8,128)S(1)}, f32[16,64,128]{1,0,2:T(8,128)}, u32[]{:S(2)}) copy-start(f32[16,64,128]{1,0,2:T(8,128)} %copy.98) | copy-start | bytes 1572868
  128.0 2.4 %copy-start.9 = (f32[16,64,128]{1,0,2:T(8,128)S(1)}, f32[16,64,128]{1,0,2:T(8,128)}, u32[]{:S(2)}) copy-start(f32[16,64,128]{1,0,2:T(8,128)} %copy.97) | copy-start | bytes 1572868
  132.0 4.0 %copy-start.2 = (f32[16,64,128]{2,1,0:T(8,128)}, f32[16,64,128]{2,1,0:T(8,128)S(1)}, u32[]{:S(2)}) copy-start(f32[16,64,128]{2,1,0:T(8,128)S(1)} %copy.109) | copy-start | bytes 1572868
  136.0 22.1 %all-to-all-start.2 = ((f32[16,64,128]{2,1,0:T(8,128)}), f32[16,64,128]{2,1,0:T(8,128)S(1)}, u32[]{:S(2)}, u32[]{:S(2)}) async-start(f32[16,64,128]{2,1,0:T(8,128)} %bitcast.17), calls=%async_computation.2 | async-start | bytes 1048576 | tf_op jit(solution)/shard_map/all_to_all | solution.py:68
where the time goes:
time: 161 us; the launch traced here: 160 us
  starting transfers between devices  47.2 us (29%)
  other arithmetic  43.5 us (27%)
  local copies, waits for them, and re-layouts  37.7 us (23%)
  waiting for transfers between devices  30.2 us (19%)
    ppermute x6, starting transfers between devices, extended(): lax.ppermute(tail, axis, [(i, (i + 1) % count) for i in range(ends)])  18.4 us
    mul x6, other arithmetic, operator(): axis_term = fourth_diff(gradient * face_buoy, along_dim, length_out)  17.3 us
    all_to_all x1, waiting for transfers between devices, route_back(): lax.all_to_all(sampled.reshape(num_gx * num_gy, capacity, depth_len), ('g...  15.3 us
    ppermute x6, waiting for transfers between devices, extended(): lax.ppermute(head, axis, [((i + 1) % count, i) for i in range(ends)])  9.88 us
    ppermute x6, starting transfers between devices, extended(): lax.ppermute(head, axis, [((i + 1) % count, i) for i in range(ends)])  8.16 us
    add x1, other arithmetic, local(): 2.0 * pressure - pressure_prev  7.83 us
    all_to_all x1, starting transfers between devices, route_out(): lax.all_to_all(dest_cols, ('gx', 'gy'), split_axis=0, concat_axis=0, tile...  7 us
    all_to_all x1, starting transfers between devices, route_out(): lax.all_to_all(outgoing, ('gx', 'gy'), split_axis=0, concat_axis=0, tiled...  6.94 us
  transfers between devices with their start and end apart: 15, of which 6 were waited for; matrix products, arithmetic and copies ran while one was open for 28% of the time, Pallas kernels for 0%

commit v1 on v0

v1 whole, which is shorter than its diff:
```python
import functools

import jax
import jax.numpy as jnp
from jax import lax
from jax.experimental import pallas as pl
from jax.experimental.pallas import tpu as pltpu
from jax.sharding import PartitionSpec as P

courant_sq = 0.05
source_gain = 0.5
lap_scale = courant_sq * 0.5 / (24.0 * 24.0)
halo = 3
tile = 8
f32 = jnp.float32
bf16 = jnp.bfloat16
VMEM_LIMIT = 16 << 20


def run(kernel, outs, *args, flops=0, scratch=()):
    size = sum(4 * a.size for a in args) + sum(4 * o.size for o in outs)
    spec = pl.BlockSpec(memory_space=pltpu.VMEM)
    return pl.pallas_call(
        kernel,
        out_shape=outs,
        in_specs=[spec] * len(args),
        out_specs=[spec] * len(outs),
        scratch_shapes=scratch,
        compiler_params=pltpu.CompilerParams(vmem_limit_bytes=VMEM_LIMIT),
        cost_estimate=pl.CostEstimate(flops=flops, bytes_accessed=size, transcendentals=0),
    )(*args)


def shaped(*shape, dtype=f32):
    return jax.ShapeDtypeStruct(shape, dtype)


def dot(a, b, contract=((1,), (0,))):
    return lax.dot_general(a, b, (contract, ((), ())), preferred_element_type=f32)


def parts_of(x):
    high = x.astype(bf16)
    rest = x - high.astype(f32)
    middle = rest.astype(bf16)
    low = (rest - middle.astype(f32)).astype(bf16)
    return jnp.concatenate([high, middle, low], axis=1)


def select_rows(one_hot, x):
    lanes = x.shape[1]
    y = dot(one_hot, parts_of(x))
    return y[:, :lanes] + y[:, lanes : 2 * lanes] + y[:, 2 * lanes :]


def one_hot_of(index, shape, dim):
    return jnp.where(lax.broadcasted_iota(jnp.int32, shape, dim) == index, 1.0, 0.0).astype(bf16)


def as_column(row):
    n = row.shape[1]
    diagonal = lax.broadcasted_iota(jnp.int32, (n, n), 0) == lax.broadcasted_iota(jnp.int32, (n, n), 1)
    return jnp.sum(jnp.where(diagonal, row, 0.0), axis=1, keepdims=True)


def pack_kernel(groups, cap, block_ref, column_ref, accel_ref, out_ref, place_ref):
    rows, lanes = accel_ref.shape
    stride = cap + tile
    block = block_ref[...]
    column = column_ref[...] + 1
    named = lax.broadcasted_iota(jnp.int32, (groups, rows), 0) == block
    matches = jnp.where(named, 1.0, 0.0).astype(bf16)
    before = lax.broadcasted_iota(jnp.int32, (rows, rows), 0) < lax.broadcasted_iota(jnp.int32, (rows, rows), 1)
    earlier = dot(matches, jnp.where(before, 1.0, 0.0).astype(bf16))
    slot = jnp.sum(jnp.where(named, earlier, 0.0), axis=0, keepdims=True).astype(jnp.int32)
    place_ref[...] = (block * cap + slot).astype(f32)
    out_ref[...] = select_rows(one_hot_of(block * stride + slot, (groups * stride, rows), 0), accel_ref[...])
    at_slot = lax.broadcasted_iota(jnp.int32, (lanes, rows), 0) % cap == slot
    high = jnp.where(at_slot, column // 32, 0).astype(f32).astype(bf16)
    low = jnp.where(at_slot, column % 32, 0).astype(f32).astype(bf16)
    columns = dot(matches, high, ((1,), (1,))) * 32.0 + dot(matches, low, ((1,), (1,)))
    for g in range(groups):
        out_ref[g * stride + cap : (g + 1) * stride, :] = jnp.broadcast_to(columns[g : g + 1], (tile, lanes))


def column_rows(got_ref, cap):
    groups, _, lanes = got_ref.shape
    per = lanes // cap
    lane = lax.broadcasted_iota(jnp.int32, (1, lanes), 1) // cap
    rows = []
    for g in range(0, groups, per):
        row = got_ref[g, cap : cap + 1, :]
        for k in range(1, per):
            row = jnp.where(lane == k, got_ref[g + k, cap : cap + 1, :], row)
        rows.append(row - 1.0)
    return rows


def mid_kernel(cap, got_ref, mid0_ref, kappa_ref, mid_ref, xe_ref, xo_ref, ye_ref, yo_ref, spread_ref):
    groups, _, lanes = got_ref.shape
    cx, cy, cz = mid0_ref.shape
    for at, row in enumerate(column_rows(got_ref, cap)):
        spread_ref[:, at * lanes : (at + 1) * lanes] = one_hot_of(row.astype(jnp.int32), (cx * cy, lanes), 0)
    rows = got_ref[:, :cap, :].reshape(groups * cap, lanes)
    source = select_rows(spread_ref[...], rows).reshape(cx, cy, cz)
    mid_ref[...] = mid0_ref[...] + kappa_ref[...] * (source_gain * source)
    send_faces(mid_ref, halo, xe_ref, xo_ref, ye_ref, yo_ref)


def gather_map_kernel(cap, cols, got_ref, map_ref):
    lanes = got_ref.shape[2]
    for at, row in enumerate(column_rows(got_ref, cap)):
        column = as_column(row).astype(jnp.int32)
        map_ref[at * lanes : (at + 1) * lanes, :] = one_hot_of(column, (lanes, cols), 1)


def unpack_map_kernel(lanes, place_ref, map_ref):
    rows, slots = map_ref.shape
    for at in range(0, rows, lanes):
        column = as_column(place_ref[:, at : at + lanes]).astype(jnp.int32)
        map_ref[at : at + lanes, :] = one_hot_of(column, (lanes, slots), 1)


def unpack_kernel(map_ref, returned_ref, out_ref):
    slots = map_ref.shape[1]
    out_ref[...] = select_rows(map_ref[...], returned_ref[...].reshape(slots, -1))


def start_of(axis, low, high, even_takes_high):
    even = lax.axis_index(axis) % 2 == 0
    return jnp.where(even, high, low) if even_takes_high else jnp.where(even, low, high)


def send_faces(ref, width, xe_ref, xo_ref, ye_ref, yo_ref):
    cx, cy, _ = ref.shape
    xe_ref[...] = ref[pl.ds(start_of("gx", 0, cx - width, True), width)]
    xo_ref[...] = ref[pl.ds(start_of("gx", 0, cx - width, False), width)]
    ye_ref[...] = ref[:, pl.ds(pl.multiple_of(start_of("gy", 0, cy - tile, True), tile), tile), :]
    yo_ref[...] = ref[:, pl.ds(pl.multiple_of(start_of("gy", 0, cy - tile, False), tile), tile), :]


def low_and_high(axis, from_even, from_odd):
    at = lax.axis_index(axis)
    even = at % 2 == 0
    low = jnp.where(at > 0, jnp.where(even, from_odd, from_even), 0.0)
    high = jnp.where(at < lax.axis_size(axis) - 1, jnp.where(even, from_even, from_odd), 0.0)
    return low, high


def swap_pairs(sizes, axis, first):
    num_gx, num_gy, num_blk = sizes
    pairs = []
    for x in range(num_gx):
        for y in range(num_gy):
            for b in range(num_blk):
                at, count = (x, num_gx) if axis == "gx" else (y, num_gy)
                other = at + 1 if at % 2 == first else at - 1
                if 0 <= other < count:
                    to = (other, y, b) if axis == "gx" else (x, other, b)
                else:
                    to = (x, y, num_blk - 1 - b)
                pairs.append(((x * num_gy + y) * num_blk + b, (to[0] * num_gy + to[1]) * num_blk + to[2]))
    return pairs


def exchange(xe, xo, ye, yo):
    axes = ("gx", "gy", "blk")
    sizes = tuple(lax.axis_size(a) for a in axes)
    return (
        lax.ppermute(xe, axes, swap_pairs(sizes, "gx", 0)),
        lax.ppermute(xo, axes, swap_pairs(sizes, "gx", 1)),
        lax.ppermute(ye, axes, swap_pairs(sizes, "gy", 0)),
        lax.ppermute(yo, axes, swap_pairs(sizes, "gy", 1)),
    )


def swap_cores(x):
    count = lax.axis_size("blk")
    return lax.ppermute(x, "blk", [(i, count - 1 - i) for i in range(count)])


def face_kernel(p_ref, b_ref, xe_ref, xo_ref, ye_ref, yo_ref):
    cx, cy, _ = p_ref.shape
    for ref, takes_high in ((xe_ref, True), (xo_ref, False)):
        ref[:halo] = p_ref[pl.ds(start_of("gx", 0, cx - halo, takes_high), halo)]
        ref[halo:] = b_ref[pl.ds(start_of("gx", 0, cx - 2, takes_high), 2)]
    row = lax.broadcasted_iota(jnp.int32, (cx, tile, 1), 1)
    for ref, takes_high in ((ye_ref, True), (yo_ref, False)):
        start = pl.multiple_of(start_of("gy", 0, cy - tile, takes_high), tile)
        p, b = p_ref[:, pl.ds(start, tile), :], b_ref[:, pl.ds(start, tile), :]
        low = jnp.where(row < halo, p, pltpu.roll(b, halo, 1))
        high = jnp.where(row >= tile - halo, p, pltpu.roll(b, tile - halo, 1))
        ref[...] = jnp.where(start == 0, low, high)


def ahead(x, beyond, lane, step):
    lanes = x.shape[-1]
    if step > 0:
        return pltpu.roll(jnp.where(lane < step, beyond, x), lanes - step, x.ndim - 1)
    return pltpu.roll(jnp.where(lane >= lanes + step, beyond, x), -step, x.ndim - 1)


def depth_halo(x, lane):
    start = jnp.where(lax.axis_index("blk") == 0, 0, x.shape[-1] - halo)
    return jnp.where((lane >= start) & (lane < start + halo), x, 0.0)


def diff(a, b, c, d):
    return 27.0 * (a - b) - (c - d)


def fill(pad_ref, own_ref, low_x, high_x, low_y, high_y):
    cx, cy, _ = own_ref.shape
    wide = (pad_ref.shape[0] - cx) // 2
    pad_ref[:wide, tile : tile + cy] = low_x
    pad_ref[wide + cx :, tile : tile + cy] = high_x
    pad_ref[wide : wide + cx, :tile] = low_y
    pad_ref[wide : wide + cx, tile : tile + cy] = own_ref[...]
    pad_ref[wide : wide + cx, tile + cy :] = high_y


def operator(own_ref, other_ref, pad_ref, fx_ref, fy_ref, bx_ref, by_ref, bz_ref, bh_ref, finish):
    cx, cy, cz = own_ref.shape
    lane = lax.broadcasted_iota(jnp.int32, (cy, cz), 1)
    for f in range(cx + 3):
        v = [pad_ref[f + k, tile : tile + cy, :] for k in range(4)]
        fx_ref[f] = diff(v[2], v[1], v[3], v[0]) * bx_ref[f]
    long = cy + tile
    for i in range(cx):
        total = diff(fx_ref[i + 2], fx_ref[i + 1], fx_ref[i + 3], fx_ref[i])
        v = [pad_ref[i + halo, 5 + k : 5 + k + long, :] for k in range(4)]
        fy_ref[i % 2] = diff(v[2], v[1], v[3], v[0]) * by_ref[i]
        f = [fy_ref[i % 2, k : k + cy, :] for k in range(4)]
        total += diff(f[2], f[1], f[3], f[0])
        u = own_ref[i]
        h = depth_halo(other_ref[i], lane)
        fu = diff(ahead(u, h, lane, 1), u, ahead(u, h, lane, 2), ahead(u, h, lane, -1)) * bz_ref[i]
        fh = diff(ahead(h, u, lane, 1), h, ahead(h, u, lane, 2), ahead(h, u, lane, -1)) * bh_ref[i]
        total += diff(fu, ahead(fu, fh, lane, -1), ahead(fu, fh, lane, 1), ahead(fu, fh, lane, -2))
        finish(i, u, total)


def first_kernel(
    p_ref, b_ref, prev_ref, kappa_ref, xe_ref, xo_ref, ye_ref, yo_ref, po_ref, bo_ref,
    mid0_ref, bx_ref, by_ref, bz_ref, bh_ref, pad_ref, bpad_ref, fx_ref, fy_ref,
):
    cx, cy, cz = p_ref.shape
    low_x, high_x = low_and_high("gx", xe_ref[...], xo_ref[...])
    low_y, high_y = low_and_high("gy", ye_ref[...], yo_ref[...])
    fill(pad_ref, p_ref, low_x[:halo], high_x[:halo], low_y, high_y)
    fill(bpad_ref, b_ref, low_x[halo:], high_x[halo:], pltpu.roll(low_y, halo, 1), pltpu.roll(high_y, tile - halo, 1))
    lane = lax.broadcasted_iota(jnp.int32, (cy, cz), 1)
    for f in range(cx + 3):
        bx_ref[f] = bpad_ref[f, tile : tile + cy, :] + bpad_ref[f + 1, tile : tile + cy, :]
    long = cy + tile
    for i in range(cx):
        by_ref[i] = bpad_ref[i + 2, 6 : 6 + long, :] + bpad_ref[i + 2, 7 : 7 + long, :]
        u, h = b_ref[i], depth_halo(bo_ref[i], lane)
        bz_ref[i] = u + ahead(u, h, lane, 1)
        bh_ref[i] = h + ahead(h, u, lane, 1)

    def finish(i, u, total):
        mid0_ref[i] = 2.0 * u - prev_ref[i] + kappa_ref[i] * (lap_scale * total)

    operator(p_ref, po_ref, pad_ref, fx_ref, fy_ref, bx_ref, by_ref, bz_ref, bh_ref, finish)


def second_kernel(
    mid_ref, mid0_ref, p_ref, kappa_ref, xe_ref, xo_ref, ye_ref, yo_ref, mo_ref, bx_ref, by_ref, bz_ref, bh_ref, map_ref,
    next_ref, picked_ref, pad_ref, fx_ref, fy_ref,
):
    cx, cy, cz = p_ref.shape
    low_x, high_x = low_and_high("gx", xe_ref[...], xo_ref[...])
    low_y, high_y = low_and_high("gy", ye_ref[...], yo_ref[...])
    fill(pad_ref, mid_ref, low_x, high_x, low_y, high_y)

    def finish(i, u, total):
        next_ref[i] = 3.0 * u - mid0_ref[i] - p_ref[i] + kappa_ref[i] * (lap_scale * total)

    operator(mid_ref, mo_ref, pad_ref, fx_ref, fy_ref, bx_ref, by_ref, bz_ref, bh_ref, finish)
    picked_ref[...] = select_rows(map_ref[...], next_ref[...].reshape(cx * cy, cz)).reshape(picked_ref.shape)


def local(pressure, pressure_prev, buoyancy, kappa, hull_accel, row_block, row_column):
    groups = lax.axis_size("gx") * lax.axis_size("gy")
    rows, lanes = hull_accel.shape
    cap = 2 * rows // groups
    cx, cy, cz = pressure.shape
    slots, stride = groups * cap, cap + tile
    block = row_block.reshape(1, rows)
    column = row_column.reshape(1, rows)

    outgoing, place = run(
        functools.partial(pack_kernel, groups, cap),
        [shaped(groups * stride, lanes), shaped(1, rows)],
        block,
        column,
        hull_accel,
        flops=6 * groups * stride * rows * lanes,
    )
    got = lax.all_to_all(
        outgoing.reshape(groups, stride, lanes), ("gx", "gy"), split_axis=0, concat_axis=0, tiled=True
    )

    faces = run(
        face_kernel,
        [shaped(halo + 2, cy, cz)] * 2 + [shaped(cx, tile, cz)] * 2,
        pressure,
        buoyancy,
    )
    pads = [pltpu.VMEM((cx + 2 * halo, cy + 2 * tile, cz), f32)]
    fluxes = [pltpu.VMEM((cx + 3, cy, cz), f32), pltpu.VMEM((2, cy + tile, cz), f32)]
    mid0, *faced = run(
        first_kernel,
        [
            shaped(cx, cy, cz),
            shaped(cx + 3, cy, cz),
            shaped(cx, cy + tile, cz),
            shaped(cx, cy, cz),
            shaped(cx, cy, cz),
        ],
        pressure,
        buoyancy,
        pressure_prev,
        kappa,
        *exchange(*faces),
        swap_cores(pressure),
        swap_cores(buoyancy),
        flops=100 * cx * cy * cz,
        scratch=pads + [pltpu.VMEM((cx + 4, cy + 2 * tile, cz), f32)] + fluxes,
    )
    (unpack_map,) = run(
        functools.partial(unpack_map_kernel, lanes), [shaped(rows, slots, dtype=bf16)], place, flops=rows * slots
    )

    mid, *mid_faces = run(
        functools.partial(mid_kernel, cap),
        [shaped(cx, cy, cz)] + [shaped(halo, cy, cz)] * 2 + [shaped(cx, tile, cz)] * 2,
        got,
        mid0,
        kappa,
        flops=6 * cx * cy * slots * lanes,
        scratch=[pltpu.VMEM((cx * cy, slots), bf16)],
    )
    (gather_map,) = run(
        functools.partial(gather_map_kernel, cap, cx * cy),
        [shaped(slots, cx * cy, dtype=bf16)],
        got,
        flops=slots * cx * cy,
    )
    pressure_next, picked = run(
        second_kernel,
        [shaped(cx, cy, cz), shaped(groups, cap, lanes)],
        mid,
        mid0,
        pressure,
        kappa,
        *exchange(*mid_faces),
        swap_cores(mid),
        *faced,
        gather_map,
        flops=100 * cx * cy * cz + 6 * slots * cx * cy * lanes,
        scratch=pads + fluxes,
    )
    returned = lax.all_to_all(picked, ("gx", "gy"), split_axis=0, concat_axis=0, tiled=True)
    (hull_pressure,) = run(unpack_kernel, [shaped(rows, lanes)], unpack_map, returned, flops=6 * rows * slots * lanes)
    return pressure_next, hull_pressure


def solution(mesh):
    cells = P("gx", "gy", "blk")
    rows = P(("gx", "gy", "blk"), None)
    return jax.shard_map(
        local,
        mesh=mesh,
        in_specs=(cells, cells, cells, cells, rows, rows, rows),
        out_specs=(cells, rows),
        check_vma=False,
    )
```

time: 161 us -> 72.1 us (0.45)
  other arithmetic: 43.5 us -> 0 us
  local copies, waits for them, and re-layouts: 37.7 us -> 6.9 us
  starting transfers between devices: 47.2 us -> 24.8 us
  Pallas kernels: 0 us -> 11 us
  waiting for transfers between devices: 30.2 us -> 28 us
    mul x7 -> x0, other arithmetic: 17.3 us -> none  [the longest x6 17.3 us: operator(): axis_term = fourth_diff(gradient * face_buoy, along_dim, length_out)]
    ppermute x12 -> x11, starting transfers between devices: 26.5 us -> 10.5 us  [the longest x2 6.7 us: exchange(): lax.ppermute(xe, axes, swap_pairs(sizes, 'gx', 0))]
    pallas_call x0 -> x8, Pallas kernels: none -> 11 us  [run(): pl.pallas_call(kernel, out_shape=outs, in_specs=[spec] * len(args), out_s...]
    add x2 -> x0, other arithmetic: 9 us -> none  [the longest x1 7.83 us: local(): 2.0 * pressure - pressure_prev]
    ppermute x6 -> x0, local copies, waits for them, and re-layouts: 9 us -> none  [the longest x3 4.51 us: extended(): lax.ppermute(tail, axis, [(i, (i + 1) % count) for i in range(ends)])]
    slice x10 -> x0, local copies, waits for them, and re-layouts: 6.6 us -> none  [the longest x5 4.19 us: extended(): lax.slice_in_dim(cells, cells.shape[dim] - width, cells.shape[dim], axis=...]
    scatter-add x1 -> x0, other arithmetic: 6.54 us -> none  [local(): jnp.zeros((columns_all, depth_len), jnp.float32).at[target_idx]]
    all_to_all x3 -> x2, starting transfers between devices: 20.6 us -> 14.3 us  [the longest x1 8.31 us: local(): lax.all_to_all(outgoing.reshape(groups, stride, lanes), ('gx', 'gy'), spl...]
  transfers between devices with their start and end apart: 15 -> 13, of which waited for: 6 -> 5; matrix products, arithmetic and copies ran while one was open for 28% -> 0% of each run, Pallas kernels for 0% -> 5%
where the time goes in v1:
time: 72.1 us; the launch traced here: 71.6 us
  waiting for transfers between devices  28 us (39%)
  starting transfers between devices  24.8 us (34%)
  Pallas kernels  11 us (15%)
  local copies, waits for them, and re-layouts  6.9 us (10%)
  between operations  0.82 us (1%)
    all_to_all x1, waiting for transfers between devices, local(): lax.all_to_all(picked, ('gx', 'gy'), split_axis=0, concat_axis=0, tiled=T...  14.6 us
    pallas_call x8, Pallas kernels, run(): pl.pallas_call(kernel, out_shape=outs, in_specs=[spec] * len(args), out_s...  11 us
    all_to_all x1, starting transfers between devices, local(): lax.all_to_all(outgoing.reshape(groups, stride, lanes), ('gx', 'gy'), spl...  8.31 us
    unnamed x26, local copies, waits for them, and re-layouts  6.9 us
    ppermute x2, starting transfers between devices, exchange(): lax.ppermute(xe, axes, swap_pairs(sizes, 'gx', 0))  6.7 us
    ppermute x2, waiting for transfers between devices, exchange(): lax.ppermute(xe, axes, swap_pairs(sizes, 'gx', 0))  6.32 us
    all_to_all x1, starting transfers between devices, local(): lax.all_to_all(picked, ('gx', 'gy'), split_axis=0, concat_axis=0, tiled=T...  6.03 us
    ppermute x2, waiting for transfers between devices, exchange(): lax.ppermute(ye, axes, swap_pairs(sizes, 'gy', 0))  5.88 us
  transfers between devices with their start and end apart: 13, of which 5 were waited for; matrix products, arithmetic and copies ran while one was open for 0% of the time, Pallas kernels for 5%

profile of v1, /device:TPU:0, one launch (start us, length us, event | category | flops | bytes accessed | tf_op | source)
XLA Modules:
  0.0 71.6 jit_solution(1099946578598066046)
XLA Ops:
  0.7 1.1 %copy-done.10 = f32[512,128]{1,0:T(8,128)S(1)} copy-done((f32[512,128]{1,0:T(8,128)S(1)}, f32[512,128]{1,0:T(8,128)}, u32[]{:S(2)}) %copy-start.10) | copy-done | bytes 262168
  1.7 0.7 copy-done.11
  2.4 0.7 copy-done.12
  3.1 1.8 %shard_map.86 = (f32[1152,128]{1,0:T(8,128)}, f32[1,512]{1,0:T(1,128)S(1)}) custom-call(s32[1,512]{1,0:T(1,128)S(1)} %bitcast.3, s32[1,512]{1,0:T(1,128)S(1)} %bitcast.4, f32[512,128]{1,0:T(8,128)S(1)} %copy-done.10), custom_call_target="tpu_custom_call" | custom-call | flops 452984832 | bytes 858112 | tf_op jit(solution)/shard_map/pallas_call | solution.py:23
  4.9 8.3 %all-to-all-start = ((f32[16,72,128]{2,1,0:T(8,128)}), f32[16,72,128]{2,1,0:T(8,128)S(1)}, u32[]{:S(2)}, u32[]{:S(2)}) async-start(f32[16,72,128]{2,1,0:T(8,128)} %bitcast.2), calls=%async_computation | async-start | bytes 1179648 | tf_op jit(solution)/shard_map/all_to_all | solution.py:301
  13.2 0.1 collective-permute-start.4
  13.3 0.5 collective-permute-start.5
  13.8 0.1 shard_map.87
  13.9 2.0 %collective-permute-start = (f32[5,64,128]{2,1,0:T(8,128)S(1)}, f32[5,64,128]{2,1,0:T(8,128)S(1)}, u32[]{:S(2)}, u32[]{:S(2)}) collective-permute-start(f32[5,64,128]{2,1,0:T(8,128)S(1)} %get-tuple-element.21), channel_id=1, source_target_pairs={{0,8},{1,9},{2,10},{3,11},{4,12},{5,13},{6,14},{7,15},{8,0},{9,1},... | collective-permute-start | bytes 491528 | tf_op jit(solution)/shard_map/ppermute | solution.py:170
  15.9 1.5 %collective-permute-start.2 = (f32[16,8,128]{2,1,0:T(8,128)S(1)}, f32[16,8,128]{2,1,0:T(8,128)S(1)}, u32[]{:S(2)}, u32[]{:S(2)}) collective-permute-start(f32[16,8,128]{2,1,0:T(8,128)S(1)} %get-tuple-element.23), channel_id=1, source_target_pairs={{0,2},{1,3},{2,0},{3,1},{4,6},{5,7},{6,4},{7,5},{8,10},{9,11},{10,... | collective-permute-start | bytes 196616 | tf_op jit(solution)/shard_map/ppermute | solution.py:172
  17.3 3.5 %collective-permute-done.2.ye_ref = f32[16,8,128]{2,1,0:T(8,128)S(1)} collective-permute-done((f32[16,8,128]{2,1,0:T(8,128)S(1)}, f32[16,8,128]{2,1,0:T(8,128)S(1)}, u32[]{:S(2)}, u32[]{:S(2)}) %collective-permute-start.2) | collective-permute-done | bytes 65568 | tf_op jit(solution)/shard_map/ppermute | solution.py:172
  20.9 1.3 %collective-permute-done.3.yo_ref = f32[16,8,128]{2,1,0:T(8,128)S(1)} collective-permute-done((f32[16,8,128]{2,1,0:T(8,128)S(1)}, f32[16,8,128]{2,1,0:T(8,128)S(1)}, u32[]{:S(2)}, u32[]{:S(2)}) %collective-permute-start.3) | collective-permute-done | bytes 65568 | tf_op jit(solution)/shard_map/ppermute | solution.py:173
  22.1 6.3 %collective-permute-done.xe_ref = f32[5,64,128]{2,1,0:T(8,128)S(1)} collective-permute-done((f32[5,64,128]{2,1,0:T(8,128)S(1)}, f32[5,64,128]{2,1,0:T(8,128)S(1)}, u32[]{:S(2)}, u32[]{:S(2)}) %collective-permute-start) | collective-permute-done | bytes 163872 | tf_op jit(solution)/shard_map/ppermute | solution.py:170
  28.5 1.0 %copy-done.3 = f32[16,64,128]{2,1,0:T(8,128)S(1)} copy-done((f32[16,64,128]{2,1,0:T(8,128)S(1)}, f32[16,64,128]{2,1,0:T(8,128)}, u32[]{:S(2)}) %copy-start.3) | copy-done | bytes 524312
  29.5 2.7 %shard_map.88 = (f32[16,64,128]{2,1,0:T(8,128)S(1)}, f32[19,64,128]{2,1,0:T(8,128)S(1)}, f32[16,72,128]{2,1,0:T(8,128)S(1)}, f32[16,64,128]{2,1,0:T(8,128)S(1)}, f32[16,64,128]{2,1,0:T(8,128)S(1)}) custom-call(f32[16,64,128]{2,1,0:T(8,128)S(1)} %copy-done, f32[16,64,128]{2,1,0:T(8,128)S(1)} %copy-done.2, f32[16,64,128]{2,1,0:T(8,128)S(1)} %copy-done.3, ...), custom_call_target="tpu_custom_call" | custom-call | flops 13107200 | bytes 6389760 | tf_op jit(solution)/shard_map/pallas_call | solution.py:23
  32.2 0.8 %copy-done.4 = f32[16,64,128]{2,1,0:T(8,128)} copy-done((f32[16,64,128]{2,1,0:T(8,128)}, f32[16,64,128]{2,1,0:T(8,128)S(1)}, u32[]{:S(2)}) %copy-start.4) | copy-done | bytes 524312
  33.0 0.8 %copy-done.6 = f32[16,64,128]{2,1,0:T(8,128)} copy-done((f32[16,64,128]{2,1,0:T(8,128)}, f32[16,64,128]{2,1,0:T(8,128)S(1)}, u32[]{:S(2)}) %copy-start.6) | copy-done | bytes 524312
  33.8 0.8 %copy-done.8 = f32[16,64,128]{2,1,0:T(8,128)} copy-done((f32[16,64,128]{2,1,0:T(8,128)}, f32[16,64,128]{2,1,0:T(8,128)S(1)}, u32[]{:S(2)}) %copy-start.8) | copy-done | bytes 524312
  34.6 1.0 %copy-done.5 = f32[16,64,128]{2,1,0:T(8,128)S(1)} copy-done((f32[16,64,128]{2,1,0:T(8,128)S(1)}, f32[16,64,128]{2,1,0:T(8,128)}, u32[]{:S(2)}) %copy-start.5) | copy-done | bytes 524312
  35.6 1.3 %shard_map.89 = (f32[16,64,128]{2,1,0:T(8,128)S(1)}, f32[3,64,128]{2,1,0:T(8,128)S(1)}, f32[3,64,128]{2,1,0:T(8,128)S(1)}, f32[16,8,128]{2,1,0:T(8,128)S(1)}, f32[16,8,128]{2,1,0:T(8,128)S(1)}) custom-call(f32[16,72,128]{2,1,0:T(8,128)S(1)} %all-to-all-done.got_ref, f32[16,64,128]{2,1,0:T(8,128)S(1)} %copy-done.5, f32[16,64,128]{2,1,0:T(8,128)S(1)} %copy-done.1), custom_call_target="tpu_custom_call" | custom-call | flops 805306368 | bytes 2490368 | tf_op jit(solution)/shard_map/pallas_call | solution.py:23
  37.0 0.1 collective-permute-start.10
  37.0 4.7 %collective-permute-start.6 = (f32[3,64,128]{2,1,0:T(8,128)S(1)}, f32[3,64,128]{2,1,0:T(8,128)S(1)}, u32[]{:S(2)}, u32[]{:S(2)}) collective-permute-start(f32[3,64,128]{2,1,0:T(8,128)S(1)} %get-tuple-element.27), channel_id=1, source_target_pairs={{0,8},{1,9},{2,10},{3,11},{4,12},{5,13},{6,14},{7,15},{8,0},{9,1},... | collective-permute-start | bytes 294920 | tf_op jit(solution)/shard_map/ppermute | solution.py:170
  41.8 0.2 collective-permute-start.7
  41.9 1.5 %collective-permute-start.8 = (f32[16,8,128]{2,1,0:T(8,128)S(1)}, f32[16,8,128]{2,1,0:T(8,128)S(1)}, u32[]{:S(2)}, u32[]{:S(2)}) collective-permute-start(f32[16,8,128]{2,1,0:T(8,128)S(1)} %get-tuple-element.29), channel_id=1, source_target_pairs={{0,2},{1,3},{2,0},{3,1},{4,6},{5,7},{6,4},{7,5},{8,10},{9,11},{10,... | collective-permute-start | bytes 196616 | tf_op jit(solution)/shard_map/ppermute | solution.py:172
  43.4 0.1 collective-permute-start.9
  43.5 0.5 shard_map.90.map_ref
  43.9 2.3 %collective-permute-done.8.ye_ref = f32[16,8,128]{2,1,0:T(8,128)S(1)} collective-permute-done((f32[16,8,128]{2,1,0:T(8,128)S(1)}, f32[16,8,128]{2,1,0:T(8,128)S(1)}, u32[]{:S(2)}, u32[]{:S(2)}) %collective-permute-start.8) | collective-permute-done | bytes 65568 | tf_op jit(solution)/shard_map/ppermute | solution.py:172
  46.3 3.0 %shard_map.91 = (f32[16,64,128]{2,1,0:T(8,128)}, f32[16,64,128]{2,1,0:T(8,128)}) custom-call(f32[16,64,128]{2,1,0:T(8,128)S(1)} %get-tuple-element.26.mid_ref, f32[16,64,128]{2,1,0:T(8,128)S(1)} %copy-done.5, f32[16,64,128]{2,1,0:T(8,128)S(1)} %copy-done, f32[16,64,128]{2,1,0:T(8,128)S(1)} %copy-done.1, f32[3,64,128]{2,1,0:T(8,128)S(1)} %collective-permute-done.6.xe_ref, ...), custom_call_target="tpu_custom_call" | custom-call | flops 818413568 | bytes 10452992 | tf_op jit(solution)/shard_map/pallas_call | solution.py:23
  49.3 6.0 %all-to-all-start.1 = ((f32[16,64,128]{2,1,0:T(8,128)}), f32[16,64,128]{2,1,0:T(8,128)S(1)}, u32[]{:S(2)}, u32[]{:S(2)}) async-start(f32[16,64,128]{2,1,0:T(8,128)} %get-tuple-element.37), calls=%async_computation.1 | async-start | bytes 1048576 | tf_op jit(solution)/shard_map/all_to_all | solution.py:365
  55.3 0.3 shard_map.92.map_ref
  55.6 14.6 %all-to-all-done.1.returned_ref = f32[16,64,128]{2,1,0:T(8,128)S(1)} async-done(((f32[16,64,128]{2,1,0:T(8,128)}), f32[16,64,128]{2,1,0:T(8,128)S(1)}, u32[]{:S(2)}, u32[]{:S(2)}) %all-to-all-start.1) | async-done | bytes 524320 | tf_op jit(solution)/shard_map/all_to_all | solution.py:365
  70.2 1.4 %shard_map.93 = f32[512,128]{1,0:T(8,128)} custom-call(bf16[512,1024]{1,0:T(8,128)(2,1)S(1)} %shard_map.92.map_ref, f32[16,64,128]{2,1,0:T(8,128)S(1)} %all-to-all-done.1.returned_ref), custom_call_target="tpu_custom_call" | custom-call | flops 402653184 | bytes 2883584 | tf_op jit(solution)/shard_map/pallas_call | solution.py:23
  (28 shorter events, 0.1 us)
Async XLA Ops:
  0.6 12.6 %copy-start = (f32[16,64,128]{2,1,0:T(8,128)S(1)}, f32[16,64,128]{2,1,0:T(8,128)}, u32[]{:S(2)}) copy-start(f32[16,64,128]{2,1,0:T(8,128)} %p_ref.5) | copy-start | bytes 1572868
  0.6 12.7 %copy-start.2 = (f32[16,64,128]{2,1,0:T(8,128)S(1)}, f32[16,64,128]{2,1,0:T(8,128)}, u32[]{:S(2)}) copy-start(f32[16,64,128]{2,1,0:T(8,128)} %b_ref.3) | copy-start | bytes 1572868
  0.7 27.8 %copy-start.1 = (f32[16,64,128]{2,1,0:T(8,128)S(1)}, f32[16,64,128]{2,1,0:T(8,128)}, u32[]{:S(2)}) copy-start(f32[16,64,128]{2,1,0:T(8,128)} %kappa_ref.5) | copy-start | bytes 1572868
  0.7 1.1 %copy-start.10 = (f32[512,128]{1,0:T(8,128)S(1)}, f32[512,128]{1,0:T(8,128)}, u32[]{:S(2)}) copy-start(f32[512,128]{1,0:T(8,128)} %accel_ref.1) | copy-start | bytes 786436
  1.7 0.7 copy-start.11
  2.4 0.7 copy-start.12
  4.9 29.7 %all-to-all-start = ((f32[16,72,128]{2,1,0:T(8,128)}), f32[16,72,128]{2,1,0:T(8,128)S(1)}, u32[]{:S(2)}, u32[]{:S(2)}) async-start(f32[16,72,128]{2,1,0:T(8,128)} %bitcast.2), calls=%async_computation | async-start | bytes 1179648 | tf_op jit(solution)/shard_map/all_to_all | solution.py:301
  13.2 15.2 %collective-permute-start.4 = (f32[16,64,128]{2,1,0:T(8,128)S(1)}, f32[16,64,128]{2,1,0:T(8,128)S(1)}, u32[]{:S(2)}, u32[]{:S(2)}) collective-permute-start(f32[16,64,128]{2,1,0:T(8,128)S(1)} %copy-done), channel_id=1, source_target_pairs={{0,1},{1,0},{2,3},{3,2},{4,5},{5,4},{6,7},{7,6},{8,9},{9,8},{10,11... | collective-permute-start | bytes 1572872 | tf_op jit(solution)/shard_map/ppermute | solution.py:179
  13.3 15.1 %collective-permute-start.5 = (f32[16,64,128]{2,1,0:T(8,128)S(1)}, f32[16,64,128]{2,1,0:T(8,128)S(1)}, u32[]{:S(2)}, u32[]{:S(2)}) collective-permute-start(f32[16,64,128]{2,1,0:T(8,128)S(1)} %copy-done.2), channel_id=1, source_target_pairs={{0,1},{1,0},{2,3},{3,2},{4,5},{5,4},{6,7},{7,6},{8,9},{9,8},{10,11... | collective-permute-start | bytes 1572872 | tf_op jit(solution)/shard_map/ppermute | solution.py:179
  13.9 14.6 %collective-permute-start = (f32[5,64,128]{2,1,0:T(8,128)S(1)}, f32[5,64,128]{2,1,0:T(8,128)S(1)}, u32[]{:S(2)}, u32[]{:S(2)}) collective-permute-start(f32[5,64,128]{2,1,0:T(8,128)S(1)} %get-tuple-element.21), channel_id=1, source_target_pairs={{0,8},{1,9},{2,10},{3,11},{4,12},{5,13},{6,14},{7,15},{8,0},{9,1},... | collective-permute-start | bytes 491528 | tf_op jit(solution)/shard_map/ppermute | solution.py:170
  15.9 12.6 %collective-permute-start.1 = (f32[5,64,128]{2,1,0:T(8,128)S(1)}, f32[5,64,128]{2,1,0:T(8,128)S(1)}, u32[]{:S(2)}, u32[]{:S(2)}) collective-permute-start(f32[5,64,128]{2,1,0:T(8,128)S(1)} %get-tuple-element.22), channel_id=1, source_target_pairs={{0,1},{1,0},{2,3},{3,2},{4,5},{5,4},{6,7},{7,6},{8,16},{9,17},{10,... | collective-permute-start | bytes 491528 | tf_op jit(solution)/shard_map/ppermute | solution.py:171
  15.9 5.0 %collective-permute-start.2 = (f32[16,8,128]{2,1,0:T(8,128)S(1)}, f32[16,8,128]{2,1,0:T(8,128)S(1)}, u32[]{:S(2)}, u32[]{:S(2)}) collective-permute-start(f32[16,8,128]{2,1,0:T(8,128)S(1)} %get-tuple-element.23), channel_id=1, source_target_pairs={{0,2},{1,3},{2,0},{3,1},{4,6},{5,7},{6,4},{7,5},{8,10},{9,11},{10,... | collective-permute-start | bytes 196616 | tf_op jit(solution)/shard_map/ppermute | solution.py:172
  20.9 1.3 %collective-permute-start.3 = (f32[16,8,128]{2,1,0:T(8,128)S(1)}, f32[16,8,128]{2,1,0:T(8,128)S(1)}, u32[]{:S(2)}, u32[]{:S(2)}) collective-permute-start(f32[16,8,128]{2,1,0:T(8,128)S(1)} %get-tuple-element.24), channel_id=1, source_target_pairs={{0,1},{1,0},{2,4},{3,5},{4,2},{5,3},{6,7},{7,6},{8,9},{9,8},{10,12... | collective-permute-start | bytes 196616 | tf_op jit(solution)/shard_map/ppermute | solution.py:173
  28.5 1.0 %copy-start.3 = (f32[16,64,128]{2,1,0:T(8,128)S(1)}, f32[16,64,128]{2,1,0:T(8,128)}, u32[]{:S(2)}) copy-start(f32[16,64,128]{2,1,0:T(8,128)} %prev_ref.1) | copy-start | bytes 1572868
  32.2 0.8 %copy-start.4 = (f32[16,64,128]{2,1,0:T(8,128)}, f32[16,64,128]{2,1,0:T(8,128)S(1)}, u32[]{:S(2)}) copy-start(f32[16,64,128]{2,1,0:T(8,128)S(1)} %get-tuple-element.25.mid0_ref) | copy-start | bytes 1572868
  33.0 0.8 %copy-start.6 = (f32[16,64,128]{2,1,0:T(8,128)}, f32[16,64,128]{2,1,0:T(8,128)S(1)}, u32[]{:S(2)}) copy-start(f32[16,64,128]{2,1,0:T(8,128)S(1)} %get-tuple-element.33.bz_ref) | copy-start | bytes 1572868
  33.8 0.8 %copy-start.8 = (f32[16,64,128]{2,1,0:T(8,128)}, f32[16,64,128]{2,1,0:T(8,128)S(1)}, u32[]{:S(2)}) copy-start(f32[16,64,128]{2,1,0:T(8,128)S(1)} %get-tuple-element.34.bh_ref) | copy-start | bytes 1572868
  34.6 1.0 %copy-start.5 = (f32[16,64,128]{2,1,0:T(8,128)S(1)}, f32[16,64,128]{2,1,0:T(8,128)}, u32[]{:S(2)}) copy-start(f32[16,64,128]{2,1,0:T(8,128)} %copy-done.4) | copy-start | bytes 1572868
  37.0 9.3 %copy-start.7 = (f32[16,64,128]{2,1,0:T(8,128)S(1)}, f32[16,64,128]{2,1,0:T(8,128)}, u32[]{:S(2)}) copy-start(f32[16,64,128]{2,1,0:T(8,128)} %copy-done.6) | copy-start | bytes 1572868
  37.0 9.3 %copy-start.9 = (f32[16,64,128]{2,1,0:T(8,128)S(1)}, f32[16,64,128]{2,1,0:T(8,128)}, u32[]{:S(2)}) copy-start(f32[16,64,128]{2,1,0:T(8,128)} %copy-done.8) | copy-start | bytes 1572868
  37.0 9.3 %collective-permute-start.10 = (f32[16,64,128]{2,1,0:T(8,128)S(1)}, f32[16,64,128]{2,1,0:T(8,128)S(1)}, u32[]{:S(2)}, u32[]{:S(2)}) collective-permute-start(f32[16,64,128]{2,1,0:T(8,128)S(1)} %get-tuple-element.26.mid_ref), channel_id=1, source_target_pairs={{0,1},{1,0},{2,3},{3,2},{4,5},{5,4},{6,7},{7,6},{8,9},{9,8},{10,11... | collective-permute-start | bytes 1572872 | tf_op jit(solution)/shard_map/ppermute | solution.py:179
  37.0 9.2 %collective-permute-start.6 = (f32[3,64,128]{2,1,0:T(8,128)S(1)}, f32[3,64,128]{2,1,0:T(8,128)S(1)}, u32[]{:S(2)}, u32[]{:S(2)}) collective-permute-start(f32[3,64,128]{2,1,0:T(8,128)S(1)} %get-tuple-element.27), channel_id=1, source_target_pairs={{0,8},{1,9},{2,10},{3,11},{4,12},{5,13},{6,14},{7,15},{8,0},{9,1},... | collective-permute-start | bytes 294920 | tf_op jit(solution)/shard_map/ppermute | solution.py:170
  41.8 4.5 %collective-permute-start.7 = (f32[3,64,128]{2,1,0:T(8,128)S(1)}, f32[3,64,128]{2,1,0:T(8,128)S(1)}, u32[]{:S(2)}, u32[]{:S(2)}) collective-permute-start(f32[3,64,128]{2,1,0:T(8,128)S(1)} %get-tuple-element.28), channel_id=1, source_target_pairs={{0,1},{1,0},{2,3},{3,2},{4,5},{5,4},{6,7},{7,6},{8,16},{9,17},{10,... | collective-permute-start | bytes 294920 | tf_op jit(solution)/shard_map/ppermute | solution.py:171
  41.9 4.3 %collective-permute-start.8 = (f32[16,8,128]{2,1,0:T(8,128)S(1)}, f32[16,8,128]{2,1,0:T(8,128)S(1)}, u32[]{:S(2)}, u32[]{:S(2)}) collective-permute-start(f32[16,8,128]{2,1,0:T(8,128)S(1)} %get-tuple-element.29), channel_id=1, source_target_pairs={{0,2},{1,3},{2,0},{3,1},{4,6},{5,7},{6,4},{7,5},{8,10},{9,11},{10,... | collective-permute-start | bytes 196616 | tf_op jit(solution)/shard_map/ppermute | solution.py:172
  43.4 2.9 %collective-permute-start.9 = (f32[16,8,128]{2,1,0:T(8,128)S(1)}, f32[16,8,128]{2,1,0:T(8,128)S(1)}, u32[]{:S(2)}, u32[]{:S(2)}) collective-permute-start(f32[16,8,128]{2,1,0:T(8,128)S(1)} %get-tuple-element.30), channel_id=1, source_target_pairs={{0,1},{1,0},{2,4},{3,5},{4,2},{5,3},{6,7},{7,6},{8,9},{9,8},{10,12... | collective-permute-start | bytes 196616 | tf_op jit(solution)/shard_map/ppermute | solution.py:173
  49.3 20.9 %all-to-all-start.1 = ((f32[16,64,128]{2,1,0:T(8,128)}), f32[16,64,128]{2,1,0:T(8,128)S(1)}, u32[]{:S(2)}, u32[]{:S(2)}) async-start(f32[16,64,128]{2,1,0:T(8,128)} %get-tuple-element.37), calls=%async_computation.1 | async-start | bytes 1048576 | tf_op jit(solution)/shard_map/all_to_all | solution.py:365

commit v2 on v1

v2 whole, which is shorter than its diff:
```python
import functools
import math

import jax
import jax.numpy as jnp
from jax import lax
from jax.experimental import pallas as pl
from jax.experimental.pallas import tpu as pltpu
from jax.sharding import PartitionSpec as P

courant_sq = 0.05
source_gain = 0.5
lap_scale = courant_sq * 0.5 / (24.0 * 24.0)
halo = 3
tile = 8
f32 = jnp.float32
bf16 = jnp.bfloat16
VMEM_LIMIT = 16 << 20


def run(kernel, outs, *args, flops=0, scratch=(), in_space=pltpu.VMEM):
    size = sum(4 * math.prod(a.shape) for a in (*args, *outs))
    spec = pl.BlockSpec(memory_space=pltpu.VMEM)
    return pl.pallas_call(
        kernel,
        out_shape=outs,
        in_specs=[pl.BlockSpec(memory_space=in_space)] * len(args),
        out_specs=[spec] * len(outs),
        scratch_shapes=list(scratch),
        compiler_params=pltpu.CompilerParams(vmem_limit_bytes=VMEM_LIMIT),
        cost_estimate=pl.CostEstimate(flops=flops, bytes_accessed=size, transcendentals=0),
    )(*args)


def shaped(*shape, dtype=f32):
    return jax.ShapeDtypeStruct(shape, dtype)


def dot(a, b, contract=((1,), (0,))):
    return lax.dot_general(a, b, (contract, ((), ())), preferred_element_type=f32)


def parts_of(x):
    high = x.astype(bf16)
    rest = x - high.astype(f32)
    middle = rest.astype(bf16)
    low = (rest - middle.astype(f32)).astype(bf16)
    return jnp.concatenate([high, middle, low], axis=1)


def select_rows(one_hot, x):
    lanes = x.shape[1]
    y = dot(one_hot, parts_of(x))
    return y[:, :lanes] + y[:, lanes : 2 * lanes] + y[:, 2 * lanes :]


def one_hot_of(index, shape, dim):
    return jnp.where(lax.broadcasted_iota(jnp.int32, shape, dim) == index, 1.0, 0.0).astype(bf16)


def as_column(row):
    n = row.shape[1]
    diagonal = lax.broadcasted_iota(jnp.int32, (n, n), 0) == lax.broadcasted_iota(jnp.int32, (n, n), 1)
    return jnp.sum(jnp.where(diagonal, row, 0.0), axis=1, keepdims=True)


def pack_kernel(groups, cap, block_hbm, column_hbm, accel_hbm, out_ref, place_ref, block_ref, column_ref, accel_ref, sems):
    copies = [
        pltpu.make_async_copy(src, dst, sems.at[i])
        for i, (src, dst) in enumerate(
            ((block_hbm, block_ref), (column_hbm, column_ref), (accel_hbm, accel_ref))
        )
    ]
    for copy in copies:
        copy.start()
    rows, lanes = accel_ref.shape
    stride = cap + 1
    before = lax.broadcasted_iota(jnp.int32, (rows, rows), 0) < lax.broadcasted_iota(jnp.int32, (rows, rows), 1)
    before = jnp.where(before, 1.0, 0.0).astype(bf16)
    for copy in copies:
        copy.wait()
    block = block_ref[...]
    column = column_ref[...] + 1
    named = lax.broadcasted_iota(jnp.int32, (groups, rows), 0) == block
    matches = jnp.where(named, 1.0, 0.0).astype(bf16)
    earlier = dot(matches, before)
    slot = jnp.sum(jnp.where(named, earlier, 0.0), axis=0, keepdims=True).astype(jnp.int32)
    place_ref[...] = (block * cap + slot).astype(f32)
    out_ref[...] = select_rows(one_hot_of(block * stride + slot, (groups * stride, rows), 0), accel_ref[...])
    at_slot = lax.broadcasted_iota(jnp.int32, (lanes, rows), 0) % cap == slot
    high = jnp.where(at_slot, column // 32, 0).astype(f32).astype(bf16)
    low = jnp.where(at_slot, column % 32, 0).astype(f32).astype(bf16)
    columns = dot(matches, high, ((1,), (1,))) * 32.0 + dot(matches, low, ((1,), (1,)))
    for g in range(groups):
        out_ref[g * stride + cap : (g + 1) * stride, :] = columns[g : g + 1]


def column_rows(got_ref, cap):
    lanes = got_ref.shape[1]
    stride = cap + 1
    groups = got_ref.shape[0] // stride
    per = lanes // cap
    lane = lax.broadcasted_iota(jnp.int32, (1, lanes), 1) // cap
    rows = []
    for g in range(0, groups, per):
        row = got_ref[g * stride + cap : (g + 1) * stride, :]
        for k in range(1, per):
            row = jnp.where(lane == k, got_ref[(g + k) * stride + cap : (g + k + 1) * stride, :], row)
        rows.append(row - 1.0)
    return rows


def mid_kernel(cap, got_ref, mid0_ref, kappa_ref, mid_ref, xe_ref, xo_ref, ye_ref, yo_ref, spread_ref, rows_ref):
    lanes = got_ref.shape[1]
    groups = got_ref.shape[0] // (cap + 1)
    cx, cy, cz = mid0_ref.shape
    for at, row in enumerate(column_rows(got_ref, cap)):
        spread_ref[:, at * lanes : (at + 1) * lanes] = one_hot_of(row.astype(jnp.int32), (cx * cy, lanes), 0)
    for g in range(groups):
        rows_ref[g * cap : (g + 1) * cap, :] = got_ref[g * (cap + 1) : (g + 1) * (cap + 1) - 1, :]
    source = select_rows(spread_ref[...], rows_ref[...]).reshape(cx, cy, cz)
    mid_ref[...] = mid0_ref[...] + kappa_ref[...] * (source_gain * source)
    send_faces(((mid_ref, halo),), xe_ref, xo_ref, ye_ref, yo_ref)


def unpack_map_kernel(lanes, place_ref, map_ref):
    rows, slots = map_ref.shape
    for at in range(0, rows, lanes):
        column = as_column(place_ref[:, at : at + lanes]).astype(jnp.int32)
        map_ref[at : at + lanes, :] = one_hot_of(column, (lanes, slots), 1)


def unpack_kernel(map_ref, returned_ref, out_ref):
    slots = map_ref.shape[1]
    out_ref[...] = select_rows(map_ref[...], returned_ref[...].reshape(slots, -1))


def even_at(axis):
    return lax.axis_index(axis) % 2 == 0


def y_row(ref, j):
    cx, cy, cz = ref.shape
    return ref.reshape(cx * cy, cz)[pl.ds(j, cx, stride=cy), :]


def send_faces(fields, xe_ref, xo_ref, ye_ref, yo_ref):
    at = 0
    for ref, width in fields:
        cx, cy, _ = ref.shape
        even = even_at("gx")
        xe_ref[at : at + width] = ref[pl.ds(jnp.where(even, cx - width, 0), width)]
        xo_ref[at : at + width] = ref[pl.ds(jnp.where(even, 0, cx - width), width)]
        even = even_at("gy")
        for k in range(width):
            low, high = y_row(ref, k), y_row(ref, cy - width + k)
            ye_ref[at + k] = jnp.where(even, high, low)
            yo_ref[at + k] = jnp.where(even, low, high)
        at += width


def low_and_high(axis, from_even, from_odd):
    at = lax.axis_index(axis)
    even = at % 2 == 0
    low = jnp.where(at > 0, jnp.where(even, from_odd, from_even), 0.0)
    high = jnp.where(at < lax.axis_size(axis) - 1, jnp.where(even, from_even, from_odd), 0.0)
    return low, high


def swap_pairs(sizes, axis, first):
    num_gx, num_gy, num_blk = sizes
    pairs = []
    for x in range(num_gx):
        for y in range(num_gy):
            for b in range(num_blk):
                at, count = (x, num_gx) if axis == "gx" else (y, num_gy)
                other = at + 1 if at % 2 == first else at - 1
                if 0 <= other < count:
                    to = (other, y, b) if axis == "gx" else (x, other, b)
                else:
                    to = (x, y, num_blk - 1 - b)
                pairs.append(((x * num_gy + y) * num_blk + b, (to[0] * num_gy + to[1]) * num_blk + to[2]))
    return pairs


def exchange(xe, xo, ye, yo):
    axes = ("gx", "gy", "blk")
    sizes = tuple(lax.axis_size(a) for a in axes)
    yo = lax.ppermute(yo, axes, swap_pairs(sizes, "gy", 1))
    xo = lax.ppermute(xo, axes, swap_pairs(sizes, "gx", 1))
    xe = lax.ppermute(xe, axes, swap_pairs(sizes, "gx", 0))
    ye = lax.ppermute(ye, axes, swap_pairs(sizes, "gy", 0))
    return xe, xo, ye, yo


def swap_cores(x):
    count = lax.axis_size("blk")
    return lax.ppermute(x, "blk", [(i, count - 1 - i) for i in range(count)])


def face_kernel(p_ref, b_ref, xe_ref, xo_ref, ye_ref, yo_ref):
    send_faces(((p_ref, halo), (b_ref, 2)), xe_ref, xo_ref, ye_ref, yo_ref)


def ahead(x, beyond, lane, step):
    lanes = x.shape[-1]
    if step > 0:
        return pltpu.roll(jnp.where(lane < step, beyond, x), lanes - step, x.ndim - 1)
    return pltpu.roll(jnp.where(lane >= lanes + step, beyond, x), -step, x.ndim - 1)


def diff(a, b, c, d):
    near = (a if b is None else -b if a is None else a - b) * 27.0
    near = near if c is None else near - c
    return near if d is None else near + d


def inner(v_ref, b_ref, vo_ref, bo_ref, vpad_ref, bpad_ref, fx_ref, fy_ref, finish):
    cx, cy, cz = v_ref.shape
    lane = lax.broadcasted_iota(jnp.int32, (cy, cz), 1)
    last = lax.broadcasted_iota(jnp.int32, (cy, cz), 0) == cy - 1
    start = jnp.where(lax.axis_index("blk") == 0, 0, cz - halo)
    near = (lane >= start) & (lane < start + halo)
    for ref in (vpad_ref, bpad_ref, fy_ref):
        ref[:, :tile] = jnp.zeros((ref.shape[0], tile, cz), f32)
        ref[:, tile + cy :] = jnp.zeros((ref.shape[0], tile, cz), f32)
    vpad_ref[:, tile : tile + cy] = v_ref[...]
    bpad_ref[:, tile : tile + cy] = b_ref[...]

    def plane(ref, i, count):
        return ref[i] if 0 <= i < count else None

    for i in range(cx - 1):
        v = [plane(v_ref, i + k, cx) for k in (-1, 0, 1, 2)]
        fx_ref[i] = diff(v[2], v[1], v[3], v[0]) * (b_ref[i] + b_ref[i + 1])
    for i in range(cx):
        f = [plane(fx_ref, i + k, cx - 1) for k in (-2, -1, 0, 1)]
        total = diff(f[2], f[1], f[3], f[0])
        v = [vpad_ref[i, tile + k : tile + k + cy, :] for k in (-1, 0, 1, 2)]
        b = jnp.where(last, 0.0, b_ref[i] + bpad_ref[i, tile + 1 : tile + 1 + cy, :])
        fy = diff(v[2], v[1], v[3], v[0]) * b
        fy_ref[i % 2, tile : tile + cy, :] = fy
        f = [fy_ref[i % 2, tile + k : tile + k + cy, :] for k in (-2, -1, 1)]
        total += diff(fy, f[1], f[2], f[0])
        u, h = v_ref[i], jnp.where(near, vo_ref[i], 0.0)
        bu, bh = b_ref[i], jnp.where(near, bo_ref[i], 0.0)
        fu = diff(ahead(u, h, lane, 1), u, ahead(u, h, lane, 2), ahead(u, h, lane, -1)) * (bu + ahead(bu, bh, lane, 1))
        fh = diff(ahead(h, u, lane, 1), h, ahead(h, u, lane, 2), ahead(h, u, lane, -1)) * (bh + ahead(bh, bu, lane, 1))
        total += diff(fu, ahead(fu, fh, lane, -1), ahead(fu, fh, lane, 1), ahead(fu, fh, lane, -2))
        finish(i, u, total)


def edge(v0, v1, w1, w2, w3, b0, b1, b3):
    f3 = diff(w1, w2, v0, w3) * b3
    f1 = diff(v0, w1, v1, w2) * b1
    d0 = w1 * b0
    return 27.0 * (d0 - f1) + f3, f1 - 27.0 * d0, d0


def add_edges(out_ref, v_ref, b_ref, kappa_ref, low_x, high_x, low_y, high_y, bx, by):
    cx, cy, cz = v_ref.shape
    flat_out = out_ref.reshape(cx * cy, cz)
    sides = ((low_x, low_y, 0, 1, 0), (high_x, high_y, -1, -1, 2))
    for x, y, first, step, at in sides:
        w = (x[0], x[1], x[2])[:: -step]
        i = first % cx
        terms = edge(v_ref[i], v_ref[i + step], *w, b_ref[i] + b_ref[i + step], bx[at], bx[at + 1])
        for k, term in enumerate(terms):
            out_ref[i + k * step] += kappa_ref[i + k * step] * (lap_scale * term)
    for x, y, first, step, at in sides:
        w = (y[0], y[1], y[2])[:: -step]
        j = first % cy
        v0, v1, b = y_row(v_ref, j), y_row(v_ref, j + step), y_row(b_ref, j) + y_row(b_ref, j + step)
        terms = edge(v0, v1, *w, b, by[at], by[at + 1])
        for k, term in enumerate(terms):
            to = pl.ds(j + k * step, cx, stride=cy)
            flat_out[to, :] = flat_out[to, :] + y_row(kappa_ref, j + k * step) * (lap_scale * term)


def first_inner_kernel(p_ref, b_ref, prev_ref, kappa_ref, po_ref, bo_ref, out_ref, *scratch):
    def finish(i, u, total):
        out_ref[i] = 2.0 * u - prev_ref[i] + kappa_ref[i] * (lap_scale * total)

    inner(p_ref, b_ref, po_ref, bo_ref, *scratch, finish)


def first_edge_kernel(part_ref, p_ref, b_ref, kappa_ref, xe_ref, xo_ref, ye_ref, yo_ref, mid0_ref, bx_ref, by_ref):
    cx, cy, _ = p_ref.shape
    low_x, high_x = low_and_high("gx", xe_ref[...], xo_ref[...])
    low_y, high_y = low_and_high("gy", ye_ref[...], yo_ref[...])
    bx_ref[0] = low_x[4] + b_ref[0]
    bx_ref[1] = low_x[3] + low_x[4]
    bx_ref[2] = high_x[3] + b_ref[cx - 1]
    bx_ref[3] = high_x[3] + high_x[4]
    by_ref[0] = low_y[4] + y_row(b_ref, 0)
    by_ref[1] = low_y[3] + low_y[4]
    by_ref[2] = high_y[3] + y_row(b_ref, cy - 1)
    by_ref[3] = high_y[3] + high_y[4]
    mid0_ref[...] = part_ref[...]
    add_edges(mid0_ref, p_ref, b_ref, kappa_ref, low_x, high_x, low_y, high_y, bx_ref, by_ref)


def second_inner_kernel(
    cap, mid_ref, mid0_ref, p_ref, b_ref, kappa_ref, mo_ref, bo_ref, got_ref, out_ref, map_ref, *scratch
):
    cx, cy, _ = p_ref.shape
    lanes = got_ref.shape[1]

    def finish(i, u, total):
        out_ref[i] = 3.0 * u - mid0_ref[i] - p_ref[i] + kappa_ref[i] * (lap_scale * total)

    inner(mid_ref, b_ref, mo_ref, bo_ref, *scratch, finish)
    for at, row in enumerate(column_rows(got_ref, cap)):
        column = as_column(row).astype(jnp.int32)
        map_ref[at * lanes : (at + 1) * lanes, :] = one_hot_of(column, (lanes, cx * cy), 1)


def second_edge_kernel(
    part_ref, mid_ref, b_ref, kappa_ref, bx_ref, by_ref, map_ref, xe_ref, xo_ref, ye_ref, yo_ref, next_ref, picked_ref
):
    cx, cy, cz = mid_ref.shape
    low_x, high_x = low_and_high("gx", xe_ref[...], xo_ref[...])
    low_y, high_y = low_and_high("gy", ye_ref[...], yo_ref[...])
    next_ref[...] = part_ref[...]
    add_edges(next_ref, mid_ref, b_ref, kappa_ref, low_x, high_x, low_y, high_y, bx_ref, by_ref)
    picked_ref[...] = select_rows(map_ref[...], next_ref[...].reshape(cx * cy, cz)).reshape(picked_ref.shape)


def local(pressure, pressure_prev, buoyancy, kappa, hull_accel, row_block, row_column):
    groups = lax.axis_size("gx") * lax.axis_size("gy")
    rows, lanes = hull_accel.shape
    cap = 2 * rows // groups
    cx, cy, cz = pressure.shape
    slots, stride = groups * cap, cap + 1
    cells = shaped(cx, cy, cz)

    in_hbm = [pltpu.with_memory_space_constraint(a, pltpu.HBM) for a in (
        row_block.reshape(1, rows), row_column.reshape(1, rows), hull_accel)]
    outgoing, place = run(
        functools.partial(pack_kernel, groups, cap),
        [pltpu.VMEM((groups * stride, lanes), f32), shaped(1, rows)],
        *in_hbm,
        in_space=pl.ANY,
        flops=6 * groups * stride * rows * lanes,
        scratch=[pltpu.VMEM(a.shape, a.dtype) for a in in_hbm] + [pltpu.SemaphoreType.DMA((3,))],
    )
    got = lax.all_to_all(
        outgoing.reshape(groups, stride, 1, lanes), ("gx", "gy"), split_axis=0, concat_axis=0, tiled=True
    ).reshape(groups * stride, lanes)

    faces = run(
        face_kernel,
        [shaped(halo + 2, cy, cz)] * 2 + [shaped(halo + 2, cx, cz)] * 2,
        pressure,
        buoyancy,
    )
    beyond = exchange(*faces)
    other_b = swap_cores(buoyancy)
    scratch = [pltpu.VMEM((cx, cy + 2 * tile, cz), f32)] * 2 + [
        pltpu.VMEM((cx, cy, cz), f32),
        pltpu.VMEM((2, cy + 2 * tile, cz), f32),
    ]
    (part,) = run(
        first_inner_kernel,
        [cells],
        pressure,
        buoyancy,
        pressure_prev,
        kappa,
        swap_cores(pressure),
        other_b,
        flops=100 * cx * cy * cz,
        scratch=scratch,
    )
    mid0, bx, by = run(
        first_edge_kernel, [cells, shaped(4, cy, cz), shaped(4, cx, cz)], part, pressure, buoyancy, kappa, *beyond
    )

    mid, *mid_faces = run(
        functools.partial(mid_kernel, cap),
        [cells] + [shaped(halo, cy, cz)] * 2 + [shaped(halo, cx, cz)] * 2,
        got,
        mid0,
        kappa,
        flops=6 * cx * cy * slots * lanes,
        scratch=[pltpu.VMEM((cx * cy, slots), bf16), pltpu.VMEM((slots, lanes), f32)],
    )
    other_mid = swap_cores(mid)
    mid_beyond = exchange(*mid_faces)
    part, gather_map = run(
        functools.partial(second_inner_kernel, cap),
        [cells, shaped(slots, cx * cy, dtype=bf16)],
        mid,
        mid0,
        pressure,
        buoyancy,
        kappa,
        other_mid,
        other_b,
        got,
        flops=100 * cx * cy * cz,
        scratch=scratch,
    )
    pressure_next, picked = run(
        second_edge_kernel,
        [pltpu.VMEM((cx, cy, cz), f32), pltpu.VMEM((groups, cap, lanes), f32)],
        part,
        mid,
        buoyancy,
        kappa,
        bx,
        by,
        gather_map,
        *mid_beyond,
        flops=6 * slots * cx * cy * lanes,
    )
    returned = lax.all_to_all(picked, ("gx", "gy"), split_axis=0, concat_axis=0, tiled=True)
    (unpack_map,) = run(
        functools.partial(unpack_map_kernel, lanes), [shaped(rows, slots, dtype=bf16)], place, flops=rows * slots
    )
    (hull_pressure,) = run(unpack_kernel, [shaped(rows, lanes)], unpack_map, returned, flops=6 * rows * slots * lanes)
    return pressure_next, hull_pressure


def solution(mesh):
    cells = P("gx", "gy", "blk")
    rows = P(("gx", "gy", "blk"), None)
    return jax.shard_map(
        local,
        mesh=mesh,
        in_specs=(cells, cells, cells, cells, rows, rows, rows),
        out_specs=(cells, rows),
        check_vma=False,
    )
```

time: 72.1 us -> 61.4 us (0.85)
  waiting for transfers between devices: 28 us -> 21.6 us
  local copies, waits for them, and re-layouts: 6.9 us -> 0.81 us
  Pallas kernels: 11 us -> 14.3 us
  starting transfers between devices: 24.8 us -> 23.6 us
    ppermute x8, waiting for transfers between devices: 13.5 us -> 7.26 us  [the longest x2 7.24 us: exchange(): xe = lax.ppermute(xe, axes, swap_pairs(sizes, 'gx', 0))]
    unnamed x26 -> x9, local copies, waits for them, and re-layouts: 6.9 us -> 0.81 us
    pallas_call x8 -> x9, Pallas kernels: 11 us -> 14.3 us  [run(): pl.pallas_call(kernel, out_shape=outs, in_specs=[pl.BlockSpec(memory_spac...]
    all_to_all x1, starting transfers between devices: 6.03 us -> 5.22 us  [local(): lax.all_to_all(picked, ('gx', 'gy'), split_axis=0, concat_axis=0, tiled=T...]
  transfers between devices with their start and end apart: 13 -> 13, of which waited for: 5 -> 3; matrix products, arithmetic and copies ran while one was open for 0% -> 1% of each run, Pallas kernels for 5% -> 11%
where the time goes in v2:
time: 61.4 us; the launch traced here: 61.1 us
  starting transfers between devices  23.6 us (38%)
  waiting for transfers between devices  21.6 us (35%)
  Pallas kernels  14.3 us (23%)
  between operations  0.82 us (1%)
  local copies, waits for them, and re-layouts  0.81 us (1%)
    pallas_call x9, Pallas kernels, run(): pl.pallas_call(kernel, out_shape=outs, in_specs=[pl.BlockSpec(memory_spac...  14.3 us
    all_to_all x1, waiting for transfers between devices, local(): lax.all_to_all(picked, ('gx', 'gy'), split_axis=0, concat_axis=0, tiled=T...  13.9 us
    all_to_all x1, starting transfers between devices, local(): lax.all_to_all(outgoing.reshape(groups, stride, 1, lanes), ('gx', 'gy'),...  8.33 us
    ppermute x2, waiting for transfers between devices, exchange(): xe = lax.ppermute(xe, axes, swap_pairs(sizes, 'gx', 0))  7.24 us
    ppermute x2, starting transfers between devices, exchange(): xe = lax.ppermute(xe, axes, swap_pairs(sizes, 'gx', 0))  5.99 us
    all_to_all x1, starting transfers between devices, local(): lax.all_to_all(picked, ('gx', 'gy'), split_axis=0, concat_axis=0, tiled=T...  5.22 us
    ppermute x2, starting transfers between devices, exchange(): ye = lax.ppermute(ye, axes, swap_pairs(sizes, 'gy', 0))  2.93 us
  transfers between devices with their start and end apart: 13, of which 3 were waited for; matrix products, arithmetic and copies ran while one was open for 1% of the time, Pallas kernels for 11%

profile of v2, /device:TPU:0, one launch (start us, length us, event | category | flops | bytes accessed | tf_op | source)
XLA Modules:
  0.0 61.1 jit_solution(6643714618571488824)
XLA Ops:
  0.7 2.9 %shard_map.86 = (f32[1040,128]{1,0:T(8,128)}, f32[1,512]{1,0:T(1,128)S(1)}) custom-call(s32[1,512]{1,0:T(1,128)} %bitcast.6, s32[1,512]{1,0:T(1,128)} %bitcast.7, f32[512,128]{1,0:T(8,128)} %accel_hbm.1), custom_call_target="tpu_custom_call" | custom-call | flops 408944640 | bytes 800768 | tf_op jit(solution)/shard_map/pallas_call | solution.py:24
  3.6 8.3 %all-to-all-start = ((f32[16,65,1,128]{3,2,1,0:T(1,128)}), f32[16,65,1,128]{3,2,1,0:T(1,128)S(1)}, u32[]{:S(2)}, u32[]{:S(2)}) async-start(f32[16,65,1,128]{3,2,1,0:T(1,128)} %bitcast.2), calls=%async_computation | async-start | bytes 1064960 | tf_op jit(solution)/shard_map/all_to_all | solution.py:347
  11.9 0.1 collective-permute-start
  12.0 0.5 collective-permute-start.1
  12.5 0.1 shard_map.88
  12.6 2.0 %collective-permute-start.2 = (f32[5,64,128]{2,1,0:T(8,128)S(1)}, f32[5,64,128]{2,1,0:T(8,128)S(1)}, u32[]{:S(2)}, u32[]{:S(2)}) collective-permute-start(f32[5,64,128]{2,1,0:T(8,128)S(1)} %get-tuple-element.21), channel_id=1, source_target_pairs={{0,8},{1,9},{2,10},{3,11},{4,12},{5,13},{6,14},{7,15},{8,0},{9,1},... | collective-permute-start | bytes 491528 | tf_op jit(solution)/shard_map/ppermute | solution.py:191
  14.5 0.0 collective-permute-start.3
  14.6 1.5 %collective-permute-start.4 = (f32[5,16,128]{2,1,0:T(8,128)S(1)}, f32[5,16,128]{2,1,0:T(8,128)S(1)}, u32[]{:S(2)}, u32[]{:S(2)}) collective-permute-start(f32[5,16,128]{2,1,0:T(8,128)S(1)} %get-tuple-element.23), channel_id=1, source_target_pairs={{0,2},{1,3},{2,0},{3,1},{4,6},{5,7},{6,4},{7,5},{8,10},{9,11},{10,... | collective-permute-start | bytes 122888 | tf_op jit(solution)/shard_map/ppermute | solution.py:192
  16.0 0.0 collective-permute-done.po_ref
  16.0 0.2 collective-permute-start.5
  16.2 0.0 collective-permute-done.1.bo_ref
  16.3 2.7 %shard_map.87.part_ref = f32[16,64,128]{2,1,0:T(8,128)S(1)} custom-call(f32[16,64,128]{2,1,0:T(8,128)S(1)} %copy-done.1, f32[16,64,128]{2,1,0:T(8,128)S(1)} %copy-done, f32[16,64,128]{2,1,0:T(8,128)S(1)} %copy-done.3, f32[16,64,128]{2,1,0:T(8,128)S(1)} %copy-done.2, f32[16,64,128]{2,1,0:T(8,128)S(1)} %collective-permute-done.po_ref, ...), custom_call_target="tpu_custom_call" | custom-call | flops 13107200 | bytes 3670016 | tf_op jit(solution)/shard_map/pallas_call | solution.py:24
  19.0 0.0 collective-permute-done.4.ye_ref
  19.0 7.2 %collective-permute-done.2.xe_ref = f32[5,64,128]{2,1,0:T(8,128)S(1)} collective-permute-done((f32[5,64,128]{2,1,0:T(8,128)S(1)}, f32[5,64,128]{2,1,0:T(8,128)S(1)}, u32[]{:S(2)}, u32[]{:S(2)}) %collective-permute-start.2) | collective-permute-done | bytes 163872 | tf_op jit(solution)/shard_map/ppermute | solution.py:191
  26.2 0.3 shard_map.89
  26.5 0.4 all-to-all-done
  26.9 1.3 %shard_map.90 = (f32[16,64,128]{2,1,0:T(8,128)S(1)}, f32[3,64,128]{2,1,0:T(8,128)S(1)}, f32[3,64,128]{2,1,0:T(8,128)S(1)}, f32[3,16,128]{2,1,0:T(8,128)S(1)}, f32[3,16,128]{2,1,0:T(8,128)S(1)}) custom-call(f32[1040,128]{1,0:T(8,128)S(1)} %bitcast.4, f32[16,64,128]{2,1,0:T(8,128)S(1)} %get-tuple-element.25.mid0_ref, f32[16,64,128]{2,1,0:T(8,128)S(1)} %copy-done.2), custom_call_target="tpu_custom_call" | custom-call | flops 805306368 | bytes 2351104 | tf_op jit(solution)/shard_map/pallas_call | solution.py:24
  28.3 0.1 collective-permute-start.6
  28.3 4.0 %collective-permute-start.7 = (f32[3,64,128]{2,1,0:T(8,128)S(1)}, f32[3,64,128]{2,1,0:T(8,128)S(1)}, u32[]{:S(2)}, u32[]{:S(2)}) collective-permute-start(f32[3,64,128]{2,1,0:T(8,128)S(1)} %get-tuple-element.31), channel_id=1, source_target_pairs={{0,8},{1,9},{2,10},{3,11},{4,12},{5,13},{6,14},{7,15},{8,0},{9,1},... | collective-permute-start | bytes 294920 | tf_op jit(solution)/shard_map/ppermute | solution.py:191
  32.3 0.2 collective-permute-start.8
  32.5 1.5 %collective-permute-start.9 = (f32[3,16,128]{2,1,0:T(8,128)S(1)}, f32[3,16,128]{2,1,0:T(8,128)S(1)}, u32[]{:S(2)}, u32[]{:S(2)}) collective-permute-start(f32[3,16,128]{2,1,0:T(8,128)S(1)} %get-tuple-element.33), channel_id=1, source_target_pairs={{0,2},{1,3},{2,0},{3,1},{4,6},{5,7},{6,4},{7,5},{8,10},{9,11},{10,... | collective-permute-start | bytes 73736 | tf_op jit(solution)/shard_map/ppermute | solution.py:192
  34.0 0.1 collective-permute-start.10
  34.0 0.0 collective-permute-done.6.mo_ref
  34.0 3.1 %shard_map.91 = (f32[16,64,128]{2,1,0:T(8,128)S(1)}, bf16[1024,1024]{1,0:T(8,128)(2,1)S(1)}) custom-call(f32[16,64,128]{2,1,0:T(8,128)S(1)} %get-tuple-element.26.mid_ref, f32[16,64,128]{2,1,0:T(8,128)S(1)} %get-tuple-element.25.mid0_ref, f32[16,64,128]{2,1,0:T(8,128)S(1)} %copy-done.1, f32[16,64,128]{2,1,0:T(8,128)S(1)} %copy-done, ...), custom_call_target="tpu_custom_call" | custom-call | flops 13107200 | bytes 8921088 | tf_op jit(solution)/shard_map/pallas_call | solution.py:24
  37.2 0.0 collective-permute-done.9.ye_ref
  37.2 0.0 collective-permute-done.8.xo_ref
  37.2 2.2 %shard_map.92 = (f32[16,64,128]{2,1,0:T(8,128)S(1)}, f32[16,64,128]{2,1,0:T(8,128)}) custom-call(f32[16,64,128]{2,1,0:T(8,128)S(1)} %get-tuple-element.27.part_ref, f32[16,64,128]{2,1,0:T(8,128)S(1)} %get-tuple-element.26.mid_ref, f32[16,64,128]{2,1,0:T(8,128)S(1)} %copy-done, f32[16,64,128]{2,1,0:T(8,128)S(1)} %copy-done.2, ...), custom_call_target="tpu_custom_call" | custom-call | flops 805306368 | bytes 7749632 | tf_op jit(solution)/shard_map/pallas_call | solution.py:24
  39.4 5.2 %all-to-all-start.1 = ((f32[16,64,128]{2,1,0:T(8,128)}), f32[16,64,128]{2,1,0:T(8,128)S(1)}, u32[]{:S(2)}, u32[]{:S(2)}) async-start(f32[16,64,128]{2,1,0:T(8,128)} %get-tuple-element.37), calls=%async_computation.1 | async-start | bytes 1048576 | tf_op jit(solution)/shard_map/all_to_all | solution.py:417
  44.7 0.3 shard_map.93.map_ref
  44.9 0.8 %copy.10 = f32[16,64,128]{2,1,0:T(8,128)} copy(f32[16,64,128]{2,1,0:T(8,128)S(1)} %get-tuple-element.38) | data formatting | bytes 1048576
  45.7 13.9 %all-to-all-done.1.returned_ref = f32[16,64,128]{2,1,0:T(8,128)S(1)} async-done(((f32[16,64,128]{2,1,0:T(8,128)}), f32[16,64,128]{2,1,0:T(8,128)S(1)}, u32[]{:S(2)}, u32[]{:S(2)}) %all-to-all-start.1) | async-done | bytes 524320 | tf_op jit(solution)/shard_map/all_to_all | solution.py:417
  59.7 1.4 %shard_map.94 = f32[512,128]{1,0:T(8,128)} custom-call(bf16[512,1024]{1,0:T(8,128)(2,1)S(1)} %shard_map.93.map_ref, f32[16,64,128]{2,1,0:T(8,128)S(1)} %all-to-all-done.1.returned_ref), custom_call_target="tpu_custom_call" | custom-call | flops 402653184 | bytes 2883584 | tf_op jit(solution)/shard_map/pallas_call | solution.py:24
  (12 shorter events, 0.0 us)
Async XLA Ops:
  0.6 11.3 %copy-start.1 = (f32[16,64,128]{2,1,0:T(8,128)S(1)}, f32[16,64,128]{2,1,0:T(8,128)}, u32[]{:S(2)}) copy-start(f32[16,64,128]{2,1,0:T(8,128)} %p_ref.7) | copy-start | bytes 1572868
  0.6 11.3 %copy-start = (f32[16,64,128]{2,1,0:T(8,128)S(1)}, f32[16,64,128]{2,1,0:T(8,128)}, u32[]{:S(2)}) copy-start(f32[16,64,128]{2,1,0:T(8,128)} %b_ref.9) | copy-start | bytes 1572868
  0.7 15.6 %copy-start.2 = (f32[16,64,128]{2,1,0:T(8,128)S(1)}, f32[16,64,128]{2,1,0:T(8,128)}, u32[]{:S(2)}) copy-start(f32[16,64,128]{2,1,0:T(8,128)} %kappa_ref.9) | copy-start | bytes 1572868
  0.7 15.6 %copy-start.3 = (f32[16,64,128]{2,1,0:T(8,128)S(1)}, f32[16,64,128]{2,1,0:T(8,128)}, u32[]{:S(2)}) copy-start(f32[16,64,128]{2,1,0:T(8,128)} %prev_ref.1) | copy-start | bytes 1572868
  3.6 23.3 %all-to-all-start = ((f32[16,65,1,128]{3,2,1,0:T(1,128)}), f32[16,65,1,128]{3,2,1,0:T(1,128)S(1)}, u32[]{:S(2)}, u32[]{:S(2)}) async-start(f32[16,65,1,128]{3,2,1,0:T(1,128)} %bitcast.2), calls=%async_computation | async-start | bytes 1064960 | tf_op jit(solution)/shard_map/all_to_all | solution.py:347
  11.9 4.1 %collective-permute-start = (f32[16,64,128]{2,1,0:T(8,128)S(1)}, f32[16,64,128]{2,1,0:T(8,128)S(1)}, u32[]{:S(2)}, u32[]{:S(2)}) collective-permute-start(f32[16,64,128]{2,1,0:T(8,128)S(1)} %copy-done.1), channel_id=1, source_target_pairs={{0,1},{1,0},{2,3},{3,2},{4,5},{5,4},{6,7},{7,6},{8,9},{9,8},{10,11... | collective-permute-start | bytes 1572872 | tf_op jit(solution)/shard_map/ppermute | solution.py:198
  12.0 4.3 %collective-permute-start.1 = (f32[16,64,128]{2,1,0:T(8,128)S(1)}, f32[16,64,128]{2,1,0:T(8,128)S(1)}, u32[]{:S(2)}, u32[]{:S(2)}) collective-permute-start(f32[16,64,128]{2,1,0:T(8,128)S(1)} %copy-done), channel_id=1, source_target_pairs={{0,1},{1,0},{2,3},{3,2},{4,5},{5,4},{6,7},{7,6},{8,9},{9,8},{10,11... | collective-permute-start | bytes 1572872 | tf_op jit(solution)/shard_map/ppermute | solution.py:198
  12.6 13.7 %collective-permute-start.2 = (f32[5,64,128]{2,1,0:T(8,128)S(1)}, f32[5,64,128]{2,1,0:T(8,128)S(1)}, u32[]{:S(2)}, u32[]{:S(2)}) collective-permute-start(f32[5,64,128]{2,1,0:T(8,128)S(1)} %get-tuple-element.21), channel_id=1, source_target_pairs={{0,8},{1,9},{2,10},{3,11},{4,12},{5,13},{6,14},{7,15},{8,0},{9,1},... | collective-permute-start | bytes 491528 | tf_op jit(solution)/shard_map/ppermute | solution.py:191
  14.5 11.7 %collective-permute-start.3 = (f32[5,64,128]{2,1,0:T(8,128)S(1)}, f32[5,64,128]{2,1,0:T(8,128)S(1)}, u32[]{:S(2)}, u32[]{:S(2)}) collective-permute-start(f32[5,64,128]{2,1,0:T(8,128)S(1)} %get-tuple-element.22), channel_id=1, source_target_pairs={{0,1},{1,0},{2,3},{3,2},{4,5},{5,4},{6,7},{7,6},{8,16},{9,17},{10,... | collective-permute-start | bytes 491528 | tf_op jit(solution)/shard_map/ppermute | solution.py:190
  14.6 4.4 %collective-permute-start.4 = (f32[5,16,128]{2,1,0:T(8,128)S(1)}, f32[5,16,128]{2,1,0:T(8,128)S(1)}, u32[]{:S(2)}, u32[]{:S(2)}) collective-permute-start(f32[5,16,128]{2,1,0:T(8,128)S(1)} %get-tuple-element.23), channel_id=1, source_target_pairs={{0,2},{1,3},{2,0},{3,1},{4,6},{5,7},{6,4},{7,5},{8,10},{9,11},{10,... | collective-permute-start | bytes 122888 | tf_op jit(solution)/shard_map/ppermute | solution.py:192
  16.0 3.0 %collective-permute-start.5 = (f32[5,16,128]{2,1,0:T(8,128)S(1)}, f32[5,16,128]{2,1,0:T(8,128)S(1)}, u32[]{:S(2)}, u32[]{:S(2)}) collective-permute-start(f32[5,16,128]{2,1,0:T(8,128)S(1)} %get-tuple-element.24), channel_id=1, source_target_pairs={{0,1},{1,0},{2,4},{3,5},{4,2},{5,3},{6,7},{7,6},{8,9},{9,8},{10,12... | collective-permute-start | bytes 122888 | tf_op jit(solution)/shard_map/ppermute | solution.py:189
  28.3 5.8 %collective-permute-start.6 = (f32[16,64,128]{2,1,0:T(8,128)S(1)}, f32[16,64,128]{2,1,0:T(8,128)S(1)}, u32[]{:S(2)}, u32[]{:S(2)}) collective-permute-start(f32[16,64,128]{2,1,0:T(8,128)S(1)} %get-tuple-element.26.mid_ref), channel_id=1, source_target_pairs={{0,1},{1,0},{2,3},{3,2},{4,5},{5,4},{6,7},{7,6},{8,9},{9,8},{10,11... | collective-permute-start | bytes 1572872 | tf_op jit(solution)/shard_map/ppermute | solution.py:198
  28.3 8.9 %collective-permute-start.7 = (f32[3,64,128]{2,1,0:T(8,128)S(1)}, f32[3,64,128]{2,1,0:T(8,128)S(1)}, u32[]{:S(2)}, u32[]{:S(2)}) collective-permute-start(f32[3,64,128]{2,1,0:T(8,128)S(1)} %get-tuple-element.31), channel_id=1, source_target_pairs={{0,8},{1,9},{2,10},{3,11},{4,12},{5,13},{6,14},{7,15},{8,0},{9,1},... | collective-permute-start | bytes 294920 | tf_op jit(solution)/shard_map/ppermute | solution.py:191
  32.3 4.9 %collective-permute-start.8 = (f32[3,64,128]{2,1,0:T(8,128)S(1)}, f32[3,64,128]{2,1,0:T(8,128)S(1)}, u32[]{:S(2)}, u32[]{:S(2)}) collective-permute-start(f32[3,64,128]{2,1,0:T(8,128)S(1)} %get-tuple-element.32), channel_id=1, source_target_pairs={{0,1},{1,0},{2,3},{3,2},{4,5},{5,4},{6,7},{7,6},{8,16},{9,17},{10,... | collective-permute-start | bytes 294920 | tf_op jit(solution)/shard_map/ppermute | solution.py:190
  32.5 4.7 %collective-permute-start.9 = (f32[3,16,128]{2,1,0:T(8,128)S(1)}, f32[3,16,128]{2,1,0:T(8,128)S(1)}, u32[]{:S(2)}, u32[]{:S(2)}) collective-permute-start(f32[3,16,128]{2,1,0:T(8,128)S(1)} %get-tuple-element.33), channel_id=1, source_target_pairs={{0,2},{1,3},{2,0},{3,1},{4,6},{5,7},{6,4},{7,5},{8,10},{9,11},{10,... | collective-permute-start | bytes 73736 | tf_op jit(solution)/shard_map/ppermute | solution.py:192
  34.0 3.2 %collective-permute-start.10 = (f32[3,16,128]{2,1,0:T(8,128)S(1)}, f32[3,16,128]{2,1,0:T(8,128)S(1)}, u32[]{:S(2)}, u32[]{:S(2)}) collective-permute-start(f32[3,16,128]{2,1,0:T(8,128)S(1)} %get-tuple-element.34), channel_id=1, source_target_pairs={{0,1},{1,0},{2,4},{3,5},{4,2},{5,3},{6,7},{7,6},{8,9},{9,8},{10,12... | collective-permute-start | bytes 73736 | tf_op jit(solution)/shard_map/ppermute | solution.py:189
  39.4 20.2 %all-to-all-start.1 = ((f32[16,64,128]{2,1,0:T(8,128)}), f32[16,64,128]{2,1,0:T(8,128)S(1)}, u32[]{:S(2)}, u32[]{:S(2)}) async-start(f32[16,64,128]{2,1,0:T(8,128)} %get-tuple-element.37), calls=%async_computation.1 | async-start | bytes 1048576 | tf_op jit(solution)/shard_map/all_to_all | solution.py:417

commit v3 on v2

--- a/solution.py
+++ b/solution.py
@@ -16,6 +16,7 @@
 f32 = jnp.float32
 bf16 = jnp.bfloat16
 VMEM_LIMIT = 16 << 20
+early = 10**11
 
 
 def run(kernel, outs, *args, flops=0, scratch=(), in_space=pltpu.VMEM):
@@ -42,16 +43,13 @@
 
 def parts_of(x):
     high = x.astype(bf16)
-    rest = x - high.astype(f32)
-    middle = rest.astype(bf16)
-    low = (rest - middle.astype(f32)).astype(bf16)
-    return jnp.concatenate([high, middle, low], axis=1)
+    return jnp.concatenate([high, (x - high.astype(f32)).astype(bf16)], axis=1)
 
 
 def select_rows(one_hot, x):
     lanes = x.shape[1]
     y = dot(one_hot, parts_of(x))
-    return y[:, :lanes] + y[:, lanes : 2 * lanes] + y[:, 2 * lanes :]
+    return y[:, :lanes] + y[:, lanes:]
 
 
 def one_hot_of(index, shape, dim):
@@ -64,35 +62,47 @@
     return jnp.sum(jnp.where(diagonal, row, 0.0), axis=1, keepdims=True)
 
 
-def pack_kernel(groups, cap, block_hbm, column_hbm, accel_hbm, out_ref, place_ref, block_ref, column_ref, accel_ref, sems):
-    copies = [
-        pltpu.make_async_copy(src, dst, sems.at[i])
-        for i, (src, dst) in enumerate(
-            ((block_hbm, block_ref), (column_hbm, column_ref), (accel_hbm, accel_ref))
-        )
-    ]
+def slot_kernel(
+    groups, cap, block_hbm, column_hbm, accel_hbm, p_hbm, b_hbm,
+    place_ref, columns_ref, accel_ref, xe_ref, xo_ref, block_ref, column_ref, sems,
+):
+    cx, even = p_hbm.shape[0], even_at("gx")
+    moves = [(block_hbm, block_ref), (column_hbm, column_ref), (accel_hbm, accel_ref)]
+    for field, width, at in ((p_hbm, halo, 0), (b_hbm, 2, halo)):
+        moves.append((field.at[pl.ds(jnp.where(even, cx - width, 0), width)], xe_ref.at[pl.ds(at, width)]))
+        moves.append((field.at[pl.ds(jnp.where(even, 0, cx - width), width)], xo_ref.at[pl.ds(at, width)]))
+    copies = [pltpu.make_async_copy(src, dst, sems.at[i]) for i, (src, dst) in enumerate(moves)]
     for copy in copies:
         copy.start()
     rows, lanes = accel_ref.shape
-    stride = cap + 1
     before = lax.broadcasted_iota(jnp.int32, (rows, rows), 0) < lax.broadcasted_iota(jnp.int32, (rows, rows), 1)
     before = jnp.where(before, 1.0, 0.0).astype(bf16)
-    for copy in copies:
-        copy.wait()
+    copies[0].wait()
+    copies[1].wait()
     block = block_ref[...]
     column = column_ref[...] + 1
     named = lax.broadcasted_iota(jnp.int32, (groups, rows), 0) == block
     matches = jnp.where(named, 1.0, 0.0).astype(bf16)
     earlier = dot(matches, before)
     slot = jnp.sum(jnp.where(named, earlier, 0.0), axis=0, keepdims=True).astype(jnp.int32)
-    place_ref[...] = (block * cap + slot).astype(f32)
-    out_ref[...] = select_rows(one_hot_of(block * stride + slot, (groups * stride, rows), 0), accel_ref[...])
+    place_ref[...] = block * (cap + 1) + slot
     at_slot = lax.broadcasted_iota(jnp.int32, (lanes, rows), 0) % cap == slot
     high = jnp.where(at_slot, column // 32, 0).astype(f32).astype(bf16)
     low = jnp.where(at_slot, column % 32, 0).astype(f32).astype(bf16)
-    columns = dot(matches, high, ((1,), (1,))) * 32.0 + dot(matches, low, ((1,), (1,)))
+    columns_ref[...] = dot(matches, high, ((1,), (1,))) * 32.0 + dot(matches, low, ((1,), (1,)))
+    for copy in copies[2:]:
+        copy.wait()
+
+
+def pack_kernel(cap, place_ref, columns_ref, accel_ref, out_ref, slot_ref):
+    rows = accel_ref.shape[0]
+    groups = columns_ref.shape[0]
+    stride = cap + 1
+    place = place_ref[...]
+    out_ref[...] = select_rows(one_hot_of(place, (groups * stride, rows), 0), accel_ref[...])
     for g in range(groups):
-        out_ref[g * stride + cap : (g + 1) * stride, :] = columns[g : g + 1]
+        out_ref[g * stride + cap : (g + 1) * stride, :] = columns_ref[g : g + 1, :]
+    slot_ref[...] = (place - place // stride).astype(f32)
 
 
 def column_rows(got_ref, cap):
@@ -120,14 +130,8 @@
         rows_ref[g * cap : (g + 1) * cap, :] = got_ref[g * (cap + 1) : (g + 1) * (cap + 1) - 1, :]
     source = select_rows(spread_ref[...], rows_ref[...]).reshape(cx, cy, cz)
     mid_ref[...] = mid0_ref[...] + kappa_ref[...] * (source_gain * source)
-    send_faces(((mid_ref, halo),), xe_ref, xo_ref, ye_ref, yo_ref)
-
-
-def unpack_map_kernel(lanes, place_ref, map_ref):
-    rows, slots = map_ref.shape
-    for at in range(0, rows, lanes):
-        column = as_column(place_ref[:, at : at + lanes]).astype(jnp.int32)
-        map_ref[at : at + lanes, :] = one_hot_of(column, (lanes, slots), 1)
+    send_planes(mid_ref, halo, xe_ref, xo_ref)
+    send_rows(((mid_ref, halo),), ye_ref, yo_ref)
 
 
 def unpack_kernel(map_ref, returned_ref, out_ref):
@@ -144,14 +148,16 @@
     return ref.reshape(cx * cy, cz)[pl.ds(j, cx, stride=cy), :]
 
 
-def send_faces(fields, xe_ref, xo_ref, ye_ref, yo_ref):
-    at = 0
+def send_planes(ref, width, xe_ref, xo_ref):
+    cx, even = ref.shape[0], even_at("gx")
+    xe_ref[...] = ref[pl.ds(jnp.where(even, cx - width, 0), width)]
+    xo_ref[...] = ref[pl.ds(jnp.where(even, 0, cx - width), width)]
+
+
+def send_rows(fields, ye_ref, yo_ref):
+    at, even = 0, even_at("gy")
     for ref, width in fields:
-        cx, cy, _ = ref.shape
-        even = even_at("gx")
-        xe_ref[at : at + width] = ref[pl.ds(jnp.where(even, cx - width, 0), width)]
-        xo_ref[at : at + width] = ref[pl.ds(jnp.where(even, 0, cx - width), width)]
-        even = even_at("gy")
+        cy = ref.shape[1]
         for k in range(width):
             low, high = y_row(ref, k), y_row(ref, cy - width + k)
             ye_ref[at + k] = jnp.where(even, high, low)
@@ -183,14 +189,11 @@
     return pairs
 
 
-def exchange(xe, xo, ye, yo):
+def exchange(axis, to_even, to_odd):
     axes = ("gx", "gy", "blk")
     sizes = tuple(lax.axis_size(a) for a in axes)
-    yo = lax.ppermute(yo, axes, swap_pairs(sizes, "gy", 1))
-    xo = lax.ppermute(xo, axes, swap_pairs(sizes, "gx", 1))
-    xe = lax.ppermute(xe, axes, swap_pairs(sizes, "gx", 0))
-    ye = lax.ppermute(ye, axes, swap_pairs(sizes, "gy", 0))
-    return xe, xo, ye, yo
+    to_odd = lax.ppermute(to_odd, axes, swap_pairs(sizes, axis, 1))
+    return lax.ppermute(to_even, axes, swap_pairs(sizes, axis, 0)), to_odd
 
 
 def swap_cores(x):
@@ -198,8 +201,20 @@
     return lax.ppermute(x, "blk", [(i, count - 1 - i) for i in range(count)])
 
 
-def face_kernel(p_ref, b_ref, xe_ref, xo_ref, ye_ref, yo_ref):
-    send_faces(((p_ref, halo), (b_ref, 2)), xe_ref, xo_ref, ye_ref, yo_ref)
+def row_face_kernel(p_ref, b_ref, slot_ref, xe_ref, xo_ref, ye_ref, yo_ref, p_out_ref, b_out_ref, bx_ref, map_ref):
+    cx, _, lanes = p_ref.shape
+    send_rows(((p_ref, halo), (b_ref, 2)), ye_ref, yo_ref)
+    p_out_ref[...] = p_ref[...]
+    b_out_ref[...] = b_ref[...]
+    low, high = low_and_high("gx", xe_ref[halo:], xo_ref[halo:])
+    bx_ref[0] = low[1] + b_ref[0]
+    bx_ref[1] = low[0] + low[1]
+    bx_ref[2] = high[0] + b_ref[cx - 1]
+    bx_ref[3] = high[0] + high[1]
+    rows, slots = map_ref.shape
+    for at in range(0, rows, lanes):
+        column = as_column(slot_ref[:, at : at + lanes]).astype(jnp.int32)
+        map_ref[at : at + lanes, :] = one_hot_of(column, (lanes, slots), 1)
 
 
 def ahead(x, beyond, lane, step):
@@ -284,14 +299,10 @@
     inner(p_ref, b_ref, po_ref, bo_ref, *scratch, finish)
 
 
-def first_edge_kernel(part_ref, p_ref, b_ref, kappa_ref, xe_ref, xo_ref, ye_ref, yo_ref, mid0_ref, bx_ref, by_ref):
-    cx, cy, _ = p_ref.shape
-    low_x, high_x = low_and_high("gx", xe_ref[...], xo_ref[...])
+def first_edge_kernel(part_ref, p_ref, b_ref, kappa_ref, bx_ref, xe_ref, xo_ref, ye_ref, yo_ref, mid0_ref, by_ref):
+    cy = p_ref.shape[1]
+    low_x, high_x = low_and_high("gx", xe_ref[:halo], xo_ref[:halo])
     low_y, high_y = low_and_high("gy", ye_ref[...], yo_ref[...])
-    bx_ref[0] = low_x[4] + b_ref[0]
-    bx_ref[1] = low_x[3] + low_x[4]
-    bx_ref[2] = high_x[3] + b_ref[cx - 1]
-    bx_ref[3] = high_x[3] + high_x[4]
     by_ref[0] = low_y[4] + y_row(b_ref, 0)
     by_ref[1] = low_y[3] + low_y[4]
     by_ref[2] = high_y[3] + y_row(b_ref, cy - 1)
@@ -335,27 +346,40 @@
     cells = shaped(cx, cy, cz)
 
     in_hbm = [pltpu.with_memory_space_constraint(a, pltpu.HBM) for a in (
-        row_block.reshape(1, rows), row_column.reshape(1, rows), hull_accel)]
-    outgoing, place = run(
-        functools.partial(pack_kernel, groups, cap),
-        [pltpu.VMEM((groups * stride, lanes), f32), shaped(1, rows)],
+        row_block.reshape(1, rows), row_column.reshape(1, rows), hull_accel, pressure, buoyancy)]
+    place, columns, accel, xe, xo = run(
+        functools.partial(slot_kernel, groups, cap),
+        [shaped(1, rows, dtype=jnp.int32), shaped(groups, lanes)] + [pltpu.VMEM(o, f32) for o in ((rows, lanes),) + ((halo + 2, cy, cz),) * 2],
         *in_hbm,
         in_space=pl.ANY,
-        flops=6 * groups * stride * rows * lanes,
-        scratch=[pltpu.VMEM(a.shape, a.dtype) for a in in_hbm] + [pltpu.SemaphoreType.DMA((3,))],
+        flops=2 * groups * rows * rows,
+        scratch=[pltpu.VMEM((1, rows), jnp.int32)] * 2 + [pltpu.SemaphoreType.DMA((7,))],
+    )
+    outgoing, slot = run(
+        functools.partial(pack_kernel, cap),
+        [shaped(groups * stride, lanes), shaped(1, rows)],
+        place,
+        columns,
+        accel,
+        flops=4 * groups * stride * rows * lanes,
     )
     got = lax.all_to_all(
         outgoing.reshape(groups, stride, 1, lanes), ("gx", "gy"), split_axis=0, concat_axis=0, tiled=True
     ).reshape(groups * stride, lanes)
 
-    faces = run(
-        face_kernel,
-        [shaped(halo + 2, cy, cz)] * 2 + [shaped(halo + 2, cx, cz)] * 2,
+    xe, xo = exchange("gx", xe, xo)
+    ye, yo, p_out, b_out, bx, unpack_map = run(
+        row_face_kernel,
+        [shaped(halo + 2, cx, cz)] * 2 + [cells] * 2 + [shaped(4, cy, cz), shaped(rows, slots, dtype=bf16)],
         pressure,
         buoyancy,
-    )
-    beyond = exchange(*faces)
-    other_b = swap_cores(buoyancy)
+        slot,
+        xe,
+        xo,
+        flops=early,
+    )
+    other_b = swap_cores(b_out)
+    ye, yo = exchange("gy", ye, yo)
     scratch = [pltpu.VMEM((cx, cy + 2 * tile, cz), f32)] * 2 + [
         pltpu.VMEM((cx, cy, cz), f32),
         pltpu.VMEM((2, cy + 2 * tile, cz), f32),
@@ -367,13 +391,13 @@
         buoyancy,
         pressure_prev,
         kappa,
-        swap_cores(pressure),
+        swap_cores(p_out),
         other_b,
         flops=100 * cx * cy * cz,
         scratch=scratch,
     )
-    mid0, bx, by = run(
-        first_edge_kernel, [cells, shaped(4, cy, cz), shaped(4, cx, cz)], part, pressure, buoyancy, kappa, *beyond
+    mid0, by = run(
+        first_edge_kernel, [cells, shaped(4, cx, cz)], part, pressure, buoyancy, kappa, bx, xe, xo, ye, yo
     )
 
     mid, *mid_faces = run(
@@ -386,7 +410,7 @@
         scratch=[pltpu.VMEM((cx * cy, slots), bf16), pltpu.VMEM((slots, lanes), f32)],
     )
     other_mid = swap_cores(mid)
-    mid_beyond = exchange(*mid_faces)
+    mid_beyond = exchange("gx", *mid_faces[:2]) + exchange("gy", *mid_faces[2:])
     part, gather_map = run(
         functools.partial(second_inner_kernel, cap),
         [cells, shaped(slots, cx * cy, dtype=bf16)],
@@ -415,9 +439,6 @@
         flops=6 * slots * cx * cy * lanes,
     )
     returned = lax.all_to_all(picked, ("gx", "gy"), split_axis=0, concat_axis=0, tiled=True)
-    (unpack_map,) = run(
-        functools.partial(unpack_map_kernel, lanes), [shaped(rows, slots, dtype=bf16)], place, flops=rows * slots
-    )
     (hull_pressure,) = run(unpack_kernel, [shaped(rows, lanes)], unpack_map, returned, flops=6 * rows * slots * lanes)
     return pressure_next, hull_pressure
 

time: 61.4 us -> 58.2 us (0.948)
  starting transfers between devices: 23.6 us -> 19.8 us
  waiting for transfers between devices: 21.6 us -> 23.3 us
  Pallas kernels: 14.3 us -> 12.8 us
    all_to_all x1, waiting for transfers between devices: 0.39 us -> 8.91 us  [local(): lax.all_to_all(outgoing.reshape(groups, stride, 1, lanes), ('gx', 'gy'),...]
    ppermute x8, waiting for transfers between devices: 7.26 us -> 0.32 us  [the longest x4 0.31 us: exchange(): return (lax.ppermute(to_even, axes, swap_pairs(sizes, axis, 0)), to_odd)]
    ppermute x8, starting transfers between devices: 9.38 us -> 7.16 us  [the longest x4 6.93 us: exchange(): return (lax.ppermute(to_even, axes, swap_pairs(sizes, axis, 0)), to_odd)]
    all_to_all x1, starting transfers between devices: 8.33 us -> 6.41 us  [local(): lax.all_to_all(outgoing.reshape(groups, stride, 1, lanes), ('gx', 'gy'),...]
    pallas_call x9, Pallas kernels: 14.3 us -> 12.8 us  [run(): pl.pallas_call(kernel, out_shape=outs, in_specs=[pl.BlockSpec(memory_spac...]
  transfers between devices with their start and end apart: 13 -> 13, of which waited for: 3 -> 4; matrix products, arithmetic and copies ran while one was open for 1% -> 1% of each run, Pallas kernels for 11% -> 13%
where the time goes in v3:
time: 58.2 us; the launch traced here: 57.8 us
  waiting for transfers between devices  23.3 us (40%)
  starting transfers between devices  19.8 us (34%)
  Pallas kernels  12.8 us (22%)
  local copies, waits for them, and re-layouts  1.07 us (2%)
  between operations  0.82 us (1%)
    all_to_all x1, waiting for transfers between devices, local(): lax.all_to_all(picked, ('gx', 'gy'), split_axis=0, concat_axis=0, tiled=T...  13.8 us
    pallas_call x9, Pallas kernels, run(): pl.pallas_call(kernel, out_shape=outs, in_specs=[pl.BlockSpec(memory_spac...  12.8 us
    all_to_all x1, waiting for transfers between devices, local(): lax.all_to_all(outgoing.reshape(groups, stride, 1, lanes), ('gx', 'gy'),...  8.91 us
    ppermute x4, starting transfers between devices, exchange(): return (lax.ppermute(to_even, axes, swap_pairs(sizes, axis, 0)), to_odd)  6.93 us
    all_to_all x1, starting transfers between devices, local(): lax.all_to_all(outgoing.reshape(groups, stride, 1, lanes), ('gx', 'gy'),...  6.41 us
    all_to_all x1, starting transfers between devices, local(): lax.all_to_all(picked, ('gx', 'gy'), split_axis=0, concat_axis=0, tiled=T...  5.65 us
  transfers between devices with their start and end apart: 13, of which 4 were waited for; matrix products, arithmetic and copies ran while one was open for 1% of the time, Pallas kernels for 13%

profile of v3, /device:TPU:0, one launch (start us, length us, event | category | flops | bytes accessed | tf_op | source)
XLA Modules:
  0.0 57.8 jit_solution(15479448202377086649)
XLA Ops:
  0.7 1.2 %shard_map.86 = (s32[1,512]{1,0:T(1,128)S(1)}, f32[16,128]{1,0:T(8,128)S(1)}, f32[512,128]{1,0:T(8,128)S(1)}, f32[5,64,128]{2,1,0:T(8,128)S(1)}, f32[5,64,128]{2,1,0:T(8,128)S(1)}) custom-call(s32[1,512]{1,0:T(1,128)} %bitcast.6, s32[1,512]{1,0:T(1,128)} %bitcast.7, f32[512,128]{1,0:T(8,128)} %accel_hbm.1, f32[16,64,128]{2,1,0:T(8,128)} %p_ref.7, ...), custom_call_target="tpu_custom_call" | custom-call | flops 8388608 | bytes 1914880 | tf_op jit(solution)/shard_map/pallas_call | solution.py:25
  1.9 3.1 %collective-permute-start = (f32[5,64,128]{2,1,0:T(8,128)S(1)}, f32[5,64,128]{2,1,0:T(8,128)S(1)}, u32[]{:S(2)}, u32[]{:S(2)}) collective-permute-start(f32[5,64,128]{2,1,0:T(8,128)S(1)} %get-tuple-element.31), channel_id=1, source_target_pairs={{0,8},{1,9},{2,10},{3,11},{4,12},{5,13},{6,14},{7,15},{8,0},{9,1},... | collective-permute-start | bytes 491528 | tf_op jit(solution)/shard_map/ppermute | solution.py:196
  5.0 0.0 collective-permute-start.1
  5.0 1.2 %shard_map.87 = (f32[1040,128]{1,0:T(8,128)}, f32[1,512]{1,0:T(1,128)S(1)}) custom-call(s32[1,512]{1,0:T(1,128)S(1)} %get-tuple-element.26.place_ref, f32[16,128]{1,0:T(8,128)S(1)} %get-tuple-element.27.columns_ref, f32[512,128]{1,0:T(8,128)S(1)} %get-tuple-element.28.accel_ref), custom_call_target="tpu_custom_call" | custom-call | flops 272629760 | bytes 806912 | tf_op jit(solution)/shard_map/pallas_call | solution.py:25
  6.2 6.4 %all-to-all-start = ((f32[16,65,1,128]{3,2,1,0:T(1,128)}), f32[16,65,1,128]{3,2,1,0:T(1,128)S(1)}, u32[]{:S(2)}, u32[]{:S(2)}) async-start(f32[16,65,1,128]{3,2,1,0:T(1,128)} %bitcast.2), calls=%async_computation | async-start | bytes 1064960 | tf_op jit(solution)/shard_map/all_to_all | solution.py:366
  12.6 0.0 collective-permute-done.xe_ref
  12.7 0.0 copy-start.6
  12.7 0.0 copy-start.2
  12.7 0.0 copy-start.5
  12.7 0.4 shard_map.88
  13.1 0.2 copy-done.6
  13.3 0.0 collective-permute-start.2
  13.3 0.5 collective-permute-start.3
  13.9 1.9 %collective-permute-start.4 = (f32[5,16,128]{2,1,0:T(8,128)S(1)}, f32[5,16,128]{2,1,0:T(8,128)S(1)}, u32[]{:S(2)}, u32[]{:S(2)}) collective-permute-start(f32[5,16,128]{2,1,0:T(8,128)S(1)} %get-tuple-element.36), channel_id=1, source_target_pairs={{0,2},{1,3},{2,0},{3,1},{4,6},{5,7},{6,4},{7,5},{8,10},{9,11},{10,... | collective-permute-start | bytes 122888 | tf_op jit(solution)/shard_map/ppermute | solution.py:196
  15.8 0.2 collective-permute-done.3.bo_ref
  16.0 2.7 %shard_map.89.part_ref = f32[16,64,128]{2,1,0:T(8,128)S(1)} custom-call(f32[16,64,128]{2,1,0:T(8,128)S(1)} %copy-done.1, f32[16,64,128]{2,1,0:T(8,128)S(1)} %copy-done, f32[16,64,128]{2,1,0:T(8,128)S(1)} %copy-done.5, f32[16,64,128]{2,1,0:T(8,128)S(1)} %copy-done.2, f32[16,64,128]{2,1,0:T(8,128)S(1)} %collective-permute-done.2.po_ref, ...), custom_call_target="tpu_custom_call" | custom-call | flops 13107200 | bytes 3670016 | tf_op jit(solution)/shard_map/pallas_call | solution.py:25
  18.7 0.0 collective-permute-done.5.yo_ref
  18.7 0.3 shard_map.90
  19.0 8.9 %all-to-all-done = f32[16,65,1,128]{3,2,1,0:T(1,128)S(1)} async-done(((f32[16,65,1,128]{3,2,1,0:T(1,128)}), f32[16,65,1,128]{3,2,1,0:T(1,128)S(1)}, u32[]{:S(2)}, u32[]{:S(2)}) %all-to-all-start) | async-done | bytes 532512 | tf_op jit(solution)/shard_map/all_to_all | solution.py:366
  27.9 1.1 %shard_map.91 = (f32[16,64,128]{2,1,0:T(8,128)S(1)}, f32[3,64,128]{2,1,0:T(8,128)S(1)}, f32[3,64,128]{2,1,0:T(8,128)S(1)}, f32[3,16,128]{2,1,0:T(8,128)S(1)}, f32[3,16,128]{2,1,0:T(8,128)S(1)}) custom-call(f32[1040,128]{1,0:T(8,128)S(1)} %bitcast.4, f32[16,64,128]{2,1,0:T(8,128)S(1)} %get-tuple-element.38.mid0_ref, f32[16,64,128]{2,1,0:T(8,128)S(1)} %copy-done.2), custom_call_target="tpu_custom_call" | custom-call | flops 805306368 | bytes 2351104 | tf_op jit(solution)/shard_map/pallas_call | solution.py:25
  29.0 0.1 collective-permute-start.6
  29.1 1.4 %collective-permute-start.7 = (f32[3,64,128]{2,1,0:T(8,128)S(1)}, f32[3,64,128]{2,1,0:T(8,128)S(1)}, u32[]{:S(2)}, u32[]{:S(2)}) collective-permute-start(f32[3,64,128]{2,1,0:T(8,128)S(1)} %get-tuple-element.43), channel_id=1, source_target_pairs={{0,8},{1,9},{2,10},{3,11},{4,12},{5,13},{6,14},{7,15},{8,0},{9,1},... | collective-permute-start | bytes 294920 | tf_op jit(solution)/shard_map/ppermute | solution.py:196
  30.4 0.2 collective-permute-start.8
  30.6 0.6 collective-permute-start.9
  31.2 0.1 collective-permute-start.10
  31.2 3.1 %shard_map.92 = (f32[16,64,128]{2,1,0:T(8,128)S(1)}, bf16[1024,1024]{1,0:T(8,128)(2,1)S(1)}) custom-call(f32[16,64,128]{2,1,0:T(8,128)S(1)} %get-tuple-element.39.mid_ref, f32[16,64,128]{2,1,0:T(8,128)S(1)} %get-tuple-element.38.mid0_ref, f32[16,64,128]{2,1,0:T(8,128)S(1)} %copy-done.1, f32[16,64,128]{2,1,0:T(8,128)S(1)} %copy-done, ...), custom_call_target="tpu_custom_call" | custom-call | flops 13107200 | bytes 8921088 | tf_op jit(solution)/shard_map/pallas_call | solution.py:25
  34.4 0.3 collective-permute-done.9.ye_ref
  34.7 1.7 %shard_map.93 = (f32[16,64,128]{2,1,0:T(8,128)S(1)}, f32[16,64,128]{2,1,0:T(8,128)}) custom-call(f32[16,64,128]{2,1,0:T(8,128)S(1)} %get-tuple-element.40.part_ref, f32[16,64,128]{2,1,0:T(8,128)S(1)} %get-tuple-element.39.mid_ref, f32[16,64,128]{2,1,0:T(8,128)S(1)} %copy-done, f32[16,64,128]{2,1,0:T(8,128)S(1)} %copy-done.2, ...), custom_call_target="tpu_custom_call" | custom-call | flops 805306368 | bytes 7749632 | tf_op jit(solution)/shard_map/pallas_call | solution.py:25
  36.4 5.7 %all-to-all-start.1 = ((f32[16,64,128]{2,1,0:T(8,128)}), f32[16,64,128]{2,1,0:T(8,128)S(1)}, u32[]{:S(2)}, u32[]{:S(2)}) async-start(f32[16,64,128]{2,1,0:T(8,128)} %get-tuple-element.49), calls=%async_computation.1 | async-start | bytes 1048576 | tf_op jit(solution)/shard_map/all_to_all | solution.py:441
  42.1 0.8 %copy.10 = f32[16,64,128]{2,1,0:T(8,128)} copy(f32[16,64,128]{2,1,0:T(8,128)S(1)} %get-tuple-element.50) | data formatting | bytes 1048576
  42.8 13.8 %all-to-all-done.1.returned_ref = f32[16,64,128]{2,1,0:T(8,128)S(1)} async-done(((f32[16,64,128]{2,1,0:T(8,128)}), f32[16,64,128]{2,1,0:T(8,128)S(1)}, u32[]{:S(2)}, u32[]{:S(2)}) %all-to-all-start.1) | async-done | bytes 524320 | tf_op jit(solution)/shard_map/all_to_all | solution.py:441
  56.7 1.1 %shard_map.94 = f32[512,128]{1,0:T(8,128)} custom-call(bf16[512,1024]{1,0:T(8,128)(2,1)S(1)} %copy-done.4, f32[16,64,128]{2,1,0:T(8,128)S(1)} %all-to-all-done.1.returned_ref), custom_call_target="tpu_custom_call" | custom-call | flops 402653184 | bytes 2883584 | tf_op jit(solution)/shard_map/pallas_call | solution.py:25
  (20 shorter events, 0.0 us)
Async XLA Ops:
  0.6 12.1 %copy-start = (f32[16,64,128]{2,1,0:T(8,128)S(1)}, f32[16,64,128]{2,1,0:T(8,128)}, u32[]{:S(2)}) copy-start(f32[16,64,128]{2,1,0:T(8,128)} %b_ref.9) | copy-start | bytes 1572868
  0.6 12.1 %copy-start.1 = (f32[16,64,128]{2,1,0:T(8,128)S(1)}, f32[16,64,128]{2,1,0:T(8,128)}, u32[]{:S(2)}) copy-start(f32[16,64,128]{2,1,0:T(8,128)} %p_ref.7) | copy-start | bytes 1572868
  1.9 10.8 %collective-permute-start = (f32[5,64,128]{2,1,0:T(8,128)S(1)}, f32[5,64,128]{2,1,0:T(8,128)S(1)}, u32[]{:S(2)}, u32[]{:S(2)}) collective-permute-start(f32[5,64,128]{2,1,0:T(8,128)S(1)} %get-tuple-element.31), channel_id=1, source_target_pairs={{0,8},{1,9},{2,10},{3,11},{4,12},{5,13},{6,14},{7,15},{8,0},{9,1},... | collective-permute-start | bytes 491528 | tf_op jit(solution)/shard_map/ppermute | solution.py:196
  5.0 7.7 %collective-permute-start.1 = (f32[5,64,128]{2,1,0:T(8,128)S(1)}, f32[5,64,128]{2,1,0:T(8,128)S(1)}, u32[]{:S(2)}, u32[]{:S(2)}) collective-permute-start(f32[5,64,128]{2,1,0:T(8,128)S(1)} %get-tuple-element.32), channel_id=1, source_target_pairs={{0,1},{1,0},{2,3},{3,2},{4,5},{5,4},{6,7},{7,6},{8,16},{9,17},{10,... | collective-permute-start | bytes 491528 | tf_op jit(solution)/shard_map/ppermute | solution.py:195
  6.2 21.7 %all-to-all-start = ((f32[16,65,1,128]{3,2,1,0:T(1,128)}), f32[16,65,1,128]{3,2,1,0:T(1,128)S(1)}, u32[]{:S(2)}, u32[]{:S(2)}) async-start(f32[16,65,1,128]{3,2,1,0:T(1,128)} %bitcast.2), calls=%async_computation | async-start | bytes 1064960 | tf_op jit(solution)/shard_map/all_to_all | solution.py:366
  12.7 0.7 %copy-start.6 = (f32[5,64,128]{2,1,0:T(8,128)}, f32[5,64,128]{2,1,0:T(8,128)S(1)}, u32[]{:S(2)}) copy-start(f32[5,64,128]{2,1,0:T(8,128)S(1)} %collective-permute-done.1.xo_ref) | copy-start | bytes 491524
  12.7 3.3 %copy-start.2 = (f32[16,64,128]{2,1,0:T(8,128)S(1)}, f32[16,64,128]{2,1,0:T(8,128)}, u32[]{:S(2)}) copy-start(f32[16,64,128]{2,1,0:T(8,128)} %kappa_ref.9) | copy-start | bytes 1572868
  12.7 3.3 %copy-start.5 = (f32[16,64,128]{2,1,0:T(8,128)S(1)}, f32[16,64,128]{2,1,0:T(8,128)}, u32[]{:S(2)}) copy-start(f32[16,64,128]{2,1,0:T(8,128)} %prev_ref.1) | copy-start | bytes 1572868
  13.3 5.4 %copy-start.3 = (bf16[512,1024]{1,0:T(8,128)(2,1)}, bf16[512,1024]{1,0:T(8,128)(2,1)S(1)}, u32[]{:S(2)}) copy-start(bf16[512,1024]{1,0:T(8,128)(2,1)S(1)} %get-tuple-element.48.map_ref) | copy-start | bytes 3145732
  13.3 5.4 %copy-start.7 = (f32[5,64,128]{2,1,0:T(8,128)S(1)}, f32[5,64,128]{2,1,0:T(8,128)}, u32[]{:S(2)}) copy-start(f32[5,64,128]{2,1,0:T(8,128)} %copy-done.6) | copy-start | bytes 491524
  13.3 2.4 %collective-permute-start.2 = (f32[16,64,128]{2,1,0:T(8,128)S(1)}, f32[16,64,128]{2,1,0:T(8,128)S(1)}, u32[]{:S(2)}, u32[]{:S(2)}) collective-permute-start(f32[16,64,128]{2,1,0:T(8,128)S(1)} %get-tuple-element.33), channel_id=1, source_target_pairs={{0,1},{1,0},{2,3},{3,2},{4,5},{5,4},{6,7},{7,6},{8,9},{9,8},{10,11... | collective-permute-start | bytes 1572872 | tf_op jit(solution)/shard_map/ppermute | solution.py:201
  13.3 2.7 %collective-permute-start.3 = (f32[16,64,128]{2,1,0:T(8,128)S(1)}, f32[16,64,128]{2,1,0:T(8,128)S(1)}, u32[]{:S(2)}, u32[]{:S(2)}) collective-permute-start(f32[16,64,128]{2,1,0:T(8,128)S(1)} %get-tuple-element.34), channel_id=1, source_target_pairs={{0,1},{1,0},{2,3},{3,2},{4,5},{5,4},{6,7},{7,6},{8,9},{9,8},{10,11... | collective-permute-start | bytes 1572872 | tf_op jit(solution)/shard_map/ppermute | solution.py:201
  13.9 4.8 %collective-permute-start.4 = (f32[5,16,128]{2,1,0:T(8,128)S(1)}, f32[5,16,128]{2,1,0:T(8,128)S(1)}, u32[]{:S(2)}, u32[]{:S(2)}) collective-permute-start(f32[5,16,128]{2,1,0:T(8,128)S(1)} %get-tuple-element.36), channel_id=1, source_target_pairs={{0,2},{1,3},{2,0},{3,1},{4,6},{5,7},{6,4},{7,5},{8,10},{9,11},{10,... | collective-permute-start | bytes 122888 | tf_op jit(solution)/shard_map/ppermute | solution.py:196
  15.8 2.9 %collective-permute-start.5 = (f32[5,16,128]{2,1,0:T(8,128)S(1)}, f32[5,16,128]{2,1,0:T(8,128)S(1)}, u32[]{:S(2)}, u32[]{:S(2)}) collective-permute-start(f32[5,16,128]{2,1,0:T(8,128)S(1)} %get-tuple-element.37), channel_id=1, source_target_pairs={{0,1},{1,0},{2,4},{3,5},{4,2},{5,3},{6,7},{7,6},{8,9},{9,8},{10,12... | collective-permute-start | bytes 122888 | tf_op jit(solution)/shard_map/ppermute | solution.py:195
  29.0 2.2 %collective-permute-start.6 = (f32[16,64,128]{2,1,0:T(8,128)S(1)}, f32[16,64,128]{2,1,0:T(8,128)S(1)}, u32[]{:S(2)}, u32[]{:S(2)}) collective-permute-start(f32[16,64,128]{2,1,0:T(8,128)S(1)} %get-tuple-element.39.mid_ref), channel_id=1, source_target_pairs={{0,1},{1,0},{2,3},{3,2},{4,5},{5,4},{6,7},{7,6},{8,9},{9,8},{10,11... | collective-permute-start | bytes 1572872 | tf_op jit(solution)/shard_map/ppermute | solution.py:201
  29.1 5.6 %collective-permute-start.7 = (f32[3,64,128]{2,1,0:T(8,128)S(1)}, f32[3,64,128]{2,1,0:T(8,128)S(1)}, u32[]{:S(2)}, u32[]{:S(2)}) collective-permute-start(f32[3,64,128]{2,1,0:T(8,128)S(1)} %get-tuple-element.43), channel_id=1, source_target_pairs={{0,8},{1,9},{2,10},{3,11},{4,12},{5,13},{6,14},{7,15},{8,0},{9,1},... | collective-permute-start | bytes 294920 | tf_op jit(solution)/shard_map/ppermute | solution.py:196
  30.4 4.2 %collective-permute-start.8 = (f32[3,64,128]{2,1,0:T(8,128)S(1)}, f32[3,64,128]{2,1,0:T(8,128)S(1)}, u32[]{:S(2)}, u32[]{:S(2)}) collective-permute-start(f32[3,64,128]{2,1,0:T(8,128)S(1)} %get-tuple-element.44), channel_id=1, source_target_pairs={{0,1},{1,0},{2,3},{3,2},{4,5},{5,4},{6,7},{7,6},{8,16},{9,17},{10,... | collective-permute-start | bytes 294920 | tf_op jit(solution)/shard_map/ppermute | solution.py:195
  30.6 4.1 %collective-permute-start.9 = (f32[3,16,128]{2,1,0:T(8,128)S(1)}, f32[3,16,128]{2,1,0:T(8,128)S(1)}, u32[]{:S(2)}, u32[]{:S(2)}) collective-permute-start(f32[3,16,128]{2,1,0:T(8,128)S(1)} %get-tuple-element.45), channel_id=1, source_target_pairs={{0,2},{1,3},{2,0},{3,1},{4,6},{5,7},{6,4},{7,5},{8,10},{9,11},{10,... | collective-permute-start | bytes 73736 | tf_op jit(solution)/shard_map/ppermute | solution.py:196
  31.2 3.5 %collective-permute-start.10 = (f32[3,16,128]{2,1,0:T(8,128)S(1)}, f32[3,16,128]{2,1,0:T(8,128)S(1)}, u32[]{:S(2)}, u32[]{:S(2)}) collective-permute-start(f32[3,16,128]{2,1,0:T(8,128)S(1)} %get-tuple-element.46), channel_id=1, source_target_pairs={{0,1},{1,0},{2,4},{3,5},{4,2},{5,3},{6,7},{7,6},{8,9},{9,8},{10,12... | collective-permute-start | bytes 73736 | tf_op jit(solution)/shard_map/ppermute | solution.py:195
  36.4 20.3 %copy-start.4 = (bf16[512,1024]{1,0:T(8,128)(2,1)S(1)}, bf16[512,1024]{1,0:T(8,128)(2,1)}, u32[]{:S(2)}) copy-start(bf16[512,1024]{1,0:T(8,128)(2,1)} %copy-done.3) | copy-start | bytes 3145732
  36.4 20.3 %all-to-all-start.1 = ((f32[16,64,128]{2,1,0:T(8,128)}), f32[16,64,128]{2,1,0:T(8,128)S(1)}, u32[]{:S(2)}, u32[]{:S(2)}) async-start(f32[16,64,128]{2,1,0:T(8,128)} %get-tuple-element.49), calls=%async_computation.1 | async-start | bytes 1048576 | tf_op jit(solution)/shard_map/all_to_all | solution.py:441

commit v4 on v3

--- a/solution.py
+++ b/solution.py
@@ -3,6 +3,7 @@
 
 import jax
 import jax.numpy as jnp
+import numpy as np
 from jax import lax
 from jax.experimental import pallas as pl
 from jax.experimental.pallas import tpu as pltpu
@@ -17,16 +18,18 @@
 bf16 = jnp.bfloat16
 VMEM_LIMIT = 16 << 20
 early = 10**11
-
-
-def run(kernel, outs, *args, flops=0, scratch=(), in_space=pltpu.VMEM):
+order_seeds = (205, 205)
+
+
+def run(kernel, outs, *args, flops=0, scratch=(), in_space=pltpu.VMEM, out_space=pltpu.VMEM):
     size = sum(4 * math.prod(a.shape) for a in (*args, *outs))
-    spec = pl.BlockSpec(memory_space=pltpu.VMEM)
     return pl.pallas_call(
         kernel,
         out_shape=outs,
         in_specs=[pl.BlockSpec(memory_space=in_space)] * len(args),
-        out_specs=[spec] * len(outs),
+        out_specs=[
+            pl.BlockSpec(memory_space=m) for m in (out_space if isinstance(out_space, list) else [out_space] * len(outs))
+        ],
         scratch_shapes=list(scratch),
         compiler_params=pltpu.CompilerParams(vmem_limit_bytes=VMEM_LIMIT),
         cost_estimate=pl.CostEstimate(flops=flops, bytes_accessed=size, transcendentals=0),
@@ -62,8 +65,20 @@
     return jnp.sum(jnp.where(diagonal, row, 0.0), axis=1, keepdims=True)
 
 
+def send_orders(groups):
+    return [[int(g) for g in np.random.default_rng(seed).permutation(groups)] for seed in order_seeds]
+
+
+def exchange_rows(x, orders):
+    num_blk = lax.axis_size("blk")
+    members = [[g * num_blk + b for g in orders[b]] for b in range(num_blk)]
+    return lax.all_to_all(
+        x, ("gx", "gy", "blk"), split_axis=0, concat_axis=0, tiled=True, axis_index_groups=members
+    )
+
+
 def slot_kernel(
-    groups, cap, block_hbm, column_hbm, accel_hbm, p_hbm, b_hbm,
+    orders, cap, block_hbm, column_hbm, accel_hbm, p_hbm, b_hbm,
     place_ref, columns_ref, accel_ref, xe_ref, xo_ref, block_ref, column_ref, sems,
 ):
     cx, even = p_hbm.shape[0], even_at("gx")
@@ -81,11 +96,17 @@
     copies[1].wait()
     block = block_ref[...]
     column = column_ref[...] + 1
-    named = lax.broadcasted_iota(jnp.int32, (groups, rows), 0) == block
+    groups = len(orders[0])
+    rank = lax.broadcasted_iota(jnp.int32, (groups, rows), 0)
+    first = lax.axis_index("blk") == 0
+    holds = jnp.zeros((groups, 1), jnp.int32)
+    for at, (one, other) in enumerate(zip(*orders)):
+        holds = jnp.where(rank[:, :1] == at, jnp.where(first, one, other), holds)
+    named = holds == block
     matches = jnp.where(named, 1.0, 0.0).astype(bf16)
     earlier = dot(matches, before)
     slot = jnp.sum(jnp.where(named, earlier, 0.0), axis=0, keepdims=True).astype(jnp.int32)
-    place_ref[...] = block * (cap + 1) + slot
+    place_ref[...] = jnp.sum(jnp.where(named, rank, 0), axis=0, keepdims=True) * (cap + 1) + slot
     at_slot = lax.broadcasted_iota(jnp.int32, (lanes, rows), 0) % cap == slot
     high = jnp.where(at_slot, column // 32, 0).astype(f32).astype(bf16)
     low = jnp.where(at_slot, column % 32, 0).astype(f32).astype(bf16)
@@ -94,15 +115,27 @@
         copy.wait()
 
 
-def pack_kernel(cap, place_ref, columns_ref, accel_ref, out_ref, slot_ref):
-    rows = accel_ref.shape[0]
-    groups = columns_ref.shape[0]
+def pack_kernel(cap, place_ref, columns_ref, accel_ref, out_hbm, slot_ref, out_ref, sems):
+    rows, lanes = accel_ref.shape
     stride = cap + 1
+    total = out_ref.shape[0]
+    chunks = sems.shape[0]
+    chunk = total // chunks
     place = place_ref[...]
-    out_ref[...] = select_rows(one_hot_of(place, (groups * stride, rows), 0), accel_ref[...])
-    for g in range(groups):
-        out_ref[g * stride + cap : (g + 1) * stride, :] = columns_ref[g : g + 1, :]
+    parts = parts_of(accel_ref[...])
+    copies = []
+    for k in range(chunks):
+        part = pl.ds(k * chunk, chunk)
+        y = dot(one_hot_of(place - k * chunk, (chunk, rows), 0), parts)
+        out_ref[part, :] = y[:, :lanes] + y[:, lanes:]
+        for at in range(k * chunk, (k + 1) * chunk):
+            if at % stride == cap:
+                out_ref[at : at + 1, :] = columns_ref[at // stride : at // stride + 1, :]
+        copies.append(pltpu.make_async_copy(out_ref.at[part], out_hbm.at[part], sems.at[k]))
+        copies[k].start()
     slot_ref[...] = (place - place // stride).astype(f32)
+    for copy in copies:
+        copy.wait()
 
 
 def column_rows(got_ref, cap):
@@ -134,9 +167,21 @@
     send_rows(((mid_ref, halo),), ye_ref, yo_ref)
 
 
-def unpack_kernel(map_ref, returned_ref, out_ref):
-    slots = map_ref.shape[1]
-    out_ref[...] = select_rows(map_ref[...], returned_ref[...].reshape(slots, -1))
+def unpack_kernel(map_ref, returned_ref, next_ref, out_hbm, next_hbm, out_ref, sems):
+    copies = [pltpu.make_async_copy(next_ref, next_hbm, sems.at[0])]
+    copies[0].start()
+    rows, slots = map_ref.shape
+    lanes = out_ref.shape[1]
+    parts = parts_of(returned_ref[...].reshape(slots, lanes))
+    half = rows // 2
+    for at in (0, half):
+        part = pl.ds(at, half)
+        y = dot(map_ref[part, :], parts)
+        out_ref[part, :] = y[:, :lanes] + y[:, lanes:]
+        copies.append(pltpu.make_async_copy(out_ref.at[part], out_hbm.at[part], sems.at[len(copies)]))
+        copies[-1].start()
+    for copy in copies:
+        copy.wait()
 
 
 def even_at(axis):
@@ -339,6 +384,7 @@
 
 def local(pressure, pressure_prev, buoyancy, kappa, hull_accel, row_block, row_column):
     groups = lax.axis_size("gx") * lax.axis_size("gy")
+    orders = send_orders(groups)
     rows, lanes = hull_accel.shape
     cap = 2 * rows // groups
     cx, cy, cz = pressure.shape
@@ -348,24 +394,25 @@
     in_hbm = [pltpu.with_memory_space_constraint(a, pltpu.HBM) for a in (
         row_block.reshape(1, rows), row_column.reshape(1, rows), hull_accel, pressure, buoyancy)]
     place, columns, accel, xe, xo = run(
-        functools.partial(slot_kernel, groups, cap),
+        functools.partial(slot_kernel, orders, cap),
         [shaped(1, rows, dtype=jnp.int32), shaped(groups, lanes)] + [pltpu.VMEM(o, f32) for o in ((rows, lanes),) + ((halo + 2, cy, cz),) * 2],
         *in_hbm,
         in_space=pl.ANY,
         flops=2 * groups * rows * rows,
         scratch=[pltpu.VMEM((1, rows), jnp.int32)] * 2 + [pltpu.SemaphoreType.DMA((7,))],
     )
+    chunks = max(n for n in range(1, 6) if groups * stride % (n * tile) == 0)
     outgoing, slot = run(
         functools.partial(pack_kernel, cap),
         [shaped(groups * stride, lanes), shaped(1, rows)],
         place,
         columns,
         accel,
+        out_space=[pl.ANY, pltpu.VMEM],
         flops=4 * groups * stride * rows * lanes,
-    )
-    got = lax.all_to_all(
-        outgoing.reshape(groups, stride, 1, lanes), ("gx", "gy"), split_axis=0, concat_axis=0, tiled=True
-    ).reshape(groups * stride, lanes)
+        scratch=[pltpu.VMEM((groups * stride, lanes), f32), pltpu.SemaphoreType.DMA((chunks,))],
+    )
+    got = exchange_rows(outgoing.reshape(groups, stride, 1, lanes), orders).reshape(groups * stride, lanes)
 
     xe, xo = exchange("gx", xe, xo)
     ye, yo, p_out, b_out, bx, unpack_map = run(
@@ -438,8 +485,17 @@
         *mid_beyond,
         flops=6 * slots * cx * cy * lanes,
     )
-    returned = lax.all_to_all(picked, ("gx", "gy"), split_axis=0, concat_axis=0, tiled=True)
-    (hull_pressure,) = run(unpack_kernel, [shaped(rows, lanes)], unpack_map, returned, flops=6 * rows * slots * lanes)
+    returned = exchange_rows(picked, orders)
+    hull_pressure, pressure_next = run(
+        unpack_kernel,
+        [shaped(rows, lanes), cells],
+        unpack_map,
+        returned,
+        pressure_next,
+        out_space=pl.ANY,
+        flops=4 * rows * slots * lanes,
+        scratch=[pltpu.VMEM((rows, lanes), f32), pltpu.SemaphoreType.DMA((3,))],
+    )
     return pressure_next, hull_pressure
 
 

time: 58.2 us -> 55.4 us (0.952)
  blocking collectives: 0 us -> 20.1 us
  waiting for transfers between devices: 23.3 us -> 8.1 us
  starting transfers between devices: 19.8 us -> 13.9 us
  Pallas kernels: 12.8 us -> 12 us
  local copies, waits for them, and re-layouts: 1.07 us -> 0.28 us
    all_to_all x0 -> x1, blocking collectives: none -> 20.1 us  [exchange_rows(): lax.all_to_all(x, ('gx', 'gy', 'blk'), split_axis=0, concat_axis=0, tiled...]
    all_to_all x2 -> x1, waiting for transfers between devices: 22.7 us -> 5.89 us  [exchange_rows(): lax.all_to_all(x, ('gx', 'gy', 'blk'), split_axis=0, concat_axis=0, tiled...]
    all_to_all x2 -> x1, starting transfers between devices: 12.1 us -> 7.8 us  [exchange_rows(): lax.all_to_all(x, ('gx', 'gy', 'blk'), split_axis=0, concat_axis=0, tiled...]
    ppermute x4, starting transfers between devices: 6.93 us -> 5.26 us  [exchange(): return (lax.ppermute(to_even, axes, swap_pairs(sizes, axis, 0)), to_odd)]
    ppermute x3, waiting for transfers between devices: 0.23 us -> 1.64 us  [swap_cores(): return lax.ppermute(x, 'blk', [(i, count - 1 - i) for i in range(count)])]
    pallas_call x9, Pallas kernels: 12.8 us -> 12 us  [run(): pl.pallas_call(kernel, out_shape=outs, in_specs=[pl.BlockSpec(memory_spac...]
    unnamed x17 -> x16, local copies, waits for them, and re-layouts: 1.07 us -> 0.28 us
  transfers between devices with their start and end apart: 13 -> 12, of which waited for: 4 -> 5; matrix products, arithmetic and copies ran while one was open for 1% -> 0% of each run, Pallas kernels for 13% -> 14%
where the time goes in v4:
time: 55.4 us; the launch traced here: 55.1 us
  blocking collectives  20.1 us (36%)
  starting transfers between devices  13.9 us (25%)
  Pallas kernels  12 us (22%)
  waiting for transfers between devices  8.1 us (15%)
  between operations  0.8 us (1%)
    all_to_all x1, blocking collectives, exchange_rows(): lax.all_to_all(x, ('gx', 'gy', 'blk'), split_axis=0, concat_axis=0, tiled...  20.1 us
    pallas_call x9, Pallas kernels, run(): pl.pallas_call(kernel, out_shape=outs, in_specs=[pl.BlockSpec(memory_spac...  12 us
    all_to_all x1, starting transfers between devices, exchange_rows(): lax.all_to_all(x, ('gx', 'gy', 'blk'), split_axis=0, concat_axis=0, tiled...  7.8 us
    all_to_all x1, waiting for transfers between devices, exchange_rows(): lax.all_to_all(x, ('gx', 'gy', 'blk'), split_axis=0, concat_axis=0, tiled...  5.89 us
    ppermute x4, starting transfers between devices, exchange(): return (lax.ppermute(to_even, axes, swap_pairs(sizes, axis, 0)), to_odd)  5.26 us
    ppermute x3, waiting for transfers between devices, swap_cores(): return lax.ppermute(x, 'blk', [(i, count - 1 - i) for i in range(count)])  1.64 us
  transfers between devices with their start and end apart: 12, of which 5 were waited for; matrix products, arithmetic and copies ran while one was open for 0% of the time, Pallas kernels for 14%

profile of v4, /device:TPU:0, one launch (start us, length us, event | category | flops | bytes accessed | tf_op | source)
XLA Modules:
  0.0 55.1 jit_solution(15813458805828369578)
XLA Ops:
  0.7 1.2 %shard_map.86 = (s32[1,512]{1,0:T(1,128)S(1)}, f32[16,128]{1,0:T(8,128)S(1)}, f32[512,128]{1,0:T(8,128)S(1)}, f32[5,64,128]{2,1,0:T(8,128)S(1)}, f32[5,64,128]{2,1,0:T(8,128)S(1)}) custom-call(s32[1,512]{1,0:T(1,128)} %bitcast.6, s32[1,512]{1,0:T(1,128)} %bitcast.7, f32[512,128]{1,0:T(8,128)} %accel_hbm.1, f32[16,64,128]{2,1,0:T(8,128)} %p_ref.7, ...), custom_call_target="tpu_custom_call" | custom-call | flops 8388608 | bytes 1914880 | tf_op jit(solution)/shard_map/pallas_call | solution.py:26
  1.9 3.1 %collective-permute-start = (f32[5,64,128]{2,1,0:T(8,128)S(1)}, f32[5,64,128]{2,1,0:T(8,128)S(1)}, u32[]{:S(2)}, u32[]{:S(2)}) collective-permute-start(f32[5,64,128]{2,1,0:T(8,128)S(1)} %get-tuple-element.32), channel_id=1, source_target_pairs={{0,8},{1,9},{2,10},{3,11},{4,12},{5,13},{6,14},{7,15},{8,0},{9,1},... | collective-permute-start | bytes 491528 | tf_op jit(solution)/shard_map/ppermute | solution.py:241
  5.0 0.0 collective-permute-start.1
  5.0 1.2 %shard_map.87 = (f32[1040,128]{1,0:T(8,128)}, f32[1,512]{1,0:T(1,128)S(1)}) custom-call(s32[1,512]{1,0:T(1,128)S(1)} %get-tuple-element.28.place_ref, f32[16,128]{1,0:T(8,128)S(1)} %get-tuple-element.29.columns_ref, f32[512,128]{1,0:T(8,128)S(1)} %get-tuple-element.30.accel_ref), custom_call_target="tpu_custom_call" | custom-call | flops 272629760 | bytes 806912 | tf_op jit(solution)/shard_map/pallas_call | solution.py:26
  6.2 7.8 %all-to-all-start = ((f32[16,65,1,128]{3,2,1,0:T(1,128)}), f32[16,65,1,128]{3,2,1,0:T(1,128)S(1)}, u32[]{:S(2)}, u32[]{:S(2)}) async-start(f32[16,65,1,128]{3,2,1,0:T(1,128)} %bitcast.2), calls=%async_computation | async-start | bytes 1064960 | tf_op jit(solution)/shard_map/all_to_all | solution.py:75
  14.0 0.0 collective-permute-done.xe_ref
  14.0 0.0 collective-permute-done.1.xo_ref
  14.0 0.0 copy-start.6
  14.0 0.0 copy-start.2
  14.0 0.0 copy-start.5
  14.0 0.4 shard_map.88
  14.4 0.2 copy-done.6
  14.7 0.0 collective-permute-start.2
  14.7 0.5 collective-permute-start.3
  15.2 1.5 %collective-permute-start.4 = (f32[5,16,128]{2,1,0:T(8,128)S(1)}, f32[5,16,128]{2,1,0:T(8,128)S(1)}, u32[]{:S(2)}, u32[]{:S(2)}) collective-permute-start(f32[5,16,128]{2,1,0:T(8,128)S(1)} %get-tuple-element.39), channel_id=1, source_target_pairs={{0,2},{1,3},{2,0},{3,1},{4,6},{5,7},{6,4},{7,5},{8,10},{9,11},{10,... | collective-permute-start | bytes 122888 | tf_op jit(solution)/shard_map/ppermute | solution.py:241
  16.6 0.0 collective-permute-start.5
  16.6 0.7 %collective-permute-done.3.bo_ref = f32[16,64,128]{2,1,0:T(8,128)S(1)} collective-permute-done((f32[16,64,128]{2,1,0:T(8,128)S(1)}, f32[16,64,128]{2,1,0:T(8,128)S(1)}, u32[]{:S(2)}, u32[]{:S(2)}) %collective-permute-start.3) | collective-permute-done | bytes 524320 | tf_op jit(solution)/shard_map/ppermute | solution.py:246
  17.3 2.7 %shard_map.89.part_ref = f32[16,64,128]{2,1,0:T(8,128)S(1)} custom-call(f32[16,64,128]{2,1,0:T(8,128)S(1)} %copy-done.1, f32[16,64,128]{2,1,0:T(8,128)S(1)} %copy-done, f32[16,64,128]{2,1,0:T(8,128)S(1)} %copy-done.5, f32[16,64,128]{2,1,0:T(8,128)S(1)} %copy-done.2, f32[16,64,128]{2,1,0:T(8,128)S(1)} %collective-permute-done.2.po_ref, ...), custom_call_target="tpu_custom_call" | custom-call | flops 13107200 | bytes 3670016 | tf_op jit(solution)/shard_map/pallas_call | solution.py:26
  20.0 0.4 collective-permute-done.4.ye_ref
  20.4 0.3 shard_map.90
  20.7 5.9 %all-to-all-done = f32[16,65,1,128]{3,2,1,0:T(1,128)S(1)} async-done(((f32[16,65,1,128]{3,2,1,0:T(1,128)}), f32[16,65,1,128]{3,2,1,0:T(1,128)S(1)}, u32[]{:S(2)}, u32[]{:S(2)}) %all-to-all-start) | async-done | bytes 532512 | tf_op jit(solution)/shard_map/all_to_all | solution.py:75
  26.6 1.1 %shard_map.91 = (f32[16,64,128]{2,1,0:T(8,128)S(1)}, f32[3,64,128]{2,1,0:T(8,128)S(1)}, f32[3,64,128]{2,1,0:T(8,128)S(1)}, f32[3,16,128]{2,1,0:T(8,128)S(1)}, f32[3,16,128]{2,1,0:T(8,128)S(1)}) custom-call(f32[1040,128]{1,0:T(8,128)S(1)} %bitcast.4, f32[16,64,128]{2,1,0:T(8,128)S(1)} %get-tuple-element.41.mid0_ref, f32[16,64,128]{2,1,0:T(8,128)S(1)} %copy-done.2), custom_call_target="tpu_custom_call" | custom-call | flops 805306368 | bytes 2351104 | tf_op jit(solution)/shard_map/pallas_call | solution.py:26
  27.7 0.1 collective-permute-start.6
  27.8 0.3 collective-permute-start.7
  28.0 0.2 collective-permute-start.8
  28.3 0.4 collective-permute-start.9
  28.7 1.0 %collective-permute-done.6.mo_ref = f32[16,64,128]{2,1,0:T(8,128)S(1)} collective-permute-done((f32[16,64,128]{2,1,0:T(8,128)S(1)}, f32[16,64,128]{2,1,0:T(8,128)S(1)}, u32[]{:S(2)}, u32[]{:S(2)}) %collective-permute-start.6) | collective-permute-done | bytes 524320 | tf_op jit(solution)/shard_map/ppermute | solution.py:246
  29.7 3.1 %shard_map.92 = (f32[16,64,128]{2,1,0:T(8,128)S(1)}, bf16[1024,1024]{1,0:T(8,128)(2,1)S(1)}) custom-call(f32[16,64,128]{2,1,0:T(8,128)S(1)} %get-tuple-element.42.mid_ref, f32[16,64,128]{2,1,0:T(8,128)S(1)} %get-tuple-element.41.mid0_ref, f32[16,64,128]{2,1,0:T(8,128)S(1)} %copy-done.1, f32[16,64,128]{2,1,0:T(8,128)S(1)} %copy-done, ...), custom_call_target="tpu_custom_call" | custom-call | flops 13107200 | bytes 8921088 | tf_op jit(solution)/shard_map/pallas_call | solution.py:26
  32.8 0.1 collective-permute-done.7.xe_ref
  33.0 0.9 %shard_map.93 = (f32[16,64,128]{2,1,0:T(8,128)S(1)}, f32[16,64,128]{2,1,0:T(8,128)S(1)}) custom-call(f32[16,64,128]{2,1,0:T(8,128)S(1)} %get-tuple-element.43.part_ref, f32[16,64,128]{2,1,0:T(8,128)S(1)} %get-tuple-element.42.mid_ref, f32[16,64,128]{2,1,0:T(8,128)S(1)} %copy-done, f32[16,64,128]{2,1,0:T(8,128)S(1)} %copy-done.2, ...), custom_call_target="tpu_custom_call" | custom-call | flops 805306368 | bytes 7749632 | tf_op jit(solution)/shard_map/pallas_call | solution.py:26
  33.9 20.1 %all_to_all.10.returned_ref = f32[16,64,128]{2,1,0:T(8,128)S(1)} all-to-all(f32[16,64,128]{2,1,0:T(8,128)S(1)} %get-tuple-element.50), channel_id=1, replica_groups={{16,4,8,20,24,12,10,28,6,26,18,30,0,14,22,2},{17,5,9,21,25,13,11,29,7,2..., dimensions={0} | all-to-all | bytes 1048576 | tf_op jit(solution)/shard_map/all_to_all | solution.py:75
  54.0 1.2 %shard_map.94 = (f32[512,128]{1,0:T(8,128)}, f32[16,64,128]{2,1,0:T(8,128)}) custom-call(bf16[512,1024]{1,0:T(8,128)(2,1)S(1)} %copy-done.4, f32[16,64,128]{2,1,0:T(8,128)S(1)} %all_to_all.10.returned_ref, f32[16,64,128]{2,1,0:T(8,128)S(1)} %get-tuple-element.51.next_ref), custom_call_target="tpu_custom_call" | custom-call | flops 268435456 | bytes 3932160 | tf_op jit(solution)/shard_map/pallas_call | solution.py:26
  (18 shorter events, 0.0 us)
Async XLA Ops:
  0.6 13.4 %copy-start = (f32[16,64,128]{2,1,0:T(8,128)S(1)}, f32[16,64,128]{2,1,0:T(8,128)}, u32[]{:S(2)}) copy-start(f32[16,64,128]{2,1,0:T(8,128)} %b_ref.9) | copy-start | bytes 1572868
  0.6 13.4 %copy-start.1 = (f32[16,64,128]{2,1,0:T(8,128)S(1)}, f32[16,64,128]{2,1,0:T(8,128)}, u32[]{:S(2)}) copy-start(f32[16,64,128]{2,1,0:T(8,128)} %p_ref.7) | copy-start | bytes 1572868
  1.9 12.1 %collective-permute-start = (f32[5,64,128]{2,1,0:T(8,128)S(1)}, f32[5,64,128]{2,1,0:T(8,128)S(1)}, u32[]{:S(2)}, u32[]{:S(2)}) collective-permute-start(f32[5,64,128]{2,1,0:T(8,128)S(1)} %get-tuple-element.32), channel_id=1, source_target_pairs={{0,8},{1,9},{2,10},{3,11},{4,12},{5,13},{6,14},{7,15},{8,0},{9,1},... | collective-permute-start | bytes 491528 | tf_op jit(solution)/shard_map/ppermute | solution.py:241
  5.0 9.0 %collective-permute-start.1 = (f32[5,64,128]{2,1,0:T(8,128)S(1)}, f32[5,64,128]{2,1,0:T(8,128)S(1)}, u32[]{:S(2)}, u32[]{:S(2)}) collective-permute-start(f32[5,64,128]{2,1,0:T(8,128)S(1)} %get-tuple-element.33), channel_id=1, source_target_pairs={{0,1},{1,0},{2,3},{3,2},{4,5},{5,4},{6,7},{7,6},{8,16},{9,17},{10,... | collective-permute-start | bytes 491528 | tf_op jit(solution)/shard_map/ppermute | solution.py:240
  6.2 20.4 %all-to-all-start = ((f32[16,65,1,128]{3,2,1,0:T(1,128)}), f32[16,65,1,128]{3,2,1,0:T(1,128)S(1)}, u32[]{:S(2)}, u32[]{:S(2)}) async-start(f32[16,65,1,128]{3,2,1,0:T(1,128)} %bitcast.2), calls=%async_computation | async-start | bytes 1064960 | tf_op jit(solution)/shard_map/all_to_all | solution.py:75
  14.0 0.7 %copy-start.6 = (f32[5,64,128]{2,1,0:T(8,128)}, f32[5,64,128]{2,1,0:T(8,128)S(1)}, u32[]{:S(2)}) copy-start(f32[5,64,128]{2,1,0:T(8,128)S(1)} %collective-permute-done.1.xo_ref) | copy-start | bytes 491524
  14.0 3.3 %copy-start.2 = (f32[16,64,128]{2,1,0:T(8,128)S(1)}, f32[16,64,128]{2,1,0:T(8,128)}, u32[]{:S(2)}) copy-start(f32[16,64,128]{2,1,0:T(8,128)} %kappa_ref.9) | copy-start | bytes 1572868
  14.0 3.3 %copy-start.5 = (f32[16,64,128]{2,1,0:T(8,128)S(1)}, f32[16,64,128]{2,1,0:T(8,128)}, u32[]{:S(2)}) copy-start(f32[16,64,128]{2,1,0:T(8,128)} %prev_ref.1) | copy-start | bytes 1572868
  14.7 5.8 %copy-start.3 = (bf16[512,1024]{1,0:T(8,128)(2,1)}, bf16[512,1024]{1,0:T(8,128)(2,1)S(1)}, u32[]{:S(2)}) copy-start(bf16[512,1024]{1,0:T(8,128)(2,1)S(1)} %get-tuple-element.34.map_ref) | copy-start | bytes 3145732
  14.7 5.8 %copy-start.7 = (f32[5,64,128]{2,1,0:T(8,128)S(1)}, f32[5,64,128]{2,1,0:T(8,128)}, u32[]{:S(2)}) copy-start(f32[5,64,128]{2,1,0:T(8,128)} %copy-done.6) | copy-start | bytes 491524
  14.7 2.0 %collective-permute-start.2 = (f32[16,64,128]{2,1,0:T(8,128)S(1)}, f32[16,64,128]{2,1,0:T(8,128)S(1)}, u32[]{:S(2)}, u32[]{:S(2)}) collective-permute-start(f32[16,64,128]{2,1,0:T(8,128)S(1)} %get-tuple-element.36), channel_id=1, source_target_pairs={{0,1},{1,0},{2,3},{3,2},{4,5},{5,4},{6,7},{7,6},{8,9},{9,8},{10,11... | collective-permute-start | bytes 1572872 | tf_op jit(solution)/shard_map/ppermute | solution.py:246
  14.7 2.7 %collective-permute-start.3 = (f32[16,64,128]{2,1,0:T(8,128)S(1)}, f32[16,64,128]{2,1,0:T(8,128)S(1)}, u32[]{:S(2)}, u32[]{:S(2)}) collective-permute-start(f32[16,64,128]{2,1,0:T(8,128)S(1)} %get-tuple-element.37), channel_id=1, source_target_pairs={{0,1},{1,0},{2,3},{3,2},{4,5},{5,4},{6,7},{7,6},{8,9},{9,8},{10,11... | collective-permute-start | bytes 1572872 | tf_op jit(solution)/shard_map/ppermute | solution.py:246
  15.2 5.2 %collective-permute-start.4 = (f32[5,16,128]{2,1,0:T(8,128)S(1)}, f32[5,16,128]{2,1,0:T(8,128)S(1)}, u32[]{:S(2)}, u32[]{:S(2)}) collective-permute-start(f32[5,16,128]{2,1,0:T(8,128)S(1)} %get-tuple-element.39), channel_id=1, source_target_pairs={{0,2},{1,3},{2,0},{3,1},{4,6},{5,7},{6,4},{7,5},{8,10},{9,11},{10,... | collective-permute-start | bytes 122888 | tf_op jit(solution)/shard_map/ppermute | solution.py:241
  16.6 3.8 %collective-permute-start.5 = (f32[5,16,128]{2,1,0:T(8,128)S(1)}, f32[5,16,128]{2,1,0:T(8,128)S(1)}, u32[]{:S(2)}, u32[]{:S(2)}) collective-permute-start(f32[5,16,128]{2,1,0:T(8,128)S(1)} %get-tuple-element.40), channel_id=1, source_target_pairs={{0,1},{1,0},{2,4},{3,5},{4,2},{5,3},{6,7},{7,6},{8,9},{9,8},{10,12... | collective-permute-start | bytes 122888 | tf_op jit(solution)/shard_map/ppermute | solution.py:240
  27.7 2.0 %collective-permute-start.6 = (f32[16,64,128]{2,1,0:T(8,128)S(1)}, f32[16,64,128]{2,1,0:T(8,128)S(1)}, u32[]{:S(2)}, u32[]{:S(2)}) collective-permute-start(f32[16,64,128]{2,1,0:T(8,128)S(1)} %get-tuple-element.42.mid_ref), channel_id=1, source_target_pairs={{0,1},{1,0},{2,3},{3,2},{4,5},{5,4},{6,7},{7,6},{8,9},{9,8},{10,11... | collective-permute-start | bytes 1572872 | tf_op jit(solution)/shard_map/ppermute | solution.py:246
  27.8 5.2 %collective-permute-start.7 = (f32[3,64,128]{2,1,0:T(8,128)S(1)}, f32[3,64,128]{2,1,0:T(8,128)S(1)}, u32[]{:S(2)}, u32[]{:S(2)}) collective-permute-start(f32[3,64,128]{2,1,0:T(8,128)S(1)} %get-tuple-element.46), channel_id=1, source_target_pairs={{0,8},{1,9},{2,10},{3,11},{4,12},{5,13},{6,14},{7,15},{8,0},{9,1},... | collective-permute-start | bytes 294920 | tf_op jit(solution)/shard_map/ppermute | solution.py:241
  28.0 4.9 %collective-permute-start.8 = (f32[3,64,128]{2,1,0:T(8,128)S(1)}, f32[3,64,128]{2,1,0:T(8,128)S(1)}, u32[]{:S(2)}, u32[]{:S(2)}) collective-permute-start(f32[3,64,128]{2,1,0:T(8,128)S(1)} %get-tuple-element.47), channel_id=1, source_target_pairs={{0,1},{1,0},{2,3},{3,2},{4,5},{5,4},{6,7},{7,6},{8,16},{9,17},{10,... | collective-permute-start | bytes 294920 | tf_op jit(solution)/shard_map/ppermute | solution.py:240
  28.3 4.5 %collective-permute-start.9 = (f32[3,16,128]{2,1,0:T(8,128)S(1)}, f32[3,16,128]{2,1,0:T(8,128)S(1)}, u32[]{:S(2)}, u32[]{:S(2)}) collective-permute-start(f32[3,16,128]{2,1,0:T(8,128)S(1)} %get-tuple-element.48), channel_id=1, source_target_pairs={{0,2},{1,3},{2,0},{3,1},{4,6},{5,7},{6,4},{7,5},{8,10},{9,11},{10,... | collective-permute-start | bytes 73736 | tf_op jit(solution)/shard_map/ppermute | solution.py:241
  28.7 4.1 %collective-permute-start.10 = (f32[3,16,128]{2,1,0:T(8,128)S(1)}, f32[3,16,128]{2,1,0:T(8,128)S(1)}, u32[]{:S(2)}, u32[]{:S(2)}) collective-permute-start(f32[3,16,128]{2,1,0:T(8,128)S(1)} %get-tuple-element.49), channel_id=1, source_target_pairs={{0,1},{1,0},{2,4},{3,5},{4,2},{5,3},{6,7},{7,6},{8,9},{9,8},{10,12... | collective-permute-start | bytes 73736 | tf_op jit(solution)/shard_map/ppermute | solution.py:240
  33.0 21.0 %copy-start.4 = (bf16[512,1024]{1,0:T(8,128)(2,1)S(1)}, bf16[512,1024]{1,0:T(8,128)(2,1)}, u32[]{:S(2)}) copy-start(bf16[512,1024]{1,0:T(8,128)(2,1)} %copy-done.3) | copy-start | bytes 3145732

commit v5 on v4

--- a/solution.py
+++ b/solution.py
@@ -18,7 +18,7 @@
 bf16 = jnp.bfloat16
 VMEM_LIMIT = 16 << 20
 early = 10**11
-order_seeds = (205, 205)
+order_seeds = (56, 205)
 
 
 def run(kernel, outs, *args, flops=0, scratch=(), in_space=pltpu.VMEM, out_space=pltpu.VMEM):
@@ -56,7 +56,9 @@
 
 
 def one_hot_of(index, shape, dim):
-    return jnp.where(lax.broadcasted_iota(jnp.int32, shape, dim) == index, 1.0, 0.0).astype(bf16)
+    short = jnp.int16
+    places = lax.broadcasted_iota(jnp.int32, shape, dim).astype(short)
+    return jnp.where(places == index.astype(short), bf16(1), bf16(0))
 
 
 def as_column(row):

time: 55.4 us -> 53.7 us (0.969)
  blocking collectives: 20.1 us -> 18.8 us
  waiting for transfers between devices: 8.1 us -> 7.19 us
  starting transfers between devices: 13.9 us -> 14.7 us
    ppermute x4, starting transfers between devices: 5.26 us -> 7 us  [exchange(): return (lax.ppermute(to_even, axes, swap_pairs(sizes, axis, 0)), to_odd)]
    all_to_all x1, blocking collectives: 20.1 us -> 18.8 us  [exchange_rows(): lax.all_to_all(x, ('gx', 'gy', 'blk'), split_axis=0, concat_axis=0, tiled...]
    ppermute x4, waiting for transfers between devices: 0.56 us -> 1.54 us  [exchange(): return (lax.ppermute(to_even, axes, swap_pairs(sizes, axis, 0)), to_odd)]
    ppermute x3, waiting for transfers between devices: 1.64 us -> 0.68 us  [swap_cores(): return lax.ppermute(x, 'blk', [(i, count - 1 - i) for i in range(count)])]
    all_to_all x1, waiting for transfers between devices: 5.89 us -> 4.96 us  [exchange_rows(): lax.all_to_all(x, ('gx', 'gy', 'blk'), split_axis=0, concat_axis=0, tiled...]
    all_to_all x1, starting transfers between devices: 7.8 us -> 6.9 us  [exchange_rows(): lax.all_to_all(x, ('gx', 'gy', 'blk'), split_axis=0, concat_axis=0, tiled...]
  transfers between devices with their start and end apart: 12 -> 12, of which waited for: 5 -> 3; matrix products, arithmetic and copies ran while one was open for 0% -> 0% of each run, Pallas kernels for 14% -> 14%
where the time goes in v5:
time: 53.7 us; the launch traced here: 53.4 us
  blocking collectives  18.8 us (35%)
  starting transfers between devices  14.7 us (27%)
  Pallas kernels  11.6 us (22%)
  waiting for transfers between devices  7.19 us (13%)
  between operations  0.82 us (2%)
    all_to_all x1, blocking collectives, exchange_rows(): lax.all_to_all(x, ('gx', 'gy', 'blk'), split_axis=0, concat_axis=0, tiled...  18.8 us
    pallas_call x9, Pallas kernels, run(): pl.pallas_call(kernel, out_shape=outs, in_specs=[pl.BlockSpec(memory_spac...  11.6 us
    ppermute x4, starting transfers between devices, exchange(): return (lax.ppermute(to_even, axes, swap_pairs(sizes, axis, 0)), to_odd)  7 us
    all_to_all x1, starting transfers between devices, exchange_rows(): lax.all_to_all(x, ('gx', 'gy', 'blk'), split_axis=0, concat_axis=0, tiled...  6.9 us
    all_to_all x1, waiting for transfers between devices, exchange_rows(): lax.all_to_all(x, ('gx', 'gy', 'blk'), split_axis=0, concat_axis=0, tiled...  4.96 us
    ppermute x4, waiting for transfers between devices, exchange(): return (lax.ppermute(to_even, axes, swap_pairs(sizes, axis, 0)), to_odd)  1.54 us
  transfers between devices with their start and end apart: 12, of which 3 were waited for; matrix products, arithmetic and copies ran while one was open for 0% of the time, Pallas kernels for 14%

profile of v5, /device:TPU:0, one launch (start us, length us, event | category | flops | bytes accessed | tf_op | source)
XLA Modules:
  0.0 53.4 jit_solution(17696634292593803042)
XLA Ops:
  0.7 1.2 %shard_map.86 = (s32[1,512]{1,0:T(1,128)S(1)}, f32[16,128]{1,0:T(8,128)S(1)}, f32[512,128]{1,0:T(8,128)S(1)}, f32[5,64,128]{2,1,0:T(8,128)S(1)}, f32[5,64,128]{2,1,0:T(8,128)S(1)}) custom-call(s32[1,512]{1,0:T(1,128)} %bitcast.6, s32[1,512]{1,0:T(1,128)} %bitcast.7, f32[512,128]{1,0:T(8,128)} %accel_hbm.1, f32[16,64,128]{2,1,0:T(8,128)} %p_ref.7, ...), custom_call_target="tpu_custom_call" | custom-call | flops 8388608 | bytes 1914880 | tf_op jit(solution)/shard_map/pallas_call | solution.py:26
  1.9 3.1 %collective-permute-start = (f32[5,64,128]{2,1,0:T(8,128)S(1)}, f32[5,64,128]{2,1,0:T(8,128)S(1)}, u32[]{:S(2)}, u32[]{:S(2)}) collective-permute-start(f32[5,64,128]{2,1,0:T(8,128)S(1)} %get-tuple-element.32), channel_id=1, source_target_pairs={{0,8},{1,9},{2,10},{3,11},{4,12},{5,13},{6,14},{7,15},{8,0},{9,1},... | collective-permute-start | bytes 491528 | tf_op jit(solution)/shard_map/ppermute | solution.py:243
  5.0 0.0 collective-permute-start.1
  5.0 1.2 %shard_map.87 = (f32[1040,128]{1,0:T(8,128)}, f32[1,512]{1,0:T(1,128)S(1)}) custom-call(s32[1,512]{1,0:T(1,128)S(1)} %get-tuple-element.28.place_ref, f32[16,128]{1,0:T(8,128)S(1)} %get-tuple-element.29.columns_ref, f32[512,128]{1,0:T(8,128)S(1)} %get-tuple-element.30.accel_ref), custom_call_target="tpu_custom_call" | custom-call | flops 272629760 | bytes 806912 | tf_op jit(solution)/shard_map/pallas_call | solution.py:26
  6.2 6.9 %all-to-all-start = ((f32[16,65,1,128]{3,2,1,0:T(1,128)}), f32[16,65,1,128]{3,2,1,0:T(1,128)S(1)}, u32[]{:S(2)}, u32[]{:S(2)}) async-start(f32[16,65,1,128]{3,2,1,0:T(1,128)} %bitcast.2), calls=%async_computation | async-start | bytes 1064960 | tf_op jit(solution)/shard_map/all_to_all | solution.py:77
  13.1 0.0 collective-permute-done.xe_ref
  13.1 0.0 copy-start.6
  13.1 0.0 copy-start.2
  13.1 0.0 copy-start.5
  13.1 0.3 shard_map.88
  13.5 0.3 copy-done.6
  13.8 0.0 collective-permute-start.2
  13.8 0.5 collective-permute-start.3
  14.3 1.5 %collective-permute-start.4 = (f32[5,16,128]{2,1,0:T(8,128)S(1)}, f32[5,16,128]{2,1,0:T(8,128)S(1)}, u32[]{:S(2)}, u32[]{:S(2)}) collective-permute-start(f32[5,16,128]{2,1,0:T(8,128)S(1)} %get-tuple-element.39), channel_id=1, source_target_pairs={{0,2},{1,3},{2,0},{3,1},{4,6},{5,7},{6,4},{7,5},{8,10},{9,11},{10,... | collective-permute-start | bytes 122888 | tf_op jit(solution)/shard_map/ppermute | solution.py:243
  15.7 0.0 collective-permute-start.5
  15.7 0.7 %collective-permute-done.3.bo_ref = f32[16,64,128]{2,1,0:T(8,128)S(1)} collective-permute-done((f32[16,64,128]{2,1,0:T(8,128)S(1)}, f32[16,64,128]{2,1,0:T(8,128)S(1)}, u32[]{:S(2)}, u32[]{:S(2)}) %collective-permute-start.3) | collective-permute-done | bytes 524320 | tf_op jit(solution)/shard_map/ppermute | solution.py:248
  16.4 2.7 %shard_map.89.part_ref = f32[16,64,128]{2,1,0:T(8,128)S(1)} custom-call(f32[16,64,128]{2,1,0:T(8,128)S(1)} %copy-done.1, f32[16,64,128]{2,1,0:T(8,128)S(1)} %copy-done, f32[16,64,128]{2,1,0:T(8,128)S(1)} %copy-done.5, f32[16,64,128]{2,1,0:T(8,128)S(1)} %copy-done.2, f32[16,64,128]{2,1,0:T(8,128)S(1)} %collective-permute-done.2.po_ref, ...), custom_call_target="tpu_custom_call" | custom-call | flops 13107200 | bytes 3670016 | tf_op jit(solution)/shard_map/pallas_call | solution.py:26
  19.1 1.5 %collective-permute-done.4.ye_ref = f32[5,16,128]{2,1,0:T(8,128)S(1)} collective-permute-done((f32[5,16,128]{2,1,0:T(8,128)S(1)}, f32[5,16,128]{2,1,0:T(8,128)S(1)}, u32[]{:S(2)}, u32[]{:S(2)}) %collective-permute-start.4) | collective-permute-done | bytes 40992 | tf_op jit(solution)/shard_map/ppermute | solution.py:243
  20.7 0.3 shard_map.90
  20.9 5.0 %all-to-all-done = f32[16,65,1,128]{3,2,1,0:T(1,128)S(1)} async-done(((f32[16,65,1,128]{3,2,1,0:T(1,128)}), f32[16,65,1,128]{3,2,1,0:T(1,128)S(1)}, u32[]{:S(2)}, u32[]{:S(2)}) %all-to-all-start) | async-done | bytes 532512 | tf_op jit(solution)/shard_map/all_to_all | solution.py:77
  25.9 0.8 %shard_map.91 = (f32[16,64,128]{2,1,0:T(8,128)S(1)}, f32[3,64,128]{2,1,0:T(8,128)S(1)}, f32[3,64,128]{2,1,0:T(8,128)S(1)}, f32[3,16,128]{2,1,0:T(8,128)S(1)}, f32[3,16,128]{2,1,0:T(8,128)S(1)}) custom-call(f32[1040,128]{1,0:T(8,128)S(1)} %bitcast.4, f32[16,64,128]{2,1,0:T(8,128)S(1)} %get-tuple-element.41.mid0_ref, f32[16,64,128]{2,1,0:T(8,128)S(1)} %copy-done.2), custom_call_target="tpu_custom_call" | custom-call | flops 805306368 | bytes 2351104 | tf_op jit(solution)/shard_map/pallas_call | solution.py:26
  26.7 0.1 collective-permute-start.6
  26.8 1.6 %collective-permute-start.7 = (f32[3,64,128]{2,1,0:T(8,128)S(1)}, f32[3,64,128]{2,1,0:T(8,128)S(1)}, u32[]{:S(2)}, u32[]{:S(2)}) collective-permute-start(f32[3,64,128]{2,1,0:T(8,128)S(1)} %get-tuple-element.46), channel_id=1, source_target_pairs={{0,8},{1,9},{2,10},{3,11},{4,12},{5,13},{6,14},{7,15},{8,0},{9,1},... | collective-permute-start | bytes 294920 | tf_op jit(solution)/shard_map/ppermute | solution.py:243
  28.4 0.2 collective-permute-start.8
  28.5 0.9 %collective-permute-start.9 = (f32[3,16,128]{2,1,0:T(8,128)S(1)}, f32[3,16,128]{2,1,0:T(8,128)S(1)}, u32[]{:S(2)}, u32[]{:S(2)}) collective-permute-start(f32[3,16,128]{2,1,0:T(8,128)S(1)} %get-tuple-element.48), channel_id=1, source_target_pairs={{0,2},{1,3},{2,0},{3,1},{4,6},{5,7},{6,4},{7,5},{8,10},{9,11},{10,... | collective-permute-start | bytes 73736 | tf_op jit(solution)/shard_map/ppermute | solution.py:243
  29.4 0.1 collective-permute-start.10
  29.5 3.0 %shard_map.92 = (f32[16,64,128]{2,1,0:T(8,128)S(1)}, bf16[1024,1024]{1,0:T(8,128)(2,1)S(1)}) custom-call(f32[16,64,128]{2,1,0:T(8,128)S(1)} %get-tuple-element.42.mid_ref, f32[16,64,128]{2,1,0:T(8,128)S(1)} %get-tuple-element.41.mid0_ref, f32[16,64,128]{2,1,0:T(8,128)S(1)} %copy-done.1, f32[16,64,128]{2,1,0:T(8,128)S(1)} %copy-done, ...), custom_call_target="tpu_custom_call" | custom-call | flops 13107200 | bytes 8921088 | tf_op jit(solution)/shard_map/pallas_call | solution.py:26
  32.5 0.0 collective-permute-done.9.ye_ref
  32.5 0.0 collective-permute-done.7.xe_ref
  32.5 0.9 %shard_map.93 = (f32[16,64,128]{2,1,0:T(8,128)S(1)}, f32[16,64,128]{2,1,0:T(8,128)S(1)}) custom-call(f32[16,64,128]{2,1,0:T(8,128)S(1)} %get-tuple-element.43.part_ref, f32[16,64,128]{2,1,0:T(8,128)S(1)} %get-tuple-element.42.mid_ref, f32[16,64,128]{2,1,0:T(8,128)S(1)} %copy-done, f32[16,64,128]{2,1,0:T(8,128)S(1)} %copy-done.2, ...), custom_call_target="tpu_custom_call" | custom-call | flops 805306368 | bytes 7749632 | tf_op jit(solution)/shard_map/pallas_call | solution.py:26
  33.4 18.8 %all_to_all.10.returned_ref = f32[16,64,128]{2,1,0:T(8,128)S(1)} all-to-all(f32[16,64,128]{2,1,0:T(8,128)S(1)} %get-tuple-element.50), channel_id=1, replica_groups={{8,14,4,12,24,16,6,0,28,30,26,2,18,22,10,20},{17,5,9,21,25,13,11,29,7,2..., dimensions={0} | all-to-all | bytes 1048576 | tf_op jit(solution)/shard_map/all_to_all | solution.py:77
  52.2 1.2 %shard_map.94 = (f32[512,128]{1,0:T(8,128)}, f32[16,64,128]{2,1,0:T(8,128)}) custom-call(bf16[512,1024]{1,0:T(8,128)(2,1)S(1)} %copy-done.4, f32[16,64,128]{2,1,0:T(8,128)S(1)} %all_to_all.10.returned_ref, f32[16,64,128]{2,1,0:T(8,128)S(1)} %get-tuple-element.51.next_ref), custom_call_target="tpu_custom_call" | custom-call | flops 268435456 | bytes 3932160 | tf_op jit(solution)/shard_map/pallas_call | solution.py:26
  (18 shorter events, 0.0 us)
Async XLA Ops:
  0.6 12.5 %copy-start = (f32[16,64,128]{2,1,0:T(8,128)S(1)}, f32[16,64,128]{2,1,0:T(8,128)}, u32[]{:S(2)}) copy-start(f32[16,64,128]{2,1,0:T(8,128)} %b_ref.9) | copy-start | bytes 1572868
  0.6 12.5 %copy-start.1 = (f32[16,64,128]{2,1,0:T(8,128)S(1)}, f32[16,64,128]{2,1,0:T(8,128)}, u32[]{:S(2)}) copy-start(f32[16,64,128]{2,1,0:T(8,128)} %p_ref.7) | copy-start | bytes 1572868
  1.9 11.2 %collective-permute-start = (f32[5,64,128]{2,1,0:T(8,128)S(1)}, f32[5,64,128]{2,1,0:T(8,128)S(1)}, u32[]{:S(2)}, u32[]{:S(2)}) collective-permute-start(f32[5,64,128]{2,1,0:T(8,128)S(1)} %get-tuple-element.32), channel_id=1, source_target_pairs={{0,8},{1,9},{2,10},{3,11},{4,12},{5,13},{6,14},{7,15},{8,0},{9,1},... | collective-permute-start | bytes 491528 | tf_op jit(solution)/shard_map/ppermute | solution.py:243
  5.0 8.1 %collective-permute-start.1 = (f32[5,64,128]{2,1,0:T(8,128)S(1)}, f32[5,64,128]{2,1,0:T(8,128)S(1)}, u32[]{:S(2)}, u32[]{:S(2)}) collective-permute-start(f32[5,64,128]{2,1,0:T(8,128)S(1)} %get-tuple-element.33), channel_id=1, source_target_pairs={{0,1},{1,0},{2,3},{3,2},{4,5},{5,4},{6,7},{7,6},{8,16},{9,17},{10,... | collective-permute-start | bytes 491528 | tf_op jit(solution)/shard_map/ppermute | solution.py:242
  6.2 19.7 %all-to-all-start = ((f32[16,65,1,128]{3,2,1,0:T(1,128)}), f32[16,65,1,128]{3,2,1,0:T(1,128)S(1)}, u32[]{:S(2)}, u32[]{:S(2)}) async-start(f32[16,65,1,128]{3,2,1,0:T(1,128)} %bitcast.2), calls=%async_computation | async-start | bytes 1064960 | tf_op jit(solution)/shard_map/all_to_all | solution.py:77
  13.1 0.7 %copy-start.6 = (f32[5,64,128]{2,1,0:T(8,128)}, f32[5,64,128]{2,1,0:T(8,128)S(1)}, u32[]{:S(2)}) copy-start(f32[5,64,128]{2,1,0:T(8,128)S(1)} %collective-permute-done.1.xo_ref) | copy-start | bytes 491524
  13.1 3.3 %copy-start.2 = (f32[16,64,128]{2,1,0:T(8,128)S(1)}, f32[16,64,128]{2,1,0:T(8,128)}, u32[]{:S(2)}) copy-start(f32[16,64,128]{2,1,0:T(8,128)} %kappa_ref.9) | copy-start | bytes 1572868
  13.1 3.3 %copy-start.5 = (f32[16,64,128]{2,1,0:T(8,128)S(1)}, f32[16,64,128]{2,1,0:T(8,128)}, u32[]{:S(2)}) copy-start(f32[16,64,128]{2,1,0:T(8,128)} %prev_ref.1) | copy-start | bytes 1572868
  13.8 6.9 %copy-start.3 = (bf16[512,1024]{1,0:T(8,128)(2,1)}, bf16[512,1024]{1,0:T(8,128)(2,1)S(1)}, u32[]{:S(2)}) copy-start(bf16[512,1024]{1,0:T(8,128)(2,1)S(1)} %get-tuple-element.34.map_ref) | copy-start | bytes 3145732
  13.8 6.9 %copy-start.7 = (f32[5,64,128]{2,1,0:T(8,128)S(1)}, f32[5,64,128]{2,1,0:T(8,128)}, u32[]{:S(2)}) copy-start(f32[5,64,128]{2,1,0:T(8,128)} %copy-done.6) | copy-start | bytes 491524
  13.8 2.0 %collective-permute-start.2 = (f32[16,64,128]{2,1,0:T(8,128)S(1)}, f32[16,64,128]{2,1,0:T(8,128)S(1)}, u32[]{:S(2)}, u32[]{:S(2)}) collective-permute-start(f32[16,64,128]{2,1,0:T(8,128)S(1)} %get-tuple-element.36), channel_id=1, source_target_pairs={{0,1},{1,0},{2,3},{3,2},{4,5},{5,4},{6,7},{7,6},{8,9},{9,8},{10,11... | collective-permute-start | bytes 1572872 | tf_op jit(solution)/shard_map/ppermute | solution.py:248
  13.8 2.7 %collective-permute-start.3 = (f32[16,64,128]{2,1,0:T(8,128)S(1)}, f32[16,64,128]{2,1,0:T(8,128)S(1)}, u32[]{:S(2)}, u32[]{:S(2)}) collective-permute-start(f32[16,64,128]{2,1,0:T(8,128)S(1)} %get-tuple-element.37), channel_id=1, source_target_pairs={{0,1},{1,0},{2,3},{3,2},{4,5},{5,4},{6,7},{7,6},{8,9},{9,8},{10,11... | collective-permute-start | bytes 1572872 | tf_op jit(solution)/shard_map/ppermute | solution.py:248
  14.3 6.4 %collective-permute-start.4 = (f32[5,16,128]{2,1,0:T(8,128)S(1)}, f32[5,16,128]{2,1,0:T(8,128)S(1)}, u32[]{:S(2)}, u32[]{:S(2)}) collective-permute-start(f32[5,16,128]{2,1,0:T(8,128)S(1)} %get-tuple-element.39), channel_id=1, source_target_pairs={{0,2},{1,3},{2,0},{3,1},{4,6},{5,7},{6,4},{7,5},{8,10},{9,11},{10,... | collective-permute-start | bytes 122888 | tf_op jit(solution)/shard_map/ppermute | solution.py:243
  15.7 4.9 %collective-permute-start.5 = (f32[5,16,128]{2,1,0:T(8,128)S(1)}, f32[5,16,128]{2,1,0:T(8,128)S(1)}, u32[]{:S(2)}, u32[]{:S(2)}) collective-permute-start(f32[5,16,128]{2,1,0:T(8,128)S(1)} %get-tuple-element.40), channel_id=1, source_target_pairs={{0,1},{1,0},{2,4},{3,5},{4,2},{5,3},{6,7},{7,6},{8,9},{9,8},{10,12... | collective-permute-start | bytes 122888 | tf_op jit(solution)/shard_map/ppermute | solution.py:242
  26.7 2.8 %collective-permute-start.6 = (f32[16,64,128]{2,1,0:T(8,128)S(1)}, f32[16,64,128]{2,1,0:T(8,128)S(1)}, u32[]{:S(2)}, u32[]{:S(2)}) collective-permute-start(f32[16,64,128]{2,1,0:T(8,128)S(1)} %get-tuple-element.42.mid_ref), channel_id=1, source_target_pairs={{0,1},{1,0},{2,3},{3,2},{4,5},{5,4},{6,7},{7,6},{8,9},{9,8},{10,11... | collective-permute-start | bytes 1572872 | tf_op jit(solution)/shard_map/ppermute | solution.py:248
  26.8 5.7 %collective-permute-start.7 = (f32[3,64,128]{2,1,0:T(8,128)S(1)}, f32[3,64,128]{2,1,0:T(8,128)S(1)}, u32[]{:S(2)}, u32[]{:S(2)}) collective-permute-start(f32[3,64,128]{2,1,0:T(8,128)S(1)} %get-tuple-element.46), channel_id=1, source_target_pairs={{0,8},{1,9},{2,10},{3,11},{4,12},{5,13},{6,14},{7,15},{8,0},{9,1},... | collective-permute-start | bytes 294920 | tf_op jit(solution)/shard_map/ppermute | solution.py:243
  28.4 4.2 %collective-permute-start.8 = (f32[3,64,128]{2,1,0:T(8,128)S(1)}, f32[3,64,128]{2,1,0:T(8,128)S(1)}, u32[]{:S(2)}, u32[]{:S(2)}) collective-permute-start(f32[3,64,128]{2,1,0:T(8,128)S(1)} %get-tuple-element.47), channel_id=1, source_target_pairs={{0,1},{1,0},{2,3},{3,2},{4,5},{5,4},{6,7},{7,6},{8,16},{9,17},{10,... | collective-permute-start | bytes 294920 | tf_op jit(solution)/shard_map/ppermute | solution.py:242
  28.5 4.0 %collective-permute-start.9 = (f32[3,16,128]{2,1,0:T(8,128)S(1)}, f32[3,16,128]{2,1,0:T(8,128)S(1)}, u32[]{:S(2)}, u32[]{:S(2)}) collective-permute-start(f32[3,16,128]{2,1,0:T(8,128)S(1)} %get-tuple-element.48), channel_id=1, source_target_pairs={{0,2},{1,3},{2,0},{3,1},{4,6},{5,7},{6,4},{7,5},{8,10},{9,11},{10,... | collective-permute-start | bytes 73736 | tf_op jit(solution)/shard_map/ppermute | solution.py:243
  29.4 3.1 %collective-permute-start.10 = (f32[3,16,128]{2,1,0:T(8,128)S(1)}, f32[3,16,128]{2,1,0:T(8,128)S(1)}, u32[]{:S(2)}, u32[]{:S(2)}) collective-permute-start(f32[3,16,128]{2,1,0:T(8,128)S(1)} %get-tuple-element.49), channel_id=1, source_target_pairs={{0,1},{1,0},{2,4},{3,5},{4,2},{5,3},{6,7},{7,6},{8,9},{9,8},{10,12... | collective-permute-start | bytes 73736 | tf_op jit(solution)/shard_map/ppermute | solution.py:242
  32.5 19.7 %copy-start.4 = (bf16[512,1024]{1,0:T(8,128)(2,1)S(1)}, bf16[512,1024]{1,0:T(8,128)(2,1)}, u32[]{:S(2)}) copy-start(bf16[512,1024]{1,0:T(8,128)(2,1)} %copy-done.3) | copy-start | bytes 3145732

commit v6 on v5

--- a/solution.py
+++ b/solution.py
@@ -18,7 +18,7 @@
 bf16 = jnp.bfloat16
 VMEM_LIMIT = 16 << 20
 early = 10**11
-order_seeds = (56, 205)
+order_seeds = ((183, 183), (150, 205))
 
 
 def run(kernel, outs, *args, flops=0, scratch=(), in_space=pltpu.VMEM, out_space=pltpu.VMEM):
@@ -67,8 +67,22 @@
     return jnp.sum(jnp.where(diagonal, row, 0.0), axis=1, keepdims=True)
 
 
-def send_orders(groups):
-    return [[int(g) for g in np.random.default_rng(seed).permutation(groups)] for seed in order_seeds]
+def block_orders(groups):
+    return [
+        [[int(g) for g in np.random.default_rng(seed).permutation(groups)] for seed in seeds] for seeds in order_seeds
+    ]
+
+
+def of_core(first, second):
+    return jnp.where(lax.axis_index("blk") == 0, first, second)
+
+
+def find_blocks(orders, block, rank):
+    held = jnp.zeros((rank.shape[0], 1), jnp.int32)
+    for at, pair in enumerate(zip(*orders)):
+        held = jnp.where(rank[:, :1] == at, of_core(*pair), held)
+    named = held == block
+    return named, jnp.sum(jnp.where(named, rank, 0), axis=0, keepdims=True)
 
 
 def exchange_rows(x, orders):
@@ -80,8 +94,8 @@
 
 
 def slot_kernel(
-    orders, cap, block_hbm, column_hbm, accel_hbm, p_hbm, b_hbm,
-    place_ref, columns_ref, accel_ref, xe_ref, xo_ref, block_ref, column_ref, sems,
+    out_orders, back_orders, cap, block_hbm, column_hbm, accel_hbm, p_hbm, b_hbm,
+    place_ref, back_ref, columns_ref, accel_ref, xe_ref, xo_ref, block_ref, column_ref, sems,
 ):
     cx, even = p_hbm.shape[0], even_at("gx")
     moves = [(block_hbm, block_ref), (column_hbm, column_ref), (accel_hbm, accel_ref)]
@@ -98,17 +112,15 @@
     copies[1].wait()
     block = block_ref[...]
     column = column_ref[...] + 1
-    groups = len(orders[0])
+    groups = len(out_orders[0])
     rank = lax.broadcasted_iota(jnp.int32, (groups, rows), 0)
-    first = lax.axis_index("blk") == 0
-    holds = jnp.zeros((groups, 1), jnp.int32)
-    for at, (one, other) in enumerate(zip(*orders)):
-        holds = jnp.where(rank[:, :1] == at, jnp.where(first, one, other), holds)
-    named = holds == block
+    named, out_at = find_blocks(out_orders, block, rank)
+    _, back_at = find_blocks(back_orders, block, rank)
     matches = jnp.where(named, 1.0, 0.0).astype(bf16)
     earlier = dot(matches, before)
     slot = jnp.sum(jnp.where(named, earlier, 0.0), axis=0, keepdims=True).astype(jnp.int32)
-    place_ref[...] = jnp.sum(jnp.where(named, rank, 0), axis=0, keepdims=True) * (cap + 1) + slot
+    place_ref[...] = out_at * (cap + 1) + slot
+    back_ref[...] = (back_at * cap + slot).astype(f32)
     at_slot = lax.broadcasted_iota(jnp.int32, (lanes, rows), 0) % cap == slot
     high = jnp.where(at_slot, column // 32, 0).astype(f32).astype(bf16)
     low = jnp.where(at_slot, column % 32, 0).astype(f32).astype(bf16)
@@ -117,7 +129,7 @@
         copy.wait()
 
 
-def pack_kernel(cap, place_ref, columns_ref, accel_ref, out_hbm, slot_ref, out_ref, sems):
+def pack_kernel(cap, place_ref, back_ref, columns_ref, accel_ref, out_hbm, slot_ref, out_ref, sems):
     rows, lanes = accel_ref.shape
     stride = cap + 1
     total = out_ref.shape[0]
@@ -135,22 +147,22 @@
                 out_ref[at : at + 1, :] = columns_ref[at // stride : at // stride + 1, :]
         copies.append(pltpu.make_async_copy(out_ref.at[part], out_hbm.at[part], sems.at[k]))
         copies[k].start()
-    slot_ref[...] = (place - place // stride).astype(f32)
+    slot_ref[...] = back_ref[...]
     for copy in copies:
         copy.wait()
 
 
-def column_rows(got_ref, cap):
+def column_rows(got_ref, cap, blocks):
     lanes = got_ref.shape[1]
     stride = cap + 1
-    groups = got_ref.shape[0] // stride
     per = lanes // cap
     lane = lax.broadcasted_iota(jnp.int32, (1, lanes), 1) // cap
     rows = []
-    for g in range(0, groups, per):
-        row = got_ref[g * stride + cap : (g + 1) * stride, :]
+    for g in range(0, len(blocks), per):
+        parts = [got_ref[pl.ds(at * stride + cap, 1), :] for at in blocks[g : g + per]]
+        row = parts[0]
         for k in range(1, per):
-            row = jnp.where(lane == k, got_ref[(g + k) * stride + cap : (g + k + 1) * stride, :], row)
+            row = jnp.where(lane == k, parts[k], row)
         rows.append(row - 1.0)
     return rows
 
@@ -159,7 +171,7 @@
     lanes = got_ref.shape[1]
     groups = got_ref.shape[0] // (cap + 1)
     cx, cy, cz = mid0_ref.shape
-    for at, row in enumerate(column_rows(got_ref, cap)):
+    for at, row in enumerate(column_rows(got_ref, cap, range(groups))):
         spread_ref[:, at * lanes : (at + 1) * lanes] = one_hot_of(row.astype(jnp.int32), (cx * cy, lanes), 0)
     for g in range(groups):
         rows_ref[g * cap : (g + 1) * cap, :] = got_ref[g * (cap + 1) : (g + 1) * (cap + 1) - 1, :]
@@ -359,7 +371,7 @@
 
 
 def second_inner_kernel(
-    cap, mid_ref, mid0_ref, p_ref, b_ref, kappa_ref, mo_ref, bo_ref, got_ref, out_ref, map_ref, *scratch
+    out_orders, back_orders, cap, mid_ref, mid0_ref, p_ref, b_ref, kappa_ref, mo_ref, bo_ref, got_ref, out_ref, map_ref, *scratch
 ):
     cx, cy, _ = p_ref.shape
     lanes = got_ref.shape[1]
@@ -368,7 +380,8 @@
         out_ref[i] = 3.0 * u - mid0_ref[i] - p_ref[i] + kappa_ref[i] * (lap_scale * total)
 
     inner(mid_ref, b_ref, mo_ref, bo_ref, *scratch, finish)
-    for at, row in enumerate(column_rows(got_ref, cap)):
+    blocks = [of_core(*(o.index(b[k]) for o, b in zip(out_orders, back_orders))) for k in range(len(out_orders[0]))]
+    for at, row in enumerate(column_rows(got_ref, cap, blocks)):
         column = as_column(row).astype(jnp.int32)
         map_ref[at * lanes : (at + 1) * lanes, :] = one_hot_of(column, (lanes, cx * cy), 1)
 
@@ -386,7 +399,7 @@
 
 def local(pressure, pressure_prev, buoyancy, kappa, hull_accel, row_block, row_column):
     groups = lax.axis_size("gx") * lax.axis_size("gy")
-    orders = send_orders(groups)
+    orders = block_orders(groups)
     rows, lanes = hull_accel.shape
     cap = 2 * rows // groups
     cx, cy, cz = pressure.shape
@@ -395,9 +408,9 @@
 
     in_hbm = [pltpu.with_memory_space_constraint(a, pltpu.HBM) for a in (
         row_block.reshape(1, rows), row_column.reshape(1, rows), hull_accel, pressure, buoyancy)]
-    place, columns, accel, xe, xo = run(
-        functools.partial(slot_kernel, orders, cap),
-        [shaped(1, rows, dtype=jnp.int32), shaped(groups, lanes)] + [pltpu.VMEM(o, f32) for o in ((rows, lanes),) + ((halo + 2, cy, cz),) * 2],
+    place, back, columns, accel, xe, xo = run(
+        functools.partial(slot_kernel, *orders, cap),
+        [shaped(1, rows, dtype=jnp.int32), shaped(1, rows), shaped(groups, lanes)] + [pltpu.VMEM(o, f32) for o in ((rows, lanes),) + ((halo + 2, cy, cz),) * 2],
         *in_hbm,
         in_space=pl.ANY,
         flops=2 * groups * rows * rows,
@@ -408,13 +421,14 @@
         functools.partial(pack_kernel, cap),
         [shaped(groups * stride, lanes), shaped(1, rows)],
         place,
+        back,
         columns,
         accel,
         out_space=[pl.ANY, pltpu.VMEM],
         flops=4 * groups * stride * rows * lanes,
         scratch=[pltpu.VMEM((groups * stride, lanes), f32), pltpu.SemaphoreType.DMA((chunks,))],
     )
-    got = exchange_rows(outgoing.reshape(groups, stride, 1, lanes), orders).reshape(groups * stride, lanes)
+    got = exchange_rows(outgoing.reshape(groups, stride, 1, lanes), orders[0]).reshape(groups * stride, lanes)
 
     xe, xo = exchange("gx", xe, xo)
     ye, yo, p_out, b_out, bx, unpack_map = run(
@@ -461,7 +475,7 @@
     other_mid = swap_cores(mid)
     mid_beyond = exchange("gx", *mid_faces[:2]) + exchange("gy", *mid_faces[2:])
     part, gather_map = run(
-        functools.partial(second_inner_kernel, cap),
+        functools.partial(second_inner_kernel, *orders, cap),
         [cells, shaped(slots, cx * cy, dtype=bf16)],
         mid,
         mid0,
@@ -487,7 +501,7 @@
         *mid_beyond,
         flops=6 * slots * cx * cy * lanes,
     )
-    returned = exchange_rows(picked, orders)
+    returned = exchange_rows(picked, orders[1])
     hull_pressure, pressure_next = run(
         unpack_kernel,
         [shaped(rows, lanes), cells],

time: 53.7 us -> 52.2 us (0.972)
  blocking collectives: 18.8 us -> 17.8 us
  waiting for transfers between devices: 7.19 us -> 6.31 us
    ppermute x4, waiting for transfers between devices: 1.54 us -> 0.21 us  [exchange(): return (lax.ppermute(to_even, axes, swap_pairs(sizes, axis, 0)), to_odd)]
    all_to_all x1, blocking collectives: 18.8 us -> 17.8 us  [exchange_rows(): lax.all_to_all(x, ('gx', 'gy', 'blk'), split_axis=0, concat_axis=0, tiled...]
    all_to_all x1, starting transfers between devices: 6.9 us -> 7.8 us  [exchange_rows(): lax.all_to_all(x, ('gx', 'gy', 'blk'), split_axis=0, concat_axis=0, tiled...]
    ppermute x4, starting transfers between devices: 7 us -> 6.46 us  [exchange(): return (lax.ppermute(to_even, axes, swap_pairs(sizes, axis, 0)), to_odd)]
where the time goes in v6:
time: 52.2 us; the launch traced here: 51.9 us
  blocking collectives  17.8 us (34%)
  starting transfers between devices  15.1 us (29%)
  Pallas kernels  11.6 us (22%)
  waiting for transfers between devices  6.31 us (12%)
  between operations  0.8 us (2%)
    all_to_all x1, blocking collectives, exchange_rows(): lax.all_to_all(x, ('gx', 'gy', 'blk'), split_axis=0, concat_axis=0, tiled...  17.8 us
    pallas_call x9, Pallas kernels, run(): pl.pallas_call(kernel, out_shape=outs, in_specs=[pl.BlockSpec(memory_spac...  11.6 us
    all_to_all x1, starting transfers between devices, exchange_rows(): lax.all_to_all(x, ('gx', 'gy', 'blk'), split_axis=0, concat_axis=0, tiled...  7.8 us
    ppermute x4, starting transfers between devices, exchange(): return (lax.ppermute(to_even, axes, swap_pairs(sizes, axis, 0)), to_odd)  6.46 us
    all_to_all x1, waiting for transfers between devices, exchange_rows(): lax.all_to_all(x, ('gx', 'gy', 'blk'), split_axis=0, concat_axis=0, tiled...  5.41 us
  transfers between devices with their start and end apart: 12, of which 3 were waited for; matrix products, arithmetic and copies ran while one was open for 0% of the time, Pallas kernels for 14%

profile of v6, /device:TPU:0, one launch (start us, length us, event | category | flops | bytes accessed | tf_op | source)
XLA Modules:
  0.0 51.9 jit_solution(10850840265015587912)
XLA Ops:
  0.7 1.2 %shard_map.86 = (s32[1,512]{1,0:T(1,128)S(1)}, f32[1,512]{1,0:T(1,128)S(1)}, f32[16,128]{1,0:T(8,128)S(1)}, f32[512,128]{1,0:T(8,128)S(1)}, f32[5,64,128]{2,1,0:T(8,128)S(1)}, /*index=5*/f32[5,64,128]{2,1,0:T(8,128)S(1)}) custom-call(s32[1,512]{1,0:T(1,128)} %bitcast.6, s32[1,512]{1,0:T(1,128)} %bitcast.7, f32[512,128]{1,0:T(8,128)} %accel_hbm.1, ...), custom_call_target="tpu_custom_call" | custom-call | flops 8388608 | bytes 1916928 | tf_op jit(solution)/shard_map/pallas_call | solution.py:26
  1.9 3.1 %collective-permute-start = (f32[5,64,128]{2,1,0:T(8,128)S(1)}, f32[5,64,128]{2,1,0:T(8,128)S(1)}, u32[]{:S(2)}, u32[]{:S(2)}) collective-permute-start(f32[5,64,128]{2,1,0:T(8,128)S(1)} %get-tuple-element.34), channel_id=1, source_target_pairs={{0,8},{1,9},{2,10},{3,11},{4,12},{5,13},{6,14},{7,15},{8,0},{9,1},... | collective-permute-start | bytes 491528 | tf_op jit(solution)/shard_map/ppermute | solution.py:255
  5.0 1.2 %shard_map.87 = (f32[1040,128]{1,0:T(8,128)}, f32[1,512]{1,0:T(1,128)S(1)}) custom-call(s32[1,512]{1,0:T(1,128)S(1)} %get-tuple-element.29.place_ref, f32[1,512]{1,0:T(1,128)S(1)} %get-tuple-element.30.back_ref, f32[16,128]{1,0:T(8,128)S(1)} %get-tuple-element.31.columns_ref, f32[512,128]{1,0:T(8,128)S(1)} %get-tuple-element.32.accel_ref), custom_call_target="tpu_custom_call" | custom-call | flops 272629760 | bytes 808960 | tf_op jit(solution)/shard_map/pallas_call | solution.py:26
  6.2 7.8 %all-to-all-start = ((f32[16,65,1,128]{3,2,1,0:T(1,128)}), f32[16,65,1,128]{3,2,1,0:T(1,128)S(1)}, u32[]{:S(2)}, u32[]{:S(2)}) async-start(f32[16,65,1,128]{3,2,1,0:T(1,128)} %bitcast.2), calls=%async_computation | async-start | bytes 1064960 | tf_op jit(solution)/shard_map/all_to_all | solution.py:91
  14.0 0.0 collective-permute-done.xe_ref
  14.0 0.0 copy-start.6
  14.0 0.0 copy-start.2
  14.0 0.0 copy-start.5
  14.0 0.3 shard_map.88
  14.4 0.3 copy-done.6
  14.7 0.0 collective-permute-start.2
  14.7 0.5 collective-permute-start.3
  15.2 1.5 %collective-permute-start.4 = (f32[5,16,128]{2,1,0:T(8,128)S(1)}, f32[5,16,128]{2,1,0:T(8,128)S(1)}, u32[]{:S(2)}, u32[]{:S(2)}) collective-permute-start(f32[5,16,128]{2,1,0:T(8,128)S(1)} %get-tuple-element.41), channel_id=1, source_target_pairs={{0,2},{1,3},{2,0},{3,1},{4,6},{5,7},{6,4},{7,5},{8,10},{9,11},{10,... | collective-permute-start | bytes 122888 | tf_op jit(solution)/shard_map/ppermute | solution.py:255
  16.6 0.0 collective-permute-start.5
  16.6 0.0 collective-permute-done.2.po_ref
  16.6 0.7 %collective-permute-done.3.bo_ref = f32[16,64,128]{2,1,0:T(8,128)S(1)} collective-permute-done((f32[16,64,128]{2,1,0:T(8,128)S(1)}, f32[16,64,128]{2,1,0:T(8,128)S(1)}, u32[]{:S(2)}, u32[]{:S(2)}) %collective-permute-start.3) | collective-permute-done | bytes 524320 | tf_op jit(solution)/shard_map/ppermute | solution.py:260
  17.3 2.7 %shard_map.89.part_ref = f32[16,64,128]{2,1,0:T(8,128)S(1)} custom-call(f32[16,64,128]{2,1,0:T(8,128)S(1)} %copy-done.1, f32[16,64,128]{2,1,0:T(8,128)S(1)} %copy-done, f32[16,64,128]{2,1,0:T(8,128)S(1)} %copy-done.5, f32[16,64,128]{2,1,0:T(8,128)S(1)} %copy-done.2, f32[16,64,128]{2,1,0:T(8,128)S(1)} %collective-permute-done.2.po_ref, ...), custom_call_target="tpu_custom_call" | custom-call | flops 13107200 | bytes 3670016 | tf_op jit(solution)/shard_map/pallas_call | solution.py:26
  20.0 0.2 collective-permute-done.4.ye_ref
  20.2 0.3 shard_map.90
  20.5 5.4 %all-to-all-done = f32[16,65,1,128]{3,2,1,0:T(1,128)S(1)} async-done(((f32[16,65,1,128]{3,2,1,0:T(1,128)}), f32[16,65,1,128]{3,2,1,0:T(1,128)S(1)}, u32[]{:S(2)}, u32[]{:S(2)}) %all-to-all-start) | async-done | bytes 532512 | tf_op jit(solution)/shard_map/all_to_all | solution.py:91
  25.9 0.8 %shard_map.91 = (f32[16,64,128]{2,1,0:T(8,128)S(1)}, f32[3,64,128]{2,1,0:T(8,128)S(1)}, f32[3,64,128]{2,1,0:T(8,128)S(1)}, f32[3,16,128]{2,1,0:T(8,128)S(1)}, f32[3,16,128]{2,1,0:T(8,128)S(1)}) custom-call(f32[1040,128]{1,0:T(8,128)S(1)} %bitcast.4, f32[16,64,128]{2,1,0:T(8,128)S(1)} %get-tuple-element.43.mid0_ref, f32[16,64,128]{2,1,0:T(8,128)S(1)} %copy-done.2), custom_call_target="tpu_custom_call" | custom-call | flops 805306368 | bytes 2351104 | tf_op jit(solution)/shard_map/pallas_call | solution.py:26
  26.7 0.1 collective-permute-start.6
  26.8 0.4 collective-permute-start.7
  27.2 0.2 collective-permute-start.8
  27.4 1.5 %collective-permute-start.9 = (f32[3,16,128]{2,1,0:T(8,128)S(1)}, f32[3,16,128]{2,1,0:T(8,128)S(1)}, u32[]{:S(2)}, u32[]{:S(2)}) collective-permute-start(f32[3,16,128]{2,1,0:T(8,128)S(1)} %get-tuple-element.50), channel_id=1, source_target_pairs={{0,2},{1,3},{2,0},{3,1},{4,6},{5,7},{6,4},{7,5},{8,10},{9,11},{10,... | collective-permute-start | bytes 73736 | tf_op jit(solution)/shard_map/ppermute | solution.py:255
  28.9 0.1 collective-permute-start.10
  28.9 3.0 %shard_map.92 = (f32[16,64,128]{2,1,0:T(8,128)S(1)}, bf16[1024,1024]{1,0:T(8,128)(2,1)S(1)}) custom-call(f32[16,64,128]{2,1,0:T(8,128)S(1)} %get-tuple-element.44.mid_ref, f32[16,64,128]{2,1,0:T(8,128)S(1)} %get-tuple-element.43.mid0_ref, f32[16,64,128]{2,1,0:T(8,128)S(1)} %copy-done.1, f32[16,64,128]{2,1,0:T(8,128)S(1)} %copy-done, ...), custom_call_target="tpu_custom_call" | custom-call | flops 13107200 | bytes 8921088 | tf_op jit(solution)/shard_map/pallas_call | solution.py:26
  31.9 0.0 collective-permute-done.9.ye_ref
  32.0 0.0 collective-permute-done.7.xe_ref
  32.0 0.9 %shard_map.93 = (f32[16,64,128]{2,1,0:T(8,128)S(1)}, f32[16,64,128]{2,1,0:T(8,128)S(1)}) custom-call(f32[16,64,128]{2,1,0:T(8,128)S(1)} %get-tuple-element.45.part_ref, f32[16,64,128]{2,1,0:T(8,128)S(1)} %get-tuple-element.44.mid_ref, f32[16,64,128]{2,1,0:T(8,128)S(1)} %copy-done, f32[16,64,128]{2,1,0:T(8,128)S(1)} %copy-done.2, ...), custom_call_target="tpu_custom_call" | custom-call | flops 805306368 | bytes 7749632 | tf_op jit(solution)/shard_map/pallas_call | solution.py:26
  32.9 17.8 %all_to_all.10.returned_ref = f32[16,64,128]{2,1,0:T(8,128)S(1)} all-to-all(f32[16,64,128]{2,1,0:T(8,128)S(1)} %get-tuple-element.52), channel_id=1, replica_groups={{20,2,22,12,6,10,4,8,24,14,0,28,16,26,18,30},{17,5,9,21,25,13,11,29,7,2..., dimensions={0} | all-to-all | bytes 1048576 | tf_op jit(solution)/shard_map/all_to_all | solution.py:91
  50.7 1.2 %shard_map.94 = (f32[512,128]{1,0:T(8,128)}, f32[16,64,128]{2,1,0:T(8,128)}) custom-call(bf16[512,1024]{1,0:T(8,128)(2,1)S(1)} %copy-done.4, f32[16,64,128]{2,1,0:T(8,128)S(1)} %all_to_all.10.returned_ref, f32[16,64,128]{2,1,0:T(8,128)S(1)} %get-tuple-element.53.next_ref), custom_call_target="tpu_custom_call" | custom-call | flops 268435456 | bytes 3932160 | tf_op jit(solution)/shard_map/pallas_call | solution.py:26
  (18 shorter events, 0.0 us)
Async XLA Ops:
  0.6 13.4 %copy-start = (f32[16,64,128]{2,1,0:T(8,128)S(1)}, f32[16,64,128]{2,1,0:T(8,128)}, u32[]{:S(2)}) copy-start(f32[16,64,128]{2,1,0:T(8,128)} %b_ref.9) | copy-start | bytes 1572868
  0.6 13.4 %copy-start.1 = (f32[16,64,128]{2,1,0:T(8,128)S(1)}, f32[16,64,128]{2,1,0:T(8,128)}, u32[]{:S(2)}) copy-start(f32[16,64,128]{2,1,0:T(8,128)} %p_ref.7) | copy-start | bytes 1572868
  1.9 12.1 %collective-permute-start = (f32[5,64,128]{2,1,0:T(8,128)S(1)}, f32[5,64,128]{2,1,0:T(8,128)S(1)}, u32[]{:S(2)}, u32[]{:S(2)}) collective-permute-start(f32[5,64,128]{2,1,0:T(8,128)S(1)} %get-tuple-element.34), channel_id=1, source_target_pairs={{0,8},{1,9},{2,10},{3,11},{4,12},{5,13},{6,14},{7,15},{8,0},{9,1},... | collective-permute-start | bytes 491528 | tf_op jit(solution)/shard_map/ppermute | solution.py:255
  5.0 9.0 %collective-permute-start.1 = (f32[5,64,128]{2,1,0:T(8,128)S(1)}, f32[5,64,128]{2,1,0:T(8,128)S(1)}, u32[]{:S(2)}, u32[]{:S(2)}) collective-permute-start(f32[5,64,128]{2,1,0:T(8,128)S(1)} %get-tuple-element.35), channel_id=1, source_target_pairs={{0,1},{1,0},{2,3},{3,2},{4,5},{5,4},{6,7},{7,6},{8,16},{9,17},{10,... | collective-permute-start | bytes 491528 | tf_op jit(solution)/shard_map/ppermute | solution.py:254
  6.2 19.7 %all-to-all-start = ((f32[16,65,1,128]{3,2,1,0:T(1,128)}), f32[16,65,1,128]{3,2,1,0:T(1,128)S(1)}, u32[]{:S(2)}, u32[]{:S(2)}) async-start(f32[16,65,1,128]{3,2,1,0:T(1,128)} %bitcast.2), calls=%async_computation | async-start | bytes 1064960 | tf_op jit(solution)/shard_map/all_to_all | solution.py:91
  14.0 0.7 %copy-start.6 = (f32[5,64,128]{2,1,0:T(8,128)}, f32[5,64,128]{2,1,0:T(8,128)S(1)}, u32[]{:S(2)}) copy-start(f32[5,64,128]{2,1,0:T(8,128)S(1)} %collective-permute-done.1.xo_ref) | copy-start | bytes 491524
  14.0 3.3 %copy-start.2 = (f32[16,64,128]{2,1,0:T(8,128)S(1)}, f32[16,64,128]{2,1,0:T(8,128)}, u32[]{:S(2)}) copy-start(f32[16,64,128]{2,1,0:T(8,128)} %kappa_ref.9) | copy-start | bytes 1572868
  14.0 3.3 %copy-start.5 = (f32[16,64,128]{2,1,0:T(8,128)S(1)}, f32[16,64,128]{2,1,0:T(8,128)}, u32[]{:S(2)}) copy-start(f32[16,64,128]{2,1,0:T(8,128)} %prev_ref.1) | copy-start | bytes 1572868
  14.7 5.5 %copy-start.3 = (bf16[512,1024]{1,0:T(8,128)(2,1)}, bf16[512,1024]{1,0:T(8,128)(2,1)S(1)}, u32[]{:S(2)}) copy-start(bf16[512,1024]{1,0:T(8,128)(2,1)S(1)} %get-tuple-element.36.map_ref) | copy-start | bytes 3145732
  14.7 5.5 %copy-start.7 = (f32[5,64,128]{2,1,0:T(8,128)S(1)}, f32[5,64,128]{2,1,0:T(8,128)}, u32[]{:S(2)}) copy-start(f32[5,64,128]{2,1,0:T(8,128)} %copy-done.6) | copy-start | bytes 491524
  14.7 2.0 %collective-permute-start.2 = (f32[16,64,128]{2,1,0:T(8,128)S(1)}, f32[16,64,128]{2,1,0:T(8,128)S(1)}, u32[]{:S(2)}, u32[]{:S(2)}) collective-permute-start(f32[16,64,128]{2,1,0:T(8,128)S(1)} %get-tuple-element.38), channel_id=1, source_target_pairs={{0,1},{1,0},{2,3},{3,2},{4,5},{5,4},{6,7},{7,6},{8,9},{9,8},{10,11... | collective-permute-start | bytes 1572872 | tf_op jit(solution)/shard_map/ppermute | solution.py:260
  14.7 2.7 %collective-permute-start.3 = (f32[16,64,128]{2,1,0:T(8,128)S(1)}, f32[16,64,128]{2,1,0:T(8,128)S(1)}, u32[]{:S(2)}, u32[]{:S(2)}) collective-permute-start(f32[16,64,128]{2,1,0:T(8,128)S(1)} %get-tuple-element.39), channel_id=1, source_target_pairs={{0,1},{1,0},{2,3},{3,2},{4,5},{5,4},{6,7},{7,6},{8,9},{9,8},{10,11... | collective-permute-start | bytes 1572872 | tf_op jit(solution)/shard_map/ppermute | solution.py:260
  15.2 5.0 %collective-permute-start.4 = (f32[5,16,128]{2,1,0:T(8,128)S(1)}, f32[5,16,128]{2,1,0:T(8,128)S(1)}, u32[]{:S(2)}, u32[]{:S(2)}) collective-permute-start(f32[5,16,128]{2,1,0:T(8,128)S(1)} %get-tuple-element.41), channel_id=1, source_target_pairs={{0,2},{1,3},{2,0},{3,1},{4,6},{5,7},{6,4},{7,5},{8,10},{9,11},{10,... | collective-permute-start | bytes 122888 | tf_op jit(solution)/shard_map/ppermute | solution.py:255
  16.6 3.6 %collective-permute-start.5 = (f32[5,16,128]{2,1,0:T(8,128)S(1)}, f32[5,16,128]{2,1,0:T(8,128)S(1)}, u32[]{:S(2)}, u32[]{:S(2)}) collective-permute-start(f32[5,16,128]{2,1,0:T(8,128)S(1)} %get-tuple-element.42), channel_id=1, source_target_pairs={{0,1},{1,0},{2,4},{3,5},{4,2},{5,3},{6,7},{7,6},{8,9},{9,8},{10,12... | collective-permute-start | bytes 122888 | tf_op jit(solution)/shard_map/ppermute | solution.py:254
  26.7 2.2 %collective-permute-start.6 = (f32[16,64,128]{2,1,0:T(8,128)S(1)}, f32[16,64,128]{2,1,0:T(8,128)S(1)}, u32[]{:S(2)}, u32[]{:S(2)}) collective-permute-start(f32[16,64,128]{2,1,0:T(8,128)S(1)} %get-tuple-element.44.mid_ref), channel_id=1, source_target_pairs={{0,1},{1,0},{2,3},{3,2},{4,5},{5,4},{6,7},{7,6},{8,9},{9,8},{10,11... | collective-permute-start | bytes 1572872 | tf_op jit(solution)/shard_map/ppermute | solution.py:260
  26.8 5.2 %collective-permute-start.7 = (f32[3,64,128]{2,1,0:T(8,128)S(1)}, f32[3,64,128]{2,1,0:T(8,128)S(1)}, u32[]{:S(2)}, u32[]{:S(2)}) collective-permute-start(f32[3,64,128]{2,1,0:T(8,128)S(1)} %get-tuple-element.48), channel_id=1, source_target_pairs={{0,8},{1,9},{2,10},{3,11},{4,12},{5,13},{6,14},{7,15},{8,0},{9,1},... | collective-permute-start | bytes 294920 | tf_op jit(solution)/shard_map/ppermute | solution.py:255
  27.2 4.8 %collective-permute-start.8 = (f32[3,64,128]{2,1,0:T(8,128)S(1)}, f32[3,64,128]{2,1,0:T(8,128)S(1)}, u32[]{:S(2)}, u32[]{:S(2)}) collective-permute-start(f32[3,64,128]{2,1,0:T(8,128)S(1)} %get-tuple-element.49), channel_id=1, source_target_pairs={{0,1},{1,0},{2,3},{3,2},{4,5},{5,4},{6,7},{7,6},{8,16},{9,17},{10,... | collective-permute-start | bytes 294920 | tf_op jit(solution)/shard_map/ppermute | solution.py:254
  27.4 4.6 %collective-permute-start.9 = (f32[3,16,128]{2,1,0:T(8,128)S(1)}, f32[3,16,128]{2,1,0:T(8,128)S(1)}, u32[]{:S(2)}, u32[]{:S(2)}) collective-permute-start(f32[3,16,128]{2,1,0:T(8,128)S(1)} %get-tuple-element.50), channel_id=1, source_target_pairs={{0,2},{1,3},{2,0},{3,1},{4,6},{5,7},{6,4},{7,5},{8,10},{9,11},{10,... | collective-permute-start | bytes 73736 | tf_op jit(solution)/shard_map/ppermute | solution.py:255
  28.9 3.1 %collective-permute-start.10 = (f32[3,16,128]{2,1,0:T(8,128)S(1)}, f32[3,16,128]{2,1,0:T(8,128)S(1)}, u32[]{:S(2)}, u32[]{:S(2)}) collective-permute-start(f32[3,16,128]{2,1,0:T(8,128)S(1)} %get-tuple-element.51), channel_id=1, source_target_pairs={{0,1},{1,0},{2,4},{3,5},{4,2},{5,3},{6,7},{7,6},{8,9},{9,8},{10,12... | collective-permute-start | bytes 73736 | tf_op jit(solution)/shard_map/ppermute | solution.py:254
  32.0 18.7 %copy-start.4 = (bf16[512,1024]{1,0:T(8,128)(2,1)S(1)}, bf16[512,1024]{1,0:T(8,128)(2,1)}, u32[]{:S(2)}) copy-start(bf16[512,1024]{1,0:T(8,128)(2,1)} %copy-done.3) | copy-start | bytes 3145732

commit v7 on v6

--- a/solution.py
+++ b/solution.py
@@ -289,7 +289,7 @@
     return near if d is None else near + d
 
 
-def inner(v_ref, b_ref, vo_ref, bo_ref, vpad_ref, bpad_ref, fx_ref, fy_ref, finish):
+def inner(v_ref, b_ref, vo_ref, bo_ref, bz_ref, first, vpad_ref, bpad_ref, fx_ref, fy_ref, finish):
     cx, cy, cz = v_ref.shape
     lane = lax.broadcasted_iota(jnp.int32, (cy, cz), 1)
     last = lax.broadcasted_iota(jnp.int32, (cy, cz), 0) == cy - 1
@@ -318,7 +318,9 @@
         total += diff(fy, f[1], f[2], f[0])
         u, h = v_ref[i], jnp.where(near, vo_ref[i], 0.0)
         bu, bh = b_ref[i], jnp.where(near, bo_ref[i], 0.0)
-        fu = diff(ahead(u, h, lane, 1), u, ahead(u, h, lane, 2), ahead(u, h, lane, -1)) * (bu + ahead(bu, bh, lane, 1))
+        if first:
+            bz_ref[i] = bu + ahead(bu, bh, lane, 1)
+        fu = diff(ahead(u, h, lane, 1), u, ahead(u, h, lane, 2), ahead(u, h, lane, -1)) * bz_ref[i]
         fh = diff(ahead(h, u, lane, 1), h, ahead(h, u, lane, 2), ahead(h, u, lane, -1)) * (bh + ahead(bh, bu, lane, 1))
         total += diff(fu, ahead(fu, fh, lane, -1), ahead(fu, fh, lane, 1), ahead(fu, fh, lane, -2))
         finish(i, u, total)
@@ -351,11 +353,11 @@
             flat_out[to, :] = flat_out[to, :] + y_row(kappa_ref, j + k * step) * (lap_scale * term)
 
 
-def first_inner_kernel(p_ref, b_ref, prev_ref, kappa_ref, po_ref, bo_ref, out_ref, *scratch):
+def first_inner_kernel(p_ref, b_ref, prev_ref, kappa_ref, po_ref, bo_ref, out_ref, bz_ref, *scratch):
     def finish(i, u, total):
         out_ref[i] = 2.0 * u - prev_ref[i] + kappa_ref[i] * (lap_scale * total)
 
-    inner(p_ref, b_ref, po_ref, bo_ref, *scratch, finish)
+    inner(p_ref, b_ref, po_ref, bo_ref, bz_ref, True, *scratch, finish)
 
 
 def first_edge_kernel(part_ref, p_ref, b_ref, kappa_ref, bx_ref, xe_ref, xo_ref, ye_ref, yo_ref, mid0_ref, by_ref):
@@ -371,7 +373,7 @@
 
 
 def second_inner_kernel(
-    out_orders, back_orders, cap, mid_ref, mid0_ref, p_ref, b_ref, kappa_ref, mo_ref, bo_ref, got_ref, out_ref, map_ref, *scratch
+    out_orders, back_orders, cap, mid_ref, mid0_ref, p_ref, b_ref, kappa_ref, mo_ref, bo_ref, bz_ref, got_ref, out_ref, map_ref, *scratch
 ):
     cx, cy, _ = p_ref.shape
     lanes = got_ref.shape[1]
@@ -379,7 +381,7 @@
     def finish(i, u, total):
         out_ref[i] = 3.0 * u - mid0_ref[i] - p_ref[i] + kappa_ref[i] * (lap_scale * total)
 
-    inner(mid_ref, b_ref, mo_ref, bo_ref, *scratch, finish)
+    inner(mid_ref, b_ref, mo_ref, bo_ref, bz_ref, False, *scratch, finish)
     blocks = [of_core(*(o.index(b[k]) for o, b in zip(out_orders, back_orders))) for k in range(len(out_orders[0]))]
     for at, row in enumerate(column_rows(got_ref, cap, blocks)):
         column = as_column(row).astype(jnp.int32)
@@ -447,9 +449,9 @@
         pltpu.VMEM((cx, cy, cz), f32),
         pltpu.VMEM((2, cy + 2 * tile, cz), f32),
     ]
-    (part,) = run(
+    part, bz = run(
         first_inner_kernel,
-        [cells],
+        [cells, cells],
         pressure,
         buoyancy,
         pressure_prev,
@@ -484,6 +486,7 @@
         kappa,
         other_mid,
         other_b,
+        bz,
         got,
         flops=100 * cx * cy * cz,
         scratch=scratch,

time: 52.2 us -> 53 us (1.015)
  local copies, waits for them, and re-layouts: 0.32 us -> 2.15 us
  waiting for transfers between devices: 6.31 us -> 5.77 us
    unnamed x16 -> x20, local copies, waits for them, and re-layouts: 0.32 us -> 2.15 us
    all_to_all x1, waiting for transfers between devices: 5.41 us -> 4.61 us  [exchange_rows(): lax.all_to_all(x, ('gx', 'gy', 'blk'), split_axis=0, concat_axis=0, tiled...]
  transfers between devices with their start and end apart: 12 -> 12, of which waited for: 3 -> 4; matrix products, arithmetic and copies ran while one was open for 0% -> 0% of each run, Pallas kernels for 14% -> 14%
where the time goes in v7:
time: 53 us; the launch traced here: 52.6 us
  blocking collectives  17.5 us (33%)
  starting transfers between devices  15.1 us (28%)
  Pallas kernels  11.3 us (21%)
  waiting for transfers between devices  5.77 us (11%)
  local copies, waits for them, and re-layouts  2.15 us (4%)
  between operations  0.81 us (2%)
    all_to_all x1, blocking collectives, exchange_rows(): lax.all_to_all(x, ('gx', 'gy', 'blk'), split_axis=0, concat_axis=0, tiled...  17.5 us
    pallas_call x9, Pallas kernels, run(): pl.pallas_call(kernel, out_shape=outs, in_specs=[pl.BlockSpec(memory_spac...  11.3 us
    all_to_all x1, starting transfers between devices, exchange_rows(): lax.all_to_all(x, ('gx', 'gy', 'blk'), split_axis=0, concat_axis=0, tiled...  7.8 us
    ppermute x4, starting transfers between devices, exchange(): return (lax.ppermute(to_even, axes, swap_pairs(sizes, axis, 0)), to_odd)  6.46 us
    all_to_all x1, waiting for transfers between devices, exchange_rows(): lax.all_to_all(x, ('gx', 'gy', 'blk'), split_axis=0, concat_axis=0, tiled...  4.61 us
    unnamed x20, local copies, waits for them, and re-layouts  2.15 us
  transfers between devices with their start and end apart: 12, of which 4 were waited for; matrix products, arithmetic and copies ran while one was open for 0% of the time, Pallas kernels for 14%

profile of v7, /device:TPU:0, one launch (start us, length us, event | category | flops | bytes accessed | tf_op | source)
XLA Modules:
  0.0 52.6 jit_solution(11623016882343520275)
XLA Ops:
  0.7 1.2 %shard_map.86 = (s32[1,512]{1,0:T(1,128)S(1)}, f32[1,512]{1,0:T(1,128)S(1)}, f32[16,128]{1,0:T(8,128)S(1)}, f32[512,128]{1,0:T(8,128)S(1)}, f32[5,64,128]{2,1,0:T(8,128)S(1)}, /*index=5*/f32[5,64,128]{2,1,0:T(8,128)S(1)}) custom-call(s32[1,512]{1,0:T(1,128)} %bitcast.6, s32[1,512]{1,0:T(1,128)} %bitcast.7, f32[512,128]{1,0:T(8,128)} %accel_hbm.1, ...), custom_call_target="tpu_custom_call" | custom-call | flops 8388608 | bytes 1916928 | tf_op jit(solution)/shard_map/pallas_call | solution.py:26
  1.9 3.1 %collective-permute-start = (f32[5,64,128]{2,1,0:T(8,128)S(1)}, f32[5,64,128]{2,1,0:T(8,128)S(1)}, u32[]{:S(2)}, u32[]{:S(2)}) collective-permute-start(f32[5,64,128]{2,1,0:T(8,128)S(1)} %get-tuple-element.36), channel_id=1, source_target_pairs={{0,8},{1,9},{2,10},{3,11},{4,12},{5,13},{6,14},{7,15},{8,0},{9,1},... | collective-permute-start | bytes 491528 | tf_op jit(solution)/shard_map/ppermute | solution.py:255
  5.0 0.0 collective-permute-start.1
  5.0 1.2 %shard_map.87 = (f32[1040,128]{1,0:T(8,128)}, f32[1,512]{1,0:T(1,128)S(1)}) custom-call(s32[1,512]{1,0:T(1,128)S(1)} %get-tuple-element.31.place_ref, f32[1,512]{1,0:T(1,128)S(1)} %get-tuple-element.32.back_ref, f32[16,128]{1,0:T(8,128)S(1)} %get-tuple-element.33.columns_ref, f32[512,128]{1,0:T(8,128)S(1)} %get-tuple-element.34.accel_ref), custom_call_target="tpu_custom_call" | custom-call | flops 272629760 | bytes 808960 | tf_op jit(solution)/shard_map/pallas_call | solution.py:26
  6.2 7.8 %all-to-all-start = ((f32[16,65,1,128]{3,2,1,0:T(1,128)}), f32[16,65,1,128]{3,2,1,0:T(1,128)S(1)}, u32[]{:S(2)}, u32[]{:S(2)}) async-start(f32[16,65,1,128]{3,2,1,0:T(1,128)} %bitcast.2), calls=%async_computation | async-start | bytes 1064960 | tf_op jit(solution)/shard_map/all_to_all | solution.py:91
  14.0 0.0 collective-permute-done.1.xo_ref
  14.0 0.0 copy-start.8
  14.0 0.0 copy-start.1
  14.0 0.0 copy-start.7
  14.1 0.3 shard_map.88
  14.4 0.3 copy-done.8
  14.7 0.5 collective-permute-start.3
  15.2 1.5 %collective-permute-start.4 = (f32[5,16,128]{2,1,0:T(8,128)S(1)}, f32[5,16,128]{2,1,0:T(8,128)S(1)}, u32[]{:S(2)}, u32[]{:S(2)}) collective-permute-start(f32[5,16,128]{2,1,0:T(8,128)S(1)} %get-tuple-element.44), channel_id=1, source_target_pairs={{0,2},{1,3},{2,0},{3,1},{4,6},{5,7},{6,4},{7,5},{8,10},{9,11},{10,... | collective-permute-start | bytes 122888 | tf_op jit(solution)/shard_map/ppermute | solution.py:255
  16.6 0.7 %collective-permute-done.3.bo_ref = f32[16,64,128]{2,1,0:T(8,128)S(1)} collective-permute-done((f32[16,64,128]{2,1,0:T(8,128)S(1)}, f32[16,64,128]{2,1,0:T(8,128)S(1)}, u32[]{:S(2)}, u32[]{:S(2)}) %collective-permute-start.3) | collective-permute-done | bytes 524320 | tf_op jit(solution)/shard_map/ppermute | solution.py:260
  17.3 2.7 %shard_map.89 = (f32[16,64,128]{2,1,0:T(8,128)S(1)}, f32[16,64,128]{2,1,0:T(8,128)S(1)}) custom-call(f32[16,64,128]{2,1,0:T(8,128)S(1)} %copy-done.2, f32[16,64,128]{2,1,0:T(8,128)S(1)} %copy-done, f32[16,64,128]{2,1,0:T(8,128)S(1)} %copy-done.7, f32[16,64,128]{2,1,0:T(8,128)S(1)} %copy-done.1, f32[16,64,128]{2,1,0:T(8,128)S(1)} %collective-permute-done.2.po_ref, ...), custom_call_target="tpu_custom_call" | custom-call | flops 13107200 | bytes 4194304 | tf_op jit(solution)/shard_map/pallas_call | solution.py:26
  20.0 0.2 collective-permute-done.4.ye_ref
  20.2 0.3 shard_map.90
  20.5 0.0 copy-start.5
  20.5 0.8 %copy-done.5 = f32[16,64,128]{2,1,0:T(8,128)} copy-done((f32[16,64,128]{2,1,0:T(8,128)}, f32[16,64,128]{2,1,0:T(8,128)S(1)}, u32[]{:S(2)}) %copy-start.5) | copy-done | bytes 524312
  21.3 4.6 %all-to-all-done = f32[16,65,1,128]{3,2,1,0:T(1,128)S(1)} async-done(((f32[16,65,1,128]{3,2,1,0:T(1,128)}), f32[16,65,1,128]{3,2,1,0:T(1,128)S(1)}, u32[]{:S(2)}, u32[]{:S(2)}) %all-to-all-start) | async-done | bytes 532512 | tf_op jit(solution)/shard_map/all_to_all | solution.py:91
  25.9 1.0 %copy-done.6 = f32[16,64,128]{2,1,0:T(8,128)S(1)} copy-done((f32[16,64,128]{2,1,0:T(8,128)S(1)}, f32[16,64,128]{2,1,0:T(8,128)}, u32[]{:S(2)}) %copy-start.6) | copy-done | bytes 524312
  26.9 0.8 %shard_map.91 = (f32[16,64,128]{2,1,0:T(8,128)S(1)}, f32[3,64,128]{2,1,0:T(8,128)S(1)}, f32[3,64,128]{2,1,0:T(8,128)S(1)}, f32[3,16,128]{2,1,0:T(8,128)S(1)}, f32[3,16,128]{2,1,0:T(8,128)S(1)}) custom-call(f32[1040,128]{1,0:T(8,128)S(1)} %bitcast.4, f32[16,64,128]{2,1,0:T(8,128)S(1)} %copy-done.6, f32[16,64,128]{2,1,0:T(8,128)S(1)} %copy-done.1), custom_call_target="tpu_custom_call" | custom-call | flops 805306368 | bytes 2351104 | tf_op jit(solution)/shard_map/pallas_call | solution.py:26
  27.7 0.1 collective-permute-start.6
  27.8 0.4 collective-permute-start.7
  28.3 0.2 collective-permute-start.8
  28.4 1.5 %collective-permute-start.9 = (f32[3,16,128]{2,1,0:T(8,128)S(1)}, f32[3,16,128]{2,1,0:T(8,128)S(1)}, u32[]{:S(2)}, u32[]{:S(2)}) collective-permute-start(f32[3,16,128]{2,1,0:T(8,128)S(1)} %get-tuple-element.54), channel_id=1, source_target_pairs={{0,2},{1,3},{2,0},{3,1},{4,6},{5,7},{6,4},{7,5},{8,10},{9,11},{10,... | collective-permute-start | bytes 73736 | tf_op jit(solution)/shard_map/ppermute | solution.py:255
  29.9 0.1 collective-permute-start.10
  30.0 2.8 %shard_map.92 = (f32[16,64,128]{2,1,0:T(8,128)S(1)}, bf16[1024,1024]{1,0:T(8,128)(2,1)S(1)}) custom-call(f32[16,64,128]{2,1,0:T(8,128)S(1)} %get-tuple-element.47.mid_ref, f32[16,64,128]{2,1,0:T(8,128)S(1)} %copy-done.6, f32[16,64,128]{2,1,0:T(8,128)S(1)} %copy-done.2, f32[16,64,128]{2,1,0:T(8,128)S(1)} %copy-done, f32[16,64,128]{2,1,0:T(8,128)S(1)} %copy-done.1, ...), custom_call_target="tpu_custom_call" | custom-call | flops 13107200 | bytes 9445376 | tf_op jit(solution)/shard_map/pallas_call | solution.py:26
  32.8 0.3 collective-permute-done.7.xe_ref
  33.0 0.9 %shard_map.93 = (f32[16,64,128]{2,1,0:T(8,128)S(1)}, f32[16,64,128]{2,1,0:T(8,128)S(1)}) custom-call(f32[16,64,128]{2,1,0:T(8,128)S(1)} %get-tuple-element.49.part_ref, f32[16,64,128]{2,1,0:T(8,128)S(1)} %get-tuple-element.47.mid_ref, f32[16,64,128]{2,1,0:T(8,128)S(1)} %copy-done, f32[16,64,128]{2,1,0:T(8,128)S(1)} %copy-done.1, ...), custom_call_target="tpu_custom_call" | custom-call | flops 805306368 | bytes 7749632 | tf_op jit(solution)/shard_map/pallas_call | solution.py:26
  33.9 17.5 %all_to_all.10.returned_ref = f32[16,64,128]{2,1,0:T(8,128)S(1)} all-to-all(f32[16,64,128]{2,1,0:T(8,128)S(1)} %get-tuple-element.56), channel_id=1, replica_groups={{20,2,22,12,6,10,4,8,24,14,0,28,16,26,18,30},{17,5,9,21,25,13,11,29,7,2..., dimensions={0} | all-to-all | bytes 1048576 | tf_op jit(solution)/shard_map/all_to_all | solution.py:91
  51.5 1.2 %shard_map.94 = (f32[512,128]{1,0:T(8,128)}, f32[16,64,128]{2,1,0:T(8,128)}) custom-call(bf16[512,1024]{1,0:T(8,128)(2,1)S(1)} %copy-done.4, f32[16,64,128]{2,1,0:T(8,128)S(1)} %all_to_all.10.returned_ref, f32[16,64,128]{2,1,0:T(8,128)S(1)} %get-tuple-element.57.next_ref), custom_call_target="tpu_custom_call" | custom-call | flops 268435456 | bytes 3932160 | tf_op jit(solution)/shard_map/pallas_call | solution.py:26
  (22 shorter events, 0.0 us)
Async XLA Ops:
  0.6 13.4 %copy-start = (f32[16,64,128]{2,1,0:T(8,128)S(1)}, f32[16,64,128]{2,1,0:T(8,128)}, u32[]{:S(2)}) copy-start(f32[16,64,128]{2,1,0:T(8,128)} %b_ref.9) | copy-start | bytes 1572868
  0.6 13.4 %copy-start.2 = (f32[16,64,128]{2,1,0:T(8,128)S(1)}, f32[16,64,128]{2,1,0:T(8,128)}, u32[]{:S(2)}) copy-start(f32[16,64,128]{2,1,0:T(8,128)} %p_ref.7) | copy-start | bytes 1572868
  1.9 12.1 %collective-permute-start = (f32[5,64,128]{2,1,0:T(8,128)S(1)}, f32[5,64,128]{2,1,0:T(8,128)S(1)}, u32[]{:S(2)}, u32[]{:S(2)}) collective-permute-start(f32[5,64,128]{2,1,0:T(8,128)S(1)} %get-tuple-element.36), channel_id=1, source_target_pairs={{0,8},{1,9},{2,10},{3,11},{4,12},{5,13},{6,14},{7,15},{8,0},{9,1},... | collective-permute-start | bytes 491528 | tf_op jit(solution)/shard_map/ppermute | solution.py:255
  5.0 9.0 %collective-permute-start.1 = (f32[5,64,128]{2,1,0:T(8,128)S(1)}, f32[5,64,128]{2,1,0:T(8,128)S(1)}, u32[]{:S(2)}, u32[]{:S(2)}) collective-permute-start(f32[5,64,128]{2,1,0:T(8,128)S(1)} %get-tuple-element.37), channel_id=1, source_target_pairs={{0,1},{1,0},{2,3},{3,2},{4,5},{5,4},{6,7},{7,6},{8,16},{9,17},{10,... | collective-permute-start | bytes 491528 | tf_op jit(solution)/shard_map/ppermute | solution.py:254
  6.2 19.7 %all-to-all-start = ((f32[16,65,1,128]{3,2,1,0:T(1,128)}), f32[16,65,1,128]{3,2,1,0:T(1,128)S(1)}, u32[]{:S(2)}, u32[]{:S(2)}) async-start(f32[16,65,1,128]{3,2,1,0:T(1,128)} %bitcast.2), calls=%async_computation | async-start | bytes 1064960 | tf_op jit(solution)/shard_map/all_to_all | solution.py:91
  14.0 0.7 %copy-start.8 = (f32[5,64,128]{2,1,0:T(8,128)}, f32[5,64,128]{2,1,0:T(8,128)S(1)}, u32[]{:S(2)}) copy-start(f32[5,64,128]{2,1,0:T(8,128)S(1)} %collective-permute-done.1.xo_ref) | copy-start | bytes 491524
  14.0 3.3 %copy-start.1 = (f32[16,64,128]{2,1,0:T(8,128)S(1)}, f32[16,64,128]{2,1,0:T(8,128)}, u32[]{:S(2)}) copy-start(f32[16,64,128]{2,1,0:T(8,128)} %kappa_ref.9) | copy-start | bytes 1572868
  14.0 3.3 %copy-start.7 = (f32[16,64,128]{2,1,0:T(8,128)S(1)}, f32[16,64,128]{2,1,0:T(8,128)}, u32[]{:S(2)}) copy-start(f32[16,64,128]{2,1,0:T(8,128)} %prev_ref.1) | copy-start | bytes 1572868
  14.7 5.5 %copy-start.3 = (bf16[512,1024]{1,0:T(8,128)(2,1)}, bf16[512,1024]{1,0:T(8,128)(2,1)S(1)}, u32[]{:S(2)}) copy-start(bf16[512,1024]{1,0:T(8,128)(2,1)S(1)} %get-tuple-element.38.map_ref) | copy-start | bytes 3145732
  14.7 5.5 %copy-start.9 = (f32[5,64,128]{2,1,0:T(8,128)S(1)}, f32[5,64,128]{2,1,0:T(8,128)}, u32[]{:S(2)}) copy-start(f32[5,64,128]{2,1,0:T(8,128)} %copy-done.8) | copy-start | bytes 491524
  14.7 2.0 %collective-permute-start.2 = (f32[16,64,128]{2,1,0:T(8,128)S(1)}, f32[16,64,128]{2,1,0:T(8,128)S(1)}, u32[]{:S(2)}, u32[]{:S(2)}) collective-permute-start(f32[16,64,128]{2,1,0:T(8,128)S(1)} %get-tuple-element.40), channel_id=1, source_target_pairs={{0,1},{1,0},{2,3},{3,2},{4,5},{5,4},{6,7},{7,6},{8,9},{9,8},{10,11... | collective-permute-start | bytes 1572872 | tf_op jit(solution)/shard_map/ppermute | solution.py:260
  14.7 2.7 %collective-permute-start.3 = (f32[16,64,128]{2,1,0:T(8,128)S(1)}, f32[16,64,128]{2,1,0:T(8,128)S(1)}, u32[]{:S(2)}, u32[]{:S(2)}) collective-permute-start(f32[16,64,128]{2,1,0:T(8,128)S(1)} %get-tuple-element.41), channel_id=1, source_target_pairs={{0,1},{1,0},{2,3},{3,2},{4,5},{5,4},{6,7},{7,6},{8,9},{9,8},{10,11... | collective-permute-start | bytes 1572872 | tf_op jit(solution)/shard_map/ppermute | solution.py:260
  15.2 5.0 %collective-permute-start.4 = (f32[5,16,128]{2,1,0:T(8,128)S(1)}, f32[5,16,128]{2,1,0:T(8,128)S(1)}, u32[]{:S(2)}, u32[]{:S(2)}) collective-permute-start(f32[5,16,128]{2,1,0:T(8,128)S(1)} %get-tuple-element.44), channel_id=1, source_target_pairs={{0,2},{1,3},{2,0},{3,1},{4,6},{5,7},{6,4},{7,5},{8,10},{9,11},{10,... | collective-permute-start | bytes 122888 | tf_op jit(solution)/shard_map/ppermute | solution.py:255
  16.6 3.6 %collective-permute-start.5 = (f32[5,16,128]{2,1,0:T(8,128)S(1)}, f32[5,16,128]{2,1,0:T(8,128)S(1)}, u32[]{:S(2)}, u32[]{:S(2)}) collective-permute-start(f32[5,16,128]{2,1,0:T(8,128)S(1)} %get-tuple-element.45), channel_id=1, source_target_pairs={{0,1},{1,0},{2,4},{3,5},{4,2},{5,3},{6,7},{7,6},{8,9},{9,8},{10,12... | collective-permute-start | bytes 122888 | tf_op jit(solution)/shard_map/ppermute | solution.py:254
  20.5 0.8 %copy-start.5 = (f32[16,64,128]{2,1,0:T(8,128)}, f32[16,64,128]{2,1,0:T(8,128)S(1)}, u32[]{:S(2)}) copy-start(f32[16,64,128]{2,1,0:T(8,128)S(1)} %get-tuple-element.46.mid0_ref) | copy-start | bytes 1572868
  25.9 1.0 %copy-start.6 = (f32[16,64,128]{2,1,0:T(8,128)S(1)}, f32[16,64,128]{2,1,0:T(8,128)}, u32[]{:S(2)}) copy-start(f32[16,64,128]{2,1,0:T(8,128)} %copy-done.5) | copy-start | bytes 1572868
  27.7 2.2 %collective-permute-start.6 = (f32[16,64,128]{2,1,0:T(8,128)S(1)}, f32[16,64,128]{2,1,0:T(8,128)S(1)}, u32[]{:S(2)}, u32[]{:S(2)}) collective-permute-start(f32[16,64,128]{2,1,0:T(8,128)S(1)} %get-tuple-element.47.mid_ref), channel_id=1, source_target_pairs={{0,1},{1,0},{2,3},{3,2},{4,5},{5,4},{6,7},{7,6},{8,9},{9,8},{10,11... | collective-permute-start | bytes 1572872 | tf_op jit(solution)/shard_map/ppermute | solution.py:260
  27.8 5.2 %collective-permute-start.7 = (f32[3,64,128]{2,1,0:T(8,128)S(1)}, f32[3,64,128]{2,1,0:T(8,128)S(1)}, u32[]{:S(2)}, u32[]{:S(2)}) collective-permute-start(f32[3,64,128]{2,1,0:T(8,128)S(1)} %get-tuple-element.52), channel_id=1, source_target_pairs={{0,8},{1,9},{2,10},{3,11},{4,12},{5,13},{6,14},{7,15},{8,0},{9,1},... | collective-permute-start | bytes 294920 | tf_op jit(solution)/shard_map/ppermute | solution.py:255
  28.3 4.8 %collective-permute-start.8 = (f32[3,64,128]{2,1,0:T(8,128)S(1)}, f32[3,64,128]{2,1,0:T(8,128)S(1)}, u32[]{:S(2)}, u32[]{:S(2)}) collective-permute-start(f32[3,64,128]{2,1,0:T(8,128)S(1)} %get-tuple-element.53), channel_id=1, source_target_pairs={{0,1},{1,0},{2,3},{3,2},{4,5},{5,4},{6,7},{7,6},{8,16},{9,17},{10,... | collective-permute-start | bytes 294920 | tf_op jit(solution)/shard_map/ppermute | solution.py:254
  28.4 4.3 %collective-permute-start.9 = (f32[3,16,128]{2,1,0:T(8,128)S(1)}, f32[3,16,128]{2,1,0:T(8,128)S(1)}, u32[]{:S(2)}, u32[]{:S(2)}) collective-permute-start(f32[3,16,128]{2,1,0:T(8,128)S(1)} %get-tuple-element.54), channel_id=1, source_target_pairs={{0,2},{1,3},{2,0},{3,1},{4,6},{5,7},{6,4},{7,5},{8,10},{9,11},{10,... | collective-permute-start | bytes 73736 | tf_op jit(solution)/shard_map/ppermute | solution.py:255
  29.9 2.9 %collective-permute-start.10 = (f32[3,16,128]{2,1,0:T(8,128)S(1)}, f32[3,16,128]{2,1,0:T(8,128)S(1)}, u32[]{:S(2)}, u32[]{:S(2)}) collective-permute-start(f32[3,16,128]{2,1,0:T(8,128)S(1)} %get-tuple-element.55), channel_id=1, source_target_pairs={{0,1},{1,0},{2,4},{3,5},{4,2},{5,3},{6,7},{7,6},{8,9},{9,8},{10,12... | collective-permute-start | bytes 73736 | tf_op jit(solution)/shard_map/ppermute | solution.py:254
  33.0 18.4 %copy-start.4 = (bf16[512,1024]{1,0:T(8,128)(2,1)S(1)}, bf16[512,1024]{1,0:T(8,128)(2,1)}, u32[]{:S(2)}) copy-start(bf16[512,1024]{1,0:T(8,128)(2,1)} %copy-done.3) | copy-start | bytes 3145732

commit v8 on v7

--- a/solution.py
+++ b/solution.py
@@ -26,7 +26,9 @@
     return pl.pallas_call(
         kernel,
         out_shape=outs,
-        in_specs=[pl.BlockSpec(memory_space=in_space)] * len(args),
+        in_specs=[
+            pl.BlockSpec(memory_space=m) for m in (in_space if isinstance(in_space, list) else [in_space] * len(args))
+        ],
         out_specs=[
             pl.BlockSpec(memory_space=m) for m in (out_space if isinstance(out_space, list) else [out_space] * len(outs))
         ],
@@ -373,12 +375,16 @@
 
 
 def second_inner_kernel(
-    out_orders, back_orders, cap, mid_ref, mid0_ref, p_ref, b_ref, kappa_ref, mo_ref, bo_ref, bz_ref, got_ref, out_ref, map_ref, *scratch
+    out_orders, back_orders, cap, mid_ref, mid0_ref, p_hbm, b_ref, kappa_ref, mo_ref, bo_ref, bz_ref, got_ref, out_ref, map_ref, p_ref, sem, *scratch
 ):
+    copy = pltpu.make_async_copy(p_hbm, p_ref, sem)
+    copy.start()
     cx, cy, _ = p_ref.shape
     lanes = got_ref.shape[1]
 
     def finish(i, u, total):
+        if i == 0:
+            copy.wait()
         out_ref[i] = 3.0 * u - mid0_ref[i] - p_ref[i] + kappa_ref[i] * (lap_scale * total)
 
     inner(mid_ref, b_ref, mo_ref, bo_ref, bz_ref, False, *scratch, finish)
@@ -481,7 +487,7 @@
         [cells, shaped(slots, cx * cy, dtype=bf16)],
         mid,
         mid0,
-        pressure,
+        in_hbm[3],
         buoyancy,
         kappa,
         other_mid,
@@ -489,7 +495,8 @@
         bz,
         got,
         flops=100 * cx * cy * cz,
-        scratch=scratch,
+        in_space=[pltpu.VMEM] * 2 + [pl.ANY] + [pltpu.VMEM] * 6,
+        scratch=[pltpu.VMEM((cx, cy, cz), f32), pltpu.SemaphoreType.DMA] + scratch,
     )
     pressure_next, picked = run(
         second_edge_kernel,

time: 53 us -> 53.9 us (1.017)
  Pallas kernels: 11.3 us -> 12.2 us
    pallas_call x9, Pallas kernels: 11.3 us -> 12.2 us  [run(): pl.pallas_call(kernel, out_shape=outs, in_specs=[pl.BlockSpec(memory_spac...]
  transfers between devices with their start and end apart: 12 -> 12, of which waited for: 4 -> 3; matrix products, arithmetic and copies ran while one was open for 0% -> 0% of each run, Pallas kernels for 14% -> 15%
where the time goes in v8:
time: 53.9 us; the launch traced here: 53.5 us
  blocking collectives  17.8 us (33%)
  starting transfers between devices  15.1 us (28%)
  Pallas kernels  12.2 us (23%)
  waiting for transfers between devices  5.52 us (10%)
  local copies, waits for them, and re-layouts  2.16 us (4%)
  between operations  0.83 us (2%)
    all_to_all x1, blocking collectives, exchange_rows(): lax.all_to_all(x, ('gx', 'gy', 'blk'), split_axis=0, concat_axis=0, tiled...  17.8 us
    pallas_call x9, Pallas kernels, run(): pl.pallas_call(kernel, out_shape=outs, in_specs=[pl.BlockSpec(memory_spac...  12.2 us
    all_to_all x1, starting transfers between devices, exchange_rows(): lax.all_to_all(x, ('gx', 'gy', 'blk'), split_axis=0, concat_axis=0, tiled...  7.8 us
    ppermute x4, starting transfers between devices, exchange(): return (lax.ppermute(to_even, axes, swap_pairs(sizes, axis, 0)), to_odd)  6.46 us
    all_to_all x1, waiting for transfers between devices, exchange_rows(): lax.all_to_all(x, ('gx', 'gy', 'blk'), split_axis=0, concat_axis=0, tiled...  4.62 us
    unnamed x20, local copies, waits for them, and re-layouts  2.16 us
  transfers between devices with their start and end apart: 12, of which 3 were waited for; matrix products, arithmetic and copies ran while one was open for 0% of the time, Pallas kernels for 15%

profile of v8, /device:TPU:0, one launch (start us, length us, event | category | flops | bytes accessed | tf_op | source)
XLA Modules:
  0.0 53.5 jit_solution(9439174736251397461)
XLA Ops:
  0.6 0.0 copy-start.2
  0.7 1.2 %shard_map.86 = (s32[1,512]{1,0:T(1,128)S(1)}, f32[1,512]{1,0:T(1,128)S(1)}, f32[16,128]{1,0:T(8,128)S(1)}, f32[512,128]{1,0:T(8,128)S(1)}, f32[5,64,128]{2,1,0:T(8,128)S(1)}, /*index=5*/f32[5,64,128]{2,1,0:T(8,128)S(1)}) custom-call(s32[1,512]{1,0:T(1,128)} %bitcast.6, s32[1,512]{1,0:T(1,128)} %bitcast.7, f32[512,128]{1,0:T(8,128)} %accel_hbm.1, ...), custom_call_target="tpu_custom_call" | custom-call | flops 8388608 | bytes 1916928 | tf_op jit(solution)/shard_map/pallas_call | solution.py:26
  1.9 3.1 %collective-permute-start = (f32[5,64,128]{2,1,0:T(8,128)S(1)}, f32[5,64,128]{2,1,0:T(8,128)S(1)}, u32[]{:S(2)}, u32[]{:S(2)}) collective-permute-start(f32[5,64,128]{2,1,0:T(8,128)S(1)} %get-tuple-element.36), channel_id=1, source_target_pairs={{0,8},{1,9},{2,10},{3,11},{4,12},{5,13},{6,14},{7,15},{8,0},{9,1},... | collective-permute-start | bytes 491528 | tf_op jit(solution)/shard_map/ppermute | solution.py:257
  5.0 1.2 %shard_map.87 = (f32[1040,128]{1,0:T(8,128)}, f32[1,512]{1,0:T(1,128)S(1)}) custom-call(s32[1,512]{1,0:T(1,128)S(1)} %get-tuple-element.31.place_ref, f32[1,512]{1,0:T(1,128)S(1)} %get-tuple-element.32.back_ref, f32[16,128]{1,0:T(8,128)S(1)} %get-tuple-element.33.columns_ref, f32[512,128]{1,0:T(8,128)S(1)} %get-tuple-element.34.accel_ref), custom_call_target="tpu_custom_call" | custom-call | flops 272629760 | bytes 808960 | tf_op jit(solution)/shard_map/pallas_call | solution.py:26
  6.2 7.8 %all-to-all-start = ((f32[16,65,1,128]{3,2,1,0:T(1,128)}), f32[16,65,1,128]{3,2,1,0:T(1,128)S(1)}, u32[]{:S(2)}, u32[]{:S(2)}) async-start(f32[16,65,1,128]{3,2,1,0:T(1,128)} %bitcast.2), calls=%async_computation | async-start | bytes 1064960 | tf_op jit(solution)/shard_map/all_to_all | solution.py:93
  14.0 0.0 collective-permute-done.xe_ref
  14.0 0.0 collective-permute-done.1.xo_ref
  14.0 0.0 copy-start.8
  14.0 0.0 copy-start.1
  14.0 0.0 copy-start.7
  14.1 0.3 shard_map.88
  14.4 0.3 copy-done.8
  14.7 0.5 collective-permute-start.3
  15.2 1.5 %collective-permute-start.4 = (f32[5,16,128]{2,1,0:T(8,128)S(1)}, f32[5,16,128]{2,1,0:T(8,128)S(1)}, u32[]{:S(2)}, u32[]{:S(2)}) collective-permute-start(f32[5,16,128]{2,1,0:T(8,128)S(1)} %get-tuple-element.44), channel_id=1, source_target_pairs={{0,2},{1,3},{2,0},{3,1},{4,6},{5,7},{6,4},{7,5},{8,10},{9,11},{10,... | collective-permute-start | bytes 122888 | tf_op jit(solution)/shard_map/ppermute | solution.py:257
  16.6 0.7 %collective-permute-done.3.bo_ref = f32[16,64,128]{2,1,0:T(8,128)S(1)} collective-permute-done((f32[16,64,128]{2,1,0:T(8,128)S(1)}, f32[16,64,128]{2,1,0:T(8,128)S(1)}, u32[]{:S(2)}, u32[]{:S(2)}) %collective-permute-start.3) | collective-permute-done | bytes 524320 | tf_op jit(solution)/shard_map/ppermute | solution.py:262
  17.3 2.7 %shard_map.89 = (f32[16,64,128]{2,1,0:T(8,128)S(1)}, f32[16,64,128]{2,1,0:T(8,128)S(1)}) custom-call(f32[16,64,128]{2,1,0:T(8,128)S(1)} %copy-done.2, f32[16,64,128]{2,1,0:T(8,128)S(1)} %copy-done, f32[16,64,128]{2,1,0:T(8,128)S(1)} %copy-done.7, f32[16,64,128]{2,1,0:T(8,128)S(1)} %copy-done.1, f32[16,64,128]{2,1,0:T(8,128)S(1)} %collective-permute-done.2.po_ref, ...), custom_call_target="tpu_custom_call" | custom-call | flops 13107200 | bytes 4194304 | tf_op jit(solution)/shard_map/pallas_call | solution.py:26
  20.0 0.2 collective-permute-done.4.ye_ref
  20.2 0.3 shard_map.90
  20.5 0.0 copy-start.5
  20.5 0.8 %copy-done.5 = f32[16,64,128]{2,1,0:T(8,128)} copy-done((f32[16,64,128]{2,1,0:T(8,128)}, f32[16,64,128]{2,1,0:T(8,128)S(1)}, u32[]{:S(2)}) %copy-start.5) | copy-done | bytes 524312
  21.3 4.6 %all-to-all-done = f32[16,65,1,128]{3,2,1,0:T(1,128)S(1)} async-done(((f32[16,65,1,128]{3,2,1,0:T(1,128)}), f32[16,65,1,128]{3,2,1,0:T(1,128)S(1)}, u32[]{:S(2)}, u32[]{:S(2)}) %all-to-all-start) | async-done | bytes 532512 | tf_op jit(solution)/shard_map/all_to_all | solution.py:93
  25.9 1.0 %copy-done.6 = f32[16,64,128]{2,1,0:T(8,128)S(1)} copy-done((f32[16,64,128]{2,1,0:T(8,128)S(1)}, f32[16,64,128]{2,1,0:T(8,128)}, u32[]{:S(2)}) %copy-start.6) | copy-done | bytes 524312
  26.9 0.8 %shard_map.91 = (f32[16,64,128]{2,1,0:T(8,128)S(1)}, f32[3,64,128]{2,1,0:T(8,128)S(1)}, f32[3,64,128]{2,1,0:T(8,128)S(1)}, f32[3,16,128]{2,1,0:T(8,128)S(1)}, f32[3,16,128]{2,1,0:T(8,128)S(1)}) custom-call(f32[1040,128]{1,0:T(8,128)S(1)} %bitcast.4, f32[16,64,128]{2,1,0:T(8,128)S(1)} %copy-done.6, f32[16,64,128]{2,1,0:T(8,128)S(1)} %copy-done.1), custom_call_target="tpu_custom_call" | custom-call | flops 805306368 | bytes 2351104 | tf_op jit(solution)/shard_map/pallas_call | solution.py:26
  27.7 0.1 collective-permute-start.6
  27.8 0.4 collective-permute-start.7
  28.3 0.2 collective-permute-start.8
  28.4 1.5 %collective-permute-start.9 = (f32[3,16,128]{2,1,0:T(8,128)S(1)}, f32[3,16,128]{2,1,0:T(8,128)S(1)}, u32[]{:S(2)}, u32[]{:S(2)}) collective-permute-start(f32[3,16,128]{2,1,0:T(8,128)S(1)} %get-tuple-element.54), channel_id=1, source_target_pairs={{0,2},{1,3},{2,0},{3,1},{4,6},{5,7},{6,4},{7,5},{8,10},{9,11},{10,... | collective-permute-start | bytes 73736 | tf_op jit(solution)/shard_map/ppermute | solution.py:257
  29.9 0.1 collective-permute-start.10
  30.0 3.6 %shard_map.92 = (f32[16,64,128]{2,1,0:T(8,128)S(1)}, bf16[1024,1024]{1,0:T(8,128)(2,1)S(1)}) custom-call(f32[16,64,128]{2,1,0:T(8,128)S(1)} %get-tuple-element.47.mid_ref, f32[16,64,128]{2,1,0:T(8,128)S(1)} %copy-done.6, f32[16,64,128]{2,1,0:T(8,128)} %p_hbm.3, f32[16,64,128]{2,1,0:T(8,128)S(1)} %copy-done, f32[16,64,128]{2,1,0:T(8,128)S(1)} %copy-done.1, ...), custom_call_target="tpu_custom_call" | custom-call | flops 13107200 | bytes 9445376 | tf_op jit(solution)/shard_map/pallas_call | solution.py:26
  33.7 0.9 %shard_map.93 = (f32[16,64,128]{2,1,0:T(8,128)S(1)}, f32[16,64,128]{2,1,0:T(8,128)S(1)}) custom-call(f32[16,64,128]{2,1,0:T(8,128)S(1)} %get-tuple-element.49.part_ref, f32[16,64,128]{2,1,0:T(8,128)S(1)} %get-tuple-element.47.mid_ref, f32[16,64,128]{2,1,0:T(8,128)S(1)} %copy-done, f32[16,64,128]{2,1,0:T(8,128)S(1)} %copy-done.1, ...), custom_call_target="tpu_custom_call" | custom-call | flops 805306368 | bytes 7749632 | tf_op jit(solution)/shard_map/pallas_call | solution.py:26
  34.6 17.8 %all_to_all.10.returned_ref = f32[16,64,128]{2,1,0:T(8,128)S(1)} all-to-all(f32[16,64,128]{2,1,0:T(8,128)S(1)} %get-tuple-element.56), channel_id=1, replica_groups={{20,2,22,12,6,10,4,8,24,14,0,28,16,26,18,30},{17,5,9,21,25,13,11,29,7,2..., dimensions={0} | all-to-all | bytes 1048576 | tf_op jit(solution)/shard_map/all_to_all | solution.py:93
  52.4 1.2 %shard_map.94 = (f32[512,128]{1,0:T(8,128)}, f32[16,64,128]{2,1,0:T(8,128)}) custom-call(bf16[512,1024]{1,0:T(8,128)(2,1)S(1)} %copy-done.4, f32[16,64,128]{2,1,0:T(8,128)S(1)} %all_to_all.10.returned_ref, f32[16,64,128]{2,1,0:T(8,128)S(1)} %get-tuple-element.57.next_ref), custom_call_target="tpu_custom_call" | custom-call | flops 268435456 | bytes 3932160 | tf_op jit(solution)/shard_map/pallas_call | solution.py:26
  (22 shorter events, 0.1 us)
Async XLA Ops:
  0.6 13.4 %copy-start = (f32[16,64,128]{2,1,0:T(8,128)S(1)}, f32[16,64,128]{2,1,0:T(8,128)}, u32[]{:S(2)}) copy-start(f32[16,64,128]{2,1,0:T(8,128)} %b_ref.9) | copy-start | bytes 1572868
  0.6 13.4 %copy-start.2 = (f32[16,64,128]{2,1,0:T(8,128)S(1)}, f32[16,64,128]{2,1,0:T(8,128)}, u32[]{:S(2)}) copy-start(f32[16,64,128]{2,1,0:T(8,128)} %p_hbm.3) | copy-start | bytes 1572868
  1.9 12.1 %collective-permute-start = (f32[5,64,128]{2,1,0:T(8,128)S(1)}, f32[5,64,128]{2,1,0:T(8,128)S(1)}, u32[]{:S(2)}, u32[]{:S(2)}) collective-permute-start(f32[5,64,128]{2,1,0:T(8,128)S(1)} %get-tuple-element.36), channel_id=1, source_target_pairs={{0,8},{1,9},{2,10},{3,11},{4,12},{5,13},{6,14},{7,15},{8,0},{9,1},... | collective-permute-start | bytes 491528 | tf_op jit(solution)/shard_map/ppermute | solution.py:257
  5.0 9.0 %collective-permute-start.1 = (f32[5,64,128]{2,1,0:T(8,128)S(1)}, f32[5,64,128]{2,1,0:T(8,128)S(1)}, u32[]{:S(2)}, u32[]{:S(2)}) collective-permute-start(f32[5,64,128]{2,1,0:T(8,128)S(1)} %get-tuple-element.37), channel_id=1, source_target_pairs={{0,1},{1,0},{2,3},{3,2},{4,5},{5,4},{6,7},{7,6},{8,16},{9,17},{10,... | collective-permute-start | bytes 491528 | tf_op jit(solution)/shard_map/ppermute | solution.py:256
  6.2 19.7 %all-to-all-start = ((f32[16,65,1,128]{3,2,1,0:T(1,128)}), f32[16,65,1,128]{3,2,1,0:T(1,128)S(1)}, u32[]{:S(2)}, u32[]{:S(2)}) async-start(f32[16,65,1,128]{3,2,1,0:T(1,128)} %bitcast.2), calls=%async_computation | async-start | bytes 1064960 | tf_op jit(solution)/shard_map/all_to_all | solution.py:93
  14.0 0.7 %copy-start.8 = (f32[5,64,128]{2,1,0:T(8,128)}, f32[5,64,128]{2,1,0:T(8,128)S(1)}, u32[]{:S(2)}) copy-start(f32[5,64,128]{2,1,0:T(8,128)S(1)} %collective-permute-done.1.xo_ref) | copy-start | bytes 491524
  14.0 3.3 %copy-start.1 = (f32[16,64,128]{2,1,0:T(8,128)S(1)}, f32[16,64,128]{2,1,0:T(8,128)}, u32[]{:S(2)}) copy-start(f32[16,64,128]{2,1,0:T(8,128)} %kappa_ref.9) | copy-start | bytes 1572868
  14.0 3.3 %copy-start.7 = (f32[16,64,128]{2,1,0:T(8,128)S(1)}, f32[16,64,128]{2,1,0:T(8,128)}, u32[]{:S(2)}) copy-start(f32[16,64,128]{2,1,0:T(8,128)} %prev_ref.1) | copy-start | bytes 1572868
  14.7 5.5 %copy-start.3 = (bf16[512,1024]{1,0:T(8,128)(2,1)}, bf16[512,1024]{1,0:T(8,128)(2,1)S(1)}, u32[]{:S(2)}) copy-start(bf16[512,1024]{1,0:T(8,128)(2,1)S(1)} %get-tuple-element.38.map_ref) | copy-start | bytes 3145732
  14.7 5.5 %copy-start.9 = (f32[5,64,128]{2,1,0:T(8,128)S(1)}, f32[5,64,128]{2,1,0:T(8,128)}, u32[]{:S(2)}) copy-start(f32[5,64,128]{2,1,0:T(8,128)} %copy-done.8) | copy-start | bytes 491524
  14.7 2.0 %collective-permute-start.2 = (f32[16,64,128]{2,1,0:T(8,128)S(1)}, f32[16,64,128]{2,1,0:T(8,128)S(1)}, u32[]{:S(2)}, u32[]{:S(2)}) collective-permute-start(f32[16,64,128]{2,1,0:T(8,128)S(1)} %get-tuple-element.40), channel_id=1, source_target_pairs={{0,1},{1,0},{2,3},{3,2},{4,5},{5,4},{6,7},{7,6},{8,9},{9,8},{10,11... | collective-permute-start | bytes 1572872 | tf_op jit(solution)/shard_map/ppermute | solution.py:262
  14.7 2.7 %collective-permute-start.3 = (f32[16,64,128]{2,1,0:T(8,128)S(1)}, f32[16,64,128]{2,1,0:T(8,128)S(1)}, u32[]{:S(2)}, u32[]{:S(2)}) collective-permute-start(f32[16,64,128]{2,1,0:T(8,128)S(1)} %get-tuple-element.41), channel_id=1, source_target_pairs={{0,1},{1,0},{2,3},{3,2},{4,5},{5,4},{6,7},{7,6},{8,9},{9,8},{10,11... | collective-permute-start | bytes 1572872 | tf_op jit(solution)/shard_map/ppermute | solution.py:262
  15.2 5.0 %collective-permute-start.4 = (f32[5,16,128]{2,1,0:T(8,128)S(1)}, f32[5,16,128]{2,1,0:T(8,128)S(1)}, u32[]{:S(2)}, u32[]{:S(2)}) collective-permute-start(f32[5,16,128]{2,1,0:T(8,128)S(1)} %get-tuple-element.44), channel_id=1, source_target_pairs={{0,2},{1,3},{2,0},{3,1},{4,6},{5,7},{6,4},{7,5},{8,10},{9,11},{10,... | collective-permute-start | bytes 122888 | tf_op jit(solution)/shard_map/ppermute | solution.py:257
  16.6 3.6 %collective-permute-start.5 = (f32[5,16,128]{2,1,0:T(8,128)S(1)}, f32[5,16,128]{2,1,0:T(8,128)S(1)}, u32[]{:S(2)}, u32[]{:S(2)}) collective-permute-start(f32[5,16,128]{2,1,0:T(8,128)S(1)} %get-tuple-element.45), channel_id=1, source_target_pairs={{0,1},{1,0},{2,4},{3,5},{4,2},{5,3},{6,7},{7,6},{8,9},{9,8},{10,12... | collective-permute-start | bytes 122888 | tf_op jit(solution)/shard_map/ppermute | solution.py:256
  20.5 0.8 %copy-start.5 = (f32[16,64,128]{2,1,0:T(8,128)}, f32[16,64,128]{2,1,0:T(8,128)S(1)}, u32[]{:S(2)}) copy-start(f32[16,64,128]{2,1,0:T(8,128)S(1)} %get-tuple-element.46.mid0_ref) | copy-start | bytes 1572868
  25.9 1.0 %copy-start.6 = (f32[16,64,128]{2,1,0:T(8,128)S(1)}, f32[16,64,128]{2,1,0:T(8,128)}, u32[]{:S(2)}) copy-start(f32[16,64,128]{2,1,0:T(8,128)} %copy-done.5) | copy-start | bytes 1572868
  27.7 2.2 %collective-permute-start.6 = (f32[16,64,128]{2,1,0:T(8,128)S(1)}, f32[16,64,128]{2,1,0:T(8,128)S(1)}, u32[]{:S(2)}, u32[]{:S(2)}) collective-permute-start(f32[16,64,128]{2,1,0:T(8,128)S(1)} %get-tuple-element.47.mid_ref), channel_id=1, source_target_pairs={{0,1},{1,0},{2,3},{3,2},{4,5},{5,4},{6,7},{7,6},{8,9},{9,8},{10,11... | collective-permute-start | bytes 1572872 | tf_op jit(solution)/shard_map/ppermute | solution.py:262
  27.8 5.8 %collective-permute-start.7 = (f32[3,64,128]{2,1,0:T(8,128)S(1)}, f32[3,64,128]{2,1,0:T(8,128)S(1)}, u32[]{:S(2)}, u32[]{:S(2)}) collective-permute-start(f32[3,64,128]{2,1,0:T(8,128)S(1)} %get-tuple-element.52), channel_id=1, source_target_pairs={{0,8},{1,9},{2,10},{3,11},{4,12},{5,13},{6,14},{7,15},{8,0},{9,1},... | collective-permute-start | bytes 294920 | tf_op jit(solution)/shard_map/ppermute | solution.py:257
  28.3 5.4 %collective-permute-start.8 = (f32[3,64,128]{2,1,0:T(8,128)S(1)}, f32[3,64,128]{2,1,0:T(8,128)S(1)}, u32[]{:S(2)}, u32[]{:S(2)}) collective-permute-start(f32[3,64,128]{2,1,0:T(8,128)S(1)} %get-tuple-element.53), channel_id=1, source_target_pairs={{0,1},{1,0},{2,3},{3,2},{4,5},{5,4},{6,7},{7,6},{8,16},{9,17},{10,... | collective-permute-start | bytes 294920 | tf_op jit(solution)/shard_map/ppermute | solution.py:256
  28.4 5.2 %collective-permute-start.9 = (f32[3,16,128]{2,1,0:T(8,128)S(1)}, f32[3,16,128]{2,1,0:T(8,128)S(1)}, u32[]{:S(2)}, u32[]{:S(2)}) collective-permute-start(f32[3,16,128]{2,1,0:T(8,128)S(1)} %get-tuple-element.54), channel_id=1, source_target_pairs={{0,2},{1,3},{2,0},{3,1},{4,6},{5,7},{6,4},{7,5},{8,10},{9,11},{10,... | collective-permute-start | bytes 73736 | tf_op jit(solution)/shard_map/ppermute | solution.py:257
  29.9 3.7 %collective-permute-start.10 = (f32[3,16,128]{2,1,0:T(8,128)S(1)}, f32[3,16,128]{2,1,0:T(8,128)S(1)}, u32[]{:S(2)}, u32[]{:S(2)}) collective-permute-start(f32[3,16,128]{2,1,0:T(8,128)S(1)} %get-tuple-element.55), channel_id=1, source_target_pairs={{0,1},{1,0},{2,4},{3,5},{4,2},{5,3},{6,7},{7,6},{8,9},{9,8},{10,12... | collective-permute-start | bytes 73736 | tf_op jit(solution)/shard_map/ppermute | solution.py:256
  33.7 18.7 %copy-start.4 = (bf16[512,1024]{1,0:T(8,128)(2,1)S(1)}, bf16[512,1024]{1,0:T(8,128)(2,1)}, u32[]{:S(2)}) copy-start(bf16[512,1024]{1,0:T(8,128)(2,1)} %copy-done.3) | copy-start | bytes 3145732
